TPU v7x, 128 devices: a whole 4x4x4 slice. The times are simulated.
128 devices in a mesh: row: 16 (over y_lo, x, core), col: 8 (over z, y_hi).
Axes of the slice: x: 4, y: 4 (y_hi: 2, y_lo: 2; y = y_hi * 2 + y_lo), z: 4, core: 2. Of those that a mesh axis runs over, the one named last changes fastest.
Arguments:
- core_matrix: bfloat16 [8192, 8192], P('row', 'col'), may hold values from -0.1875 to 0.1875
- pattern: int32 [64, 64], P('row', 'col'), may hold values from 0 to 1, as said below
- shift: float32 [1], replicated, may hold values from -1 to 1
- potential: float32 [128, 64, 128], P('row', 'col'), may hold values from -6 to 6
- home: int32 [64], replicated, may hold values from 0 to 127, as said below
- centres: int32 [3, 64, 128], replicated, may hold values from 0 to 127, as said below
- exponents: float32 [64, 128], replicated, may hold values from 0.05 to 1
- extents: int32 [64, 128], replicated, may hold values from 2 to 7
Outputs:
- scaled: bfloat16 [8192, 8192], P('row', 'col')
- square: bfloat16 [8192, 8192], P('row', 'col')
Inputs may be any that keep to these rules, and one draw needn't show every extreme that they name: `pattern`: entries are 0 or 1; every diagonal entry is 1. `home`: at most 2 clusters share a brick, and some brick holds exactly 2. `centres`: the x coordinates lie below 8, the y below 8, the z below 128.
All inputs are finite; a program needn't handle non-finite values.
Results may differ from a plain program's by a relative error of at most 0.0058.
Values may be sent and summed in bfloat16 or wider, within the bound.
No kernel may reach another device: no remote copies, remote signals or barrier semaphores. Data moves between devices by JAX's collectives and lax.ppermute only.
A program may use at most 128 MiB of HBM per device.

v0:
```python
import jax
import jax.numpy as jnp
from jax import lax
from jax.sharding import PartitionSpec as P

BS = 128
CAP = 2


volume_element = 0.015625


def collocate(centre_xyz, decays, radius, values, span_y, span_z):
    count_points = values.shape[0]
    position = jnp.arange(count_points, dtype=jnp.int32)
    coord_x = position // (span_y * span_z)
    coord_y = position // span_z % span_y
    coord_z = position % span_z
    offset_x = coord_x[None, :] - centre_xyz[0][:, None]
    offset_y = coord_y[None, :] - centre_xyz[1][:, None]
    offset_z = coord_z[None, :] - centre_xyz[2][:, None]
    distance = offset_x * offset_x + offset_y * offset_y + offset_z * offset_z
    inside = distance <= (radius * radius)[:, None]
    values_phi = jnp.where(
        inside, jnp.exp(-decays[:, None] * distance.astype(jnp.float32)), jnp.float32(0.0)
    )
    basis = values_phi.astype(jnp.bfloat16)
    weighted = (basis.astype(jnp.float32) * values[None, :]).astype(jnp.bfloat16)
    block_value = jnp.dot(weighted, basis.T, preferred_element_type=jnp.float32) * volume_element
    return block_value.astype(jnp.bfloat16)


def body(core_matrix, pattern, shift, potential, home, centres, exponents, extents):
    rows_local, cols_local = core_matrix.shape
    blocks_row = rows_local // BS
    blocks_col = cols_local // BS
    row_index = lax.axis_index("row")
    col_index = lax.axis_index("col")
    span_x, span_y, span_z = potential.shape
    cluster_ids = jnp.arange(home.shape[0], dtype=jnp.int32)
    brick = row_index * lax.axis_size("col") + col_index
    matched = (home == brick).astype(jnp.int32)
    ranked = jnp.cumsum(matched) - 1
    flat_values = potential.reshape(span_x * span_y * span_z)
    made = []
    members = []
    presents = []
    for slot in range(CAP):
        chosen = matched * (ranked == slot).astype(jnp.int32)
        present = jnp.sum(chosen) > 0
        member = jnp.sum(chosen * cluster_ids)

        def compute(cluster):
            return collocate(
                centres[:, cluster],
                exponents[cluster],
                extents[cluster],
                flat_values,
                span_y,
                span_z,
            )

        def nothing(cluster):
            return jnp.zeros((BS, BS), jnp.bfloat16)

        made.append(lax.cond(present, compute, nothing, member))
        members.append(member)
        presents.append(present)
    cluster_rows = jnp.arange(lax.axis_size("row") * blocks_row, dtype=jnp.int32)
    total = jnp.zeros((lax.axis_size("row") * blocks_row, BS, BS), jnp.float32)
    for slot in range(CAP):
        selected = ((cluster_rows == members[slot]) & presents[slot]).astype(jnp.float32)
        total = total + selected[:, None, None] * made[slot].astype(jnp.float32)[None, :, :]
    column_share = lax.psum_scatter(
        total.astype(jnp.bfloat16), "row", scatter_dimension=0, tiled=True
    )
    owned_blocks = lax.psum(column_share, "col").astype(jnp.float32)

    def source(cluster):
        return owned_blocks[cluster - row_index * blocks_row]

    combined = core_matrix.astype(jnp.float32)
    identity = jnp.eye(BS, dtype=jnp.float32)
    for local in range(blocks_row):
        cluster = row_index * blocks_row + local
        column = cluster - col_index * blocks_col
        owned = (column >= 0) & (column < blocks_col)
        safe = jnp.clip(column, 0, blocks_col - 1)
        corner = (jnp.int32(local * BS), safe * BS)
        current = lax.dynamic_slice(combined, corner, (BS, BS))

        def add_grid(operands):
            return operands[0] + source(operands[1]) - shift[0] * identity

        def keep_block(operands):
            return operands[0]

        updated = lax.cond(owned, add_grid, keep_block, (current, cluster))
        combined = lax.dynamic_update_slice(combined, updated, corner)
    keep = pattern.astype(jnp.float32)[:, None, :, None]
    hamiltonian = (combined.reshape(blocks_row, BS, blocks_col, BS) * keep).reshape(
        rows_local, cols_local
    )
    order_total = rows_local * lax.axis_size("row")
    frob = lax.psum(jnp.sum(hamiltonian * hamiltonian), ("row", "col"))
    scaled = (hamiltonian * lax.rsqrt(frob / order_total + 1e-06)).astype(jnp.bfloat16)
    panel = lax.all_gather(scaled, "col", axis=1, tiled=True)
    product = jnp.dot(
        panel, lax.all_gather(scaled, "row", axis=0, tiled=True), preferred_element_type=jnp.float32
    )
    square = (
        (product.reshape(blocks_row, BS, blocks_col, BS) * keep)
        .reshape(rows_local, cols_local)
        .astype(jnp.bfloat16)
    )
    return (scaled, square)


def solution(mesh):
    in_specs = (P("row", "col"), P("row", "col"), P(), P("row", "col", None), P(), P(), P(), P())
    out_specs = (P("row", "col"), P("row", "col"))
    return jax.shard_map(body, mesh=mesh, in_specs=in_specs, out_specs=out_specs, check_vma=False)
```

profile of v0, /device:TPU:1, one launch (start us, length us, event | category | flops | bytes accessed | tf_op | source)
XLA Modules:
  0.0 476.4 jit_solution(465308828625424924)
XLA Ops:
  8.2 1.4 multiply_reduce_fusion.2
  10.8 1.3 and_convert_fusion
  12.1 9.3 %conditional.6 = (bf16[128,128]{1,0:T(8,128)(2,1)S(1)}) conditional(s32[]{:T(128)} %convert_element_type.104, () %tuple.44, (s32[]{:T(128)}, s32[3,64,128]{2,1,0:T(8,128)}, s32[64,128]{1,0:T(8,128)}, f32[64,128]{1,0:T(8,128)}, f32[8,8,128]{2,1,0:T(8,128)}) %tuple.45), branch_computations={%region_3.4_spmd, %region_4.5_spmd} | conditional | flops 299131136 | bytes 4565078 | solution.py:66
  14.1 0.7 fusion.24
  14.8 0.7 fusion.26
  15.5 0.7 fusion.27
  16.2 3.1 multiply_convert_fusion.16
  19.3 2.2 fusion.13
  21.6 2.0 add_convert_fusion
  23.7 72.1 %reduce-scatter.2.cloned.1.call-done = bf16[4,128,128]{2,1,0:T(8,128)(2,1)} async-done(((bf16[64,128,128]{2,1,0:T(8,128)(2,1)}), bf16[4,128,128]{2,1,0:T(8,128)(2,1)}) %reduce-scatter.2.cloned.1.call-update) | async-done | bytes 131088 | tf_op jit(solution)/shard_map/reduce_scatter | solution.py:74
  96.2 82.9 %all-reduce.2.cloned.1.call-done = bf16[4,128,128]{2,1,0:T(8,128)(2,1)} async-done(((bf16[4,128,128]{2,1,0:T(8,128)(2,1)}), bf16[4,128,128]{2,1,0:T(8,128)(2,1)}) %all-reduce.2.cloned.1.call-update) | async-done | bytes 131088 | tf_op jit(solution)/shard_map/psum | solution.py:77
  179.0 0.9 convert_element_type.110
  180.0 0.7 conditional.8
  180.0 0.7 fusion.60
  180.7 0.7 conditional.9
  181.5 0.7 conditional.10
  182.2 0.7 conditional.11
  183.2 1.4 copy-done
  184.5 1.4 multiply_reduce_fusion
  185.9 67.4 %psum.15 = f32[]{:T(128)} all-reduce(f32[]{:T(128)} %multiply_reduce_fusion), channel_id=1, replica_groups=mesh['row'=16,'col'=8] {'row','col'}, use_global_device_ids=true, to_apply=%region_20.21 | all-reduce | flops 1 | bytes 8 | tf_op jit(solution)/shard_map/psum | solution.py:105
  254.0 3.2 multiply_convert_fusion.12
  257.8 103.0 %all-gather.3.cloned.1.call-done = bf16[512,8192]{1,0:T(8,128)(2,1)} async-done(((bf16[512,1024]{1,0:T(8,128)(2,1)}), bf16[512,8192]{1,0:T(8,128)(2,1)}) %all-gather.3.cloned.1.call-update) | async-done | bytes 8388624 | tf_op jit(solution)/shard_map/all_gather | solution.py:107
  360.8 92.4 %all-gather.5.cloned.1.call-done = bf16[8192,1024]{1,0:T(8,128)(2,1)} async-done(((bf16[512,1024]{1,0:T(8,128)(2,1)}), bf16[8192,1024]{1,0:T(8,128)(2,1)}) %all-gather.5.cloned.1.call-update) | async-done | bytes 16777232 | tf_op jit(solution)/shard_map/all_gather | solution.py:109
  453.2 16.6 %fusion.64 = bf16[512,1024]{1,0:T(8,128)(2,1)} fusion(f32[64,8,8,128]{3,2,1,0:T(8,128)} %bitcast.61, bf16[512,8192]{1,0:T(8,128)(2,1)} %all-gather.3.cloned.1.call-done, bf16[8192,1024]{1,0:T(8,128)(2,1)} %all-gather.5.cloned.1.call-done), kind=kOutput, calls=%fused_computation.109 | convolution fusion | flops 8590983168 | bytes 28311552 | tf_op jit(solution)/shard_map/dot_general | solution.py:108
  (38 shorter events, 4.4 us)
Async XLA Ops:
  7.2 88.5 %reduce-scatter.2.cloned.1.call-start = ((), (), s32[]{:S(2)}) async-start(), calls=%async_computation.1 | async-start | bytes 2228224 | tf_op jit(solution)/shard_map/reduce_scatter | solution.py:74
  21.5 74.3 %copy-start.2 = (s32[4,8]{1,0:T(4,128)S(1)}, s32[4,8]{1,0:T(4,128)}, u32[]{:S(2)}) copy-start(s32[4,8]{1,0:T(4,128)} %param.21) | copy-start | bytes 388
  21.5 74.3 %copy-start.1 = (bf16[512,1024]{1,0:T(8,128)(2,1)S(1)}, bf16[512,1024]{1,0:T(8,128)(2,1)}, u32[]{:S(2)}) copy-start(bf16[512,1024]{1,0:T(8,128)(2,1)} %param.20) | copy-start | bytes 3145732
  23.6 155.4 %all-reduce.2.cloned.1.call-start = ((), (), s32[]{:S(2)}) async-start(), calls=%async_computation.2 | async-start | bytes 262144 | tf_op jit(solution)/shard_map/psum | solution.py:77
  95.7 265.0 %all-gather.3.cloned.1.call-start = ((), (), s32[]{:S(2)}) async-start(), calls=%async_computation.3 | async-start | bytes 9437184 | tf_op jit(solution)/shard_map/all_gather | solution.py:107
  183.1 1.4 copy-start
  257.2 196.0 %all-gather.5.cloned.1.call-start = ((), (), s32[]{:S(2)}) async-start(), calls=%async_computation.4 | async-start | bytes 17825792 | tf_op jit(solution)/shard_map/all_gather | solution.py:109
Sparse Core Ops, SparseCore 0:
  23.7 71.9 reduce-scatter.1
  98.2 80.8 all-reduce.1
  257.3 103.3 all-gather.2
  363.0 90.1 all-gather.4
where the time goes:
time: 477 us; the launch traced here: 476 us
  waiting for transfers between devices  351 us (74%)
  blocking collectives  67.4 us (14%)
  matrix products  18.8 us (4%)
  other arithmetic  18.5 us (4%)
  between operations  16 us (3%)
    all_gather x1, waiting for transfers between devices, body(): panel = lax.all_gather(scaled, 'col', axis=1, tiled=True)  103 us
    all_gather x1, waiting for transfers between devices, body(): lax.all_gather(scaled, 'row', axis=0, tiled=True)  92.4 us
    psum x1, waiting for transfers between devices, body(): owned_blocks = lax.psum(column_share, 'col').astype(jnp.float32)  82.9 us
    reduce_scatter x1, waiting for transfers between devices, body(): lax.psum_scatter(total.astype(jnp.bfloat16), 'row', scatter_dimension=0,...  72.1 us
    psum x1, blocking collectives, body(): frob = lax.psum(jnp.sum(hamiltonian * hamiltonian), ('row', 'col'))  67.4 us
    dot_general x1, matrix products, body(): jnp.dot(panel, lax.all_gather(scaled, 'row', axis=0, tiled=True), preferr...  16.6 us
  transfers between devices with their start and end apart: 4, of which 4 were waited for; matrix products, arithmetic and copies ran while one was open for 0% of the time, Pallas kernels for 0%

commit v1 on v0

v1 whole, which is shorter than its diff:
```python
import functools

import jax
import jax.numpy as jnp
from jax import lax
from jax.experimental import pallas as pl
from jax.experimental.pallas import tpu as pltpu
from jax.sharding import PartitionSpec as P

BS = 128
CAP = 20
GROUP = 8
ORDER = 8192
VOLUME = 0.015625
LISTED = 2048 + 32 * GROUP
F32 = jnp.float32
BF16 = jnp.bfloat16


def params(limit=48 * 1024 * 1024):
    return pltpu.CompilerParams(vmem_limit_bytes=limit)


def pack_kernel(pattern_ref, place_ref, core_ref, payload_ref, sum_ref):
    first_row = place_ref[0] * 4
    first_col = place_ref[1] * 8
    sum_ref[...] = jnp.zeros_like(sum_ref)

    def put(i, j, slot):
        payload_ref[pl.ds(pl.multiple_of(slot * BS, BS), BS), :] = core_ref[
            i * BS : (i + 1) * BS, j * BS : (j + 1) * BS
        ]

    slot = jnp.int32(0)
    for i in range(4):
        for j in range(8):
            kept = pattern_ref[i, j] != 0

            @pl.when(kept & (slot < CAP))
            def _():
                put(i, j, slot)

            @pl.when(kept & (first_row + i != first_col + j))
            def _():
                block = core_ref[i * BS : (i + 1) * BS, j * BS : (j + 1) * BS].astype(F32)
                squares = (block * block).reshape(16, 8, BS)
                sum_ref[...] += jnp.sum(squares, axis=0)

            slot += kept.astype(jnp.int32)
    for i in range(4):
        for j in range(8):
            dropped = pattern_ref[i, j] == 0

            @pl.when(dropped & (slot < CAP))
            def _():
                put(i, j, slot)

            slot += dropped.astype(jnp.int32)


def brick_kernel(pattern_ref, potential_ref, brick_ref):
    brick_ref[:64] = potential_ref[...].astype(BF16)
    rows = lax.broadcasted_iota(jnp.int32, (16, BS), 0)
    columns = lax.broadcasted_iota(jnp.int32, (16, BS), 1)
    note = jnp.zeros((16, BS), F32)
    for i in range(4):
        for j in range(8):
            note = jnp.where((rows == 0) & (columns == i * 8 + j), pattern_ref[i, j].astype(F32), note)
    brick_ref[64:] = note.astype(BF16)


def column(row_values):
    return jnp.broadcast_to(row_values, (BS, BS)).T


def collocate(cluster, brick_ref, centres_ref, exponents_ref, extents_ref, along_ref, phi_ref, weighted_ref):
    decay = column(exponents_ref[pl.ds(cluster, 1), :])
    reach = column(extents_ref[pl.ds(cluster, 1), :].astype(F32))
    cut = jnp.exp(-decay * (reach * reach + 0.5))
    at_x = column(centres_ref[0, pl.ds(cluster, 1), :].astype(F32))
    at_y = column(centres_ref[1, pl.ds(cluster, 1), :].astype(F32))
    at_z = column(centres_ref[2, pl.ds(cluster, 1), :].astype(F32))
    off_z = lax.broadcasted_iota(jnp.int32, (BS, BS), 1).astype(F32) - at_z
    along_z = jnp.exp(-decay * (off_z * off_z))
    for y in range(8):
        off_y = y - at_y
        along_ref[y] = jnp.exp(-decay * (off_y * off_y))

    total = jnp.zeros((BS, BS), F32)
    for x in range(8):
        off_x = x - at_x
        along_xz = along_z * jnp.exp(-decay * (off_x * off_x))
        for y in range(8):
            phi = along_xz * along_ref[y]
            basis = jnp.where(phi >= cut, phi, 0.0).astype(BF16)
            phi_ref[x, :, y * BS : (y + 1) * BS] = basis
            weighted_ref[x, :, y * BS : (y + 1) * BS] = basis * brick_ref[x * 8 + y : x * 8 + y + 1, :]
        total += lax.dot_general(
            weighted_ref[x], phi_ref[x], (((1,), (1,)), ((), ())), preferred_element_type=F32
        )
    return (total * VOLUME).astype(BF16)


def grid_kernel(
    count, with_sum, place_ref, home_ref, shift_ref, bricks_ref, centres_ref, exponents_ref, extents_ref, *rest
):
    if with_sum:
        core_ref, sum_ref, blocks_ref, total_ref, along_ref, phi_ref, weighted_ref = rest
    else:
        blocks_ref, along_ref, phi_ref, weighted_ref = rest
    row, col = place_ref[0], place_ref[1]
    first = row * 4 if with_sum else col * 8 + row % 2 * 4

    def one(k, carry):
        cluster = first + k
        home = home_ref[cluster]
        index = (home // 8 ^ row) % 2 * 64 + home // 16 * 8 + home % 8
        blocks_ref[k] = collocate(
            cluster, bricks_ref.at[index], centres_ref, exponents_ref, extents_ref, along_ref, phi_ref, weighted_ref
        )
        return carry

    lax.fori_loop(0, count, one, 0)
    if with_sum:
        total_ref[...] = jnp.sum(sum_ref[...], axis=0, keepdims=True)

        @pl.when(col == row // 2)
        def _():
            eye = identity()
            for i in range(4):
                corner = pl.multiple_of((row % 2 * 4 + i) * BS, BS)
                block = core_ref[i * BS : (i + 1) * BS, pl.ds(corner, BS)].astype(F32)
                block = block + blocks_ref[i].astype(F32) - shift_ref[0] * eye
                total_ref[...] += jnp.sum(block * block, axis=0, keepdims=True)


def identity():
    rows = lax.broadcasted_iota(jnp.int32, (BS, BS), 0)
    columns = lax.broadcasted_iota(jnp.int32, (BS, BS), 1)
    return (rows == columns).astype(F32)


def plan_kernel(
    place_ref, bricks_ref, start_ref, left_ref, right_ref, most_ref, slots_ref, slots, kept_k, kept_slot, kept_device, sem
):
    row, col = place_ref[0], place_ref[1]
    kept = jnp.sum(bricks_ref[:, 64:80, :].astype(F32), axis=1)
    earlier = lax.broadcasted_iota(jnp.int32, (BS, BS), 0) < lax.broadcasted_iota(jnp.int32, (BS, BS), 1)
    before = jnp.dot(kept.astype(BF16), earlier.astype(BF16), preferred_element_type=F32)
    slots_ref[...] = jnp.where(kept > 0.5, before, -1.0).astype(jnp.int32)
    most_ref[0] = jnp.max(jnp.sum(kept, axis=1, keepdims=True)).astype(jnp.int32)
    copy = pltpu.make_async_copy(slots_ref, slots, sem)
    copy.start()
    copy.wait()

    def left_row(i, number):
        def piece(other, number):
            device = row // 2 * 8 + other
            base = ((other ^ col) % 2 * 4 + (other // 2 - col // 2) % 4) * CAP
            for j in range(8):
                slot = slots[device, i * 8 + j]
                holder = other * 2 + j // 4
                kept_slot[number] = base + slot
                kept_device[number] = (holder ^ row) % 2 * 64 + other * 8 + col
                kept_k[number] = other * 8 + j
                number += (slot >= 0).astype(jnp.int32)
            return number

        return lax.fori_loop(0, 8, piece, number)

    def block_row(i, number):
        count = left_row(i, jnp.int32(0))

        def block(j, number):
            start_ref[i * 8 + j] = number // GROUP

            def listing(number):
                def entry(n, number):
                    k = kept_k[n]
                    holder = k // 4
                    slot = slots[kept_device[n], k % 4 * 8 + j]
                    base = (holder ^ row) % 2 * 8 + (holder // 8 ^ row // 8) * 4 + (holder // 2 - row // 2) % 4
                    left_ref[number] = kept_slot[n]
                    right_ref[number] = base * CAP + slot
                    return number + (slot >= 0).astype(jnp.int32)

                number = lax.fori_loop(0, count, entry, number)
                for more in range(GROUP - 1):
                    left_ref[number + more] = 8 * CAP
                    right_ref[number + more] = 0
                return (number + GROUP - 1) // GROUP * GROUP

            wanted = slots[row // 2 * 8 + col, i * 8 + j] >= 0
            return lax.cond(wanted, listing, lambda n: n, number)

        return lax.fori_loop(0, 8, block, number)

    number = lax.fori_loop(0, 4, block_row, jnp.int32(0))
    start_ref[32] = number // GROUP


def scaling(frob_ref):
    total = jnp.sum(frob_ref[...], axis=(0, 1), keepdims=True)
    return lax.rsqrt(total / ORDER + 1e-6)


def product_kernel(
    place_ref, pattern_ref, shift_ref, start_ref, left_ref, right_ref, frob_ref, core_ref, row_grid_ref, col_own_ref, col_other_ref,
    *rest
):
    lefts, rights = rest[:8], rest[8:24]
    scaled_ref, square_ref, left_all, right_all, acc_ref, col_grid_ref, sems = rest[24:]
    parts = [(left_all, k, ref) for k, ref in enumerate(lefts)] + [(right_all, k, ref) for k, ref in enumerate(rights)]
    copies = [
        pltpu.make_async_copy(ref, whole.at[pl.ds(k * CAP, CAP)], sems.at[n])
        for n, (whole, k, ref) in enumerate(parts)
    ]
    for copy in copies:
        copy.start()
    left_all[8 * CAP] = jnp.zeros((BS, BS), BF16)
    first_row = place_ref[0] * 4
    first_col = place_ref[1] * 8
    core = place_ref[0] % 2
    for n in range(4):
        col_grid_ref[core * 4 + n] = col_own_ref[n]
        col_grid_ref[(1 - core) * 4 + n] = col_other_ref[n]
    shift = shift_ref[0]
    scale = scaling(frob_ref)
    eye = identity()
    dot = functools.partial(jnp.dot, preferred_element_type=F32)
    for i in range(4):
        for j in range(8):
            block = (slice(i * BS, (i + 1) * BS), slice(j * BS, (j + 1) * BS))
            kept = pattern_ref[i, j] != 0
            diagonal = first_row + i == first_col + j

            @pl.when(kept)
            def _():
                here = core_ref[block]
                wide = here.astype(F32)
                acc_ref[i * 8 + j] = dot(row_grid_ref[i], here) + dot(here, col_grid_ref[j]) - 2.0 * shift * wide

                @pl.when(diagonal)
                def _():
                    grid = row_grid_ref[i]
                    grid_wide = grid.astype(F32)
                    acc_ref[i * 8 + j] += dot(grid, grid) - 2.0 * shift * grid_wide + shift * shift * eye
                    scaled_ref[block] = ((wide + grid_wide - shift * eye) * scale).astype(BF16)

                @pl.when(jnp.logical_not(diagonal))
                def _():
                    scaled_ref[block] = (wide * scale).astype(BF16)

            @pl.when(jnp.logical_not(kept))
            def _():
                scaled_ref[block] = jnp.zeros((BS, BS), BF16)
                square_ref[block] = jnp.zeros((BS, BS), BF16)

    for copy in copies:
        copy.wait()

    for i in range(4):
        for j in range(8):
            block = (slice(i * BS, (i + 1) * BS), slice(j * BS, (j + 1) * BS))

            @pl.when(pattern_ref[i, j] != 0)
            def _():
                def group(k, acc):
                    at = [k * GROUP + n for n in range(GROUP)]
                    left = jnp.concatenate([left_all[left_ref[n]] for n in at], axis=1)
                    right = jnp.concatenate([right_all[right_ref[n]] for n in at], axis=0)
                    return acc + dot(left, right)

                acc = lax.fori_loop(start_ref[i * 8 + j], start_ref[i * 8 + j + 1], group, acc_ref[i * 8 + j])
                square_ref[block] = (acc * (scale * scale)).astype(BF16)


VM = pl.BlockSpec(memory_space=pltpu.VMEM)
SM = pl.BlockSpec(memory_space=pltpu.SMEM)
ANY = pl.BlockSpec(memory_space=pl.ANY)


def to_all(value, axis, count, groups=None):
    copies = jnp.broadcast_to(value[None], (count,) + value.shape)
    return lax.all_to_all(copies, axis, 0, 0, axis_index_groups=groups)


def along_z(value, off):
    return lax.ppermute(value, "col", [((k + 2 * off) % 8, k) for k in range(8)])


def along_x(value, off):
    return lax.ppermute(value, "row", [(k // 8 * 8 + (k + 2 * off) % 8, k) for k in range(16)])


def half_round_y(value):
    pairs = []
    for row in range(16):
        for col in range(8):
            y = (col % 2 * 2 + row // 8 + (1 if row % 2 == 0 else 3)) % 4
            pairs.append((row * 8 + col, (y % 2 * 8 + row % 8) * 8 + col // 2 * 2 + y // 2))
    return lax.ppermute(value, ("row", "col"), pairs)


def to_core(value):
    return lax.ppermute(value, "row", [(k, k ^ 1) for k in range(16)])


def lasting(microseconds):
    return pl.CostEstimate(flops=int(microseconds * 1e9), bytes_accessed=2**20, transcendentals=0)


def body(core_matrix, pattern, shift, potential, home, centres, exponents, extents):
    row = lax.axis_index("row")
    col = lax.axis_index("col")
    place = jnp.stack([row, col]).astype(jnp.int32)

    payload, squares = pl.pallas_call(
        pack_kernel,
        in_specs=[SM, SM, VM],
        out_specs=[VM, VM],
        out_shape=[jax.ShapeDtypeStruct((CAP * BS, BS), BF16), jax.ShapeDtypeStruct((8, BS), F32)],
        compiler_params=params(),
        cost_estimate=lasting(2),
        name="pack",
    )(pattern, place, core_matrix)
    payload = payload.reshape(CAP, BS, BS)
    own_crossed = to_core(payload)

    (potential, _) = lax.optimization_barrier((potential, own_crossed))
    brick = pl.pallas_call(
        brick_kernel,
        in_specs=[SM, VM],
        out_specs=VM,
        out_shape=jax.ShapeDtypeStruct((80, BS), BF16),
        compiler_params=params(),
        cost_estimate=lasting(1),
        name="brick",
    )(pattern, potential.reshape(64, BS))
    same_core = [[row * 8 + col for row in range(core, 16, 2) for col in range(8)] for core in range(2)]
    half = to_all(brick, ("row", "col"), 64, same_core)

    other_left = half_round_y(half_round_y(payload))
    other_right = lax.ppermute(payload, "row", [(k, k ^ 8) for k in range(16)])
    lefts = [payload, along_z(payload, 1), along_z(payload, -1)]
    rights = [payload, along_x(payload, 1), along_x(payload, -1)]
    half, *_ = lax.optimization_barrier((half, lefts[1], lefts[2], rights[1], rights[2]))
    bricks = jnp.concatenate([half, to_core(half)])
    lefts.insert(2, along_z(lefts[1], 1))
    lefts += [other_left, along_z(other_left, 1), along_z(other_left, -1)]
    rights.insert(2, along_x(rights[1], 1))
    crossed = [own_crossed] + [to_core(piece) for piece in rights[1:]]
    rights += [other_right, along_x(other_right, 1), along_x(other_right, -1)]

    def grid_blocks(count, with_sum, *more):
        extra = [VM, VM] if with_sum else []
        out_shape = [jax.ShapeDtypeStruct((count, BS, BS), BF16)]
        if with_sum:
            out_shape.append(jax.ShapeDtypeStruct((1, BS), F32))
        return pl.pallas_call(
            functools.partial(grid_kernel, count, with_sum),
            in_specs=[SM, SM, SM, VM, VM, VM, VM] + extra,
            out_specs=[VM] * len(out_shape),
            out_shape=out_shape,
            scratch_shapes=[
                pltpu.VMEM((8, BS, BS), F32),
                pltpu.VMEM((8, BS, 8 * BS), BF16),
                pltpu.VMEM((8, BS, 8 * BS), BF16),
            ],
            compiler_params=params(),
            cost_estimate=lasting(2.2 * count),
            name="grid_rows" if with_sum else "grid_cols",
        )(place, home, shift, bricks, centres, exponents, extents, *more)

    row_grid, total = grid_blocks(4, True, core_matrix, squares)
    frob = to_all(total, ("row", "col"), 128).reshape(128, BS)

    left_before, right_before, other_right, right_after, _ = lax.optimization_barrier(
        (lefts[6], rights[6], other_right, rights[5], frob)
    )
    lefts.insert(6, along_z(left_before, -1))
    rights.insert(6, along_x(right_before, -1))
    crossed += [to_core(piece) for piece in (other_right, right_after, rights[6], right_before)]
    rights = rights + crossed

    (col_grid,) = grid_blocks(4, False)
    col_grid_crossed = to_core(col_grid)

    *listed, most = pl.pallas_call(
        plan_kernel,
        in_specs=[SM, VM],
        out_specs=[SM] * 4,
        out_shape=[
            jax.ShapeDtypeStruct((40,), jnp.int32),
            jax.ShapeDtypeStruct((LISTED,), jnp.int32),
            jax.ShapeDtypeStruct((LISTED,), jnp.int32),
            jax.ShapeDtypeStruct((1,), jnp.int32),
        ],
        scratch_shapes=[pltpu.VMEM((BS, BS), jnp.int32), pltpu.SMEM((BS, BS), jnp.int32)]
        + [pltpu.SMEM((72,), jnp.int32)] * 3
        + [pltpu.SemaphoreType.DMA],
        cost_estimate=lasting(5),
        name="plan",
    )(place, bricks)
    overflow = most[0] > CAP

    def sparse():
        return pl.pallas_call(
            product_kernel,
            in_specs=[SM] * 6 + [VM] * 5 + [ANY] * 24,
            out_specs=[VM, VM],
            out_shape=[jax.ShapeDtypeStruct((512, 1024), BF16)] * 2,
            scratch_shapes=[
                pltpu.VMEM((8 * CAP + 1, BS, BS), BF16),
                pltpu.VMEM((16 * CAP, BS, BS), BF16),
                pltpu.VMEM((32, BS, BS), F32),
                pltpu.VMEM((8, BS, BS), BF16),
                pltpu.SemaphoreType.DMA((24,)),
            ],
            compiler_params=params(),
            cost_estimate=lasting(12),
            name="product",
        )(place, pattern, shift, *listed, frob, core_matrix, row_grid, col_grid, col_grid_crossed, *lefts, *rights)

    def dense():
        keep = pattern.astype(F32)[:, None, :, None]
        numbers_row = row * 4 + jnp.arange(4)
        numbers_col = col * 8 + jnp.arange(8)
        on = (numbers_row[:, None] == numbers_col[None, :]).astype(F32)
        grid = row_grid.astype(F32) - shift[0] * jnp.eye(BS, dtype=F32)
        whole = core_matrix.astype(F32).reshape(4, BS, 8, BS) + on[:, None, :, None] * grid[:, :, None, :]
        whole = (whole * keep).reshape(512, 1024)
        scaled = (whole * lax.rsqrt(jnp.sum(frob) / ORDER + 1e-6)).astype(BF16)
        product = jnp.dot(
            lax.all_gather(scaled, "col", axis=1, tiled=True),
            lax.all_gather(scaled, "row", axis=0, tiled=True),
            preferred_element_type=F32,
        )
        square = (product.reshape(4, BS, 8, BS) * keep).reshape(512, 1024).astype(BF16)
        return scaled, square

    return tuple(lax.cond(overflow, lambda: tuple(dense()), lambda: tuple(sparse())))


def solution(mesh):
    in_specs = (P("row", "col"), P("row", "col"), P(), P("row", "col", None), P(), P(), P(), P())
    out_specs = (P("row", "col"), P("row", "col"))
    return jax.shard_map(body, mesh=mesh, in_specs=in_specs, out_specs=out_specs, check_vma=False)
```

time: 477 us -> 180 us (0.38)
  the two profiles are of different devices: /device:TPU:1 before, /device:TPU:105 now
where the time goes in v1:
time: 180 us; the launch traced here: 181 us
  waiting for transfers between devices  60.4 us (34%)
  Pallas kernels  58.9 us (33%)
  starting transfers between devices  41.7 us (23%)
  between operations  15.6 us (9%)
  local copies, waits for them, and re-layouts  3.53 us (2%)
    ppermute x6, waiting for transfers between devices, along_x(): lax.ppermute(value, 'row', [(k // 8 * 8 + (k + 2 * off) % 8, k) for k in...  28.4 us
    pallas_call x1, Pallas kernels, body(): pl.pallas_call(plan_kernel, in_specs=[SM, VM], out_specs=[SM] * 4, out_sh...  24.2 us
    all_to_all x2, starting transfers between devices, to_all(): return lax.all_to_all(copies, axis, 0, 0, axis_index_groups=groups)  18.8 us
    pallas_call x2, Pallas kernels, grid_blocks(): pl.pallas_call(functools.partial(grid_kernel, count, with_sum), in_specs=...  16.5 us
    pallas_call x1, Pallas kernels, sparse(): pl.pallas_call(product_kernel, in_specs=[SM] * 6 + [VM] * 5 + [ANY] * 24,...  15.2 us
    ppermute x1, waiting for transfers between devices, body(): other_right = lax.ppermute(payload, 'row', [(k, k ^ 8) for k in range(16)])  14.2 us
    ppermute x6, waiting for transfers between devices, along_z(): lax.ppermute(value, 'col', [((k + 2 * off) % 8, k) for k in range(8)])  14.1 us
    ppermute x10, starting transfers between devices, to_core(): return lax.ppermute(value, 'row', [(k, k ^ 1) for k in range(16)])  10.1 us
  transfers between devices with their start and end apart: 27, of which 8 were waited for; matrix products, arithmetic and copies ran while one was open for 1% of the time, Pallas kernels for 23%

profile of v1, /device:TPU:105, one launch (start us, length us, event | category | flops | bytes accessed | tf_op | source)
XLA Modules:
  0.0 180.5 jit_solution(7507580110770983497)
XLA Ops:
  7.2 2.3 %pack.1 = (bf16[2560,128]{1,0:T(8,128)(2,1)S(1)}, f32[8,128]{1,0:T(8,128)S(1)}) custom-call(s32[4,8]{1,0:T(4,128)} %pattern_ref.3, s32[2]{0:T(128)S(1)} %pad_add_fusion.place_ref, bf16[512,1024]{1,0:T(8,128)(2,1)} %rest_0_.1), custom_call_target="tpu_custom_call" | custom-call | flops 2000000000 | bytes 1048576 | tf_op jit(solution)/shard_map/pack/pallas_call | solution.py:318
  10.3 1.7 collective-permute-done
  12.6 1.2 broadcast_in_dim.6
  13.9 9.7 %all-to-all-start = ((bf16[64,80,128]{2,1,0:T(8,128)(2,1)}), bf16[64,80,128]{2,1,0:T(8,128)(2,1)}, u32[]{:S(2)}, u32[]{:S(2)}) async-start(bf16[64,80,128]{2,1,0:T(8,128)(2,1)} %broadcast_in_dim.6), calls=%async_computation | async-start | bytes 2621440 | tf_op jit(solution)/shard_map/all_to_all | solution.py:285
  23.5 1.3 collective-permute-start.4
  24.9 1.4 collective-permute-start.3
  27.9 26.6 %collective-permute-done.4 = bf16[20,128,128]{2,1,0:T(8,128)(2,1)} collective-permute-done((bf16[20,128,128]{2,1,0:T(8,128)(2,1)S(1)}, bf16[20,128,128]{2,1,0:T(8,128)(2,1)}, u32[]{:S(2)}, u32[]{:S(2)}) %collective-permute-start.4) | collective-permute-done | bytes 655392 | tf_op jit(solution)/shard_map/ppermute | solution.py:293
  55.8 1.4 collective-permute-start.9
  57.9 14.2 %collective-permute-done.12 = bf16[20,128,128]{2,1,0:T(8,128)(2,1)} collective-permute-done((bf16[20,128,128]{2,1,0:T(8,128)(2,1)S(1)}, bf16[20,128,128]{2,1,0:T(8,128)(2,1)}, u32[]{:S(2)}, u32[]{:S(2)}) %collective-permute-start.12) | collective-permute-done | bytes 655392 | tf_op jit(solution)/shard_map/ppermute | solution.py:344
  73.6 1.4 collective-permute-start.20
  75.0 1.4 constant_dynamic-update-slice_fusion.1
  77.5 1.4 collective-permute-start.16
  78.9 2.1 %collective-permute-start.11 = (bf16[20,128,128]{2,1,0:T(8,128)(2,1)}, bf16[20,128,128]{2,1,0:T(8,128)(2,1)}, u32[]{:S(2)}, u32[]{:S(2)}) collective-permute-start(bf16[20,128,128]{2,1,0:T(8,128)(2,1)} %collective-permute-done.9), channel_id=1, source_target_pairs={{6,0},{7,1},{0,2},{1,3},{2,4},{3,5},{4,6},{5,7},{14,8},{15,9},{8,1... | collective-permute-start | bytes 1966088 | tf_op jit(solution)/shard_map/ppermute | solution.py:289
  81.2 8.3 %grid_rows.1 = (bf16[4,128,128]{2,1,0:T(8,128)(2,1)S(1)}, f32[1,128]{1,0:T(1,128)S(1)}) custom-call(s32[2]{0:T(128)S(1)} %pad_add_fusion.place_ref, s32[64]{0:T(128)S(1)} %copy-done.5, f32[1]{0:T(128)S(6)} %copy.24.shift_ref, bf16[128,80,128]{2,1,0:T(8,128)(2,1)S(1)} %constant_dynamic-update-slice_fusion.bricks_ref, s32[3,64,128]{2,1,0:T(8,128)S(1)} %copy-done.1, ...), custom_call_target="tpu_custom_call" | custom-call | flops 8800000000 | bytes 1048576 | tf_op jit(solution)/shard_map/grid_rows/pallas_call | solution.py:360
  90.1 9.2 %all-to-all-start.1 = ((f32[128,1,128]{2,1,0:T(1,128)}), f32[128,1,128]{2,1,0:T(1,128)S(1)}, u32[]{:S(2)}, u32[]{:S(2)}) async-start(f32[128,1,128]{2,1,0:T(1,128)} %broadcast_in_dim.8), calls=%async_computation.1 | async-start | bytes 131072 | tf_op jit(solution)/shard_map/all_to_all | solution.py:285
  100.1 1.8 collective-permute-done.16
  102.4 2.4 %collective-permute-start.19 = (bf16[20,128,128]{2,1,0:T(8,128)(2,1)}, bf16[20,128,128]{2,1,0:T(8,128)(2,1)}, u32[]{:S(2)}, u32[]{:S(2)}) collective-permute-start(bf16[20,128,128]{2,1,0:T(8,128)(2,1)} %collective-permute-done.16), channel_id=1, source_target_pairs={{0,8},{8,0},{16,24},{24,16},{32,40},{40,32},{48,56},{56,48},{64,72... | collective-permute-start | bytes 1966088 | tf_op jit(solution)/shard_map/ppermute | solution.py:306
  106.8 8.3 %grid_cols.1 = bf16[4,128,128]{2,1,0:T(8,128)(2,1)S(1)} custom-call(s32[2]{0:T(128)S(1)} %pad_add_fusion.place_ref, s32[64]{0:T(128)S(1)} %copy-done.5, f32[1]{0:T(128)S(6)} %copy.24.shift_ref, bf16[128,80,128]{2,1,0:T(8,128)(2,1)S(1)} %constant_dynamic-update-slice_fusion.bricks_ref, s32[3,64,128]{2,1,0:T(8,128)S(1)} %copy-done.1, f32[64,128]{1,0:T(8,128)S(1)} %copy-done.3, ...), custom_call_target="tpu_custom_call" | custom-call | flops 8800000000 | bytes 1048576 | tf_op jit(solution)/shard_map/grid_cols/pallas_call | solution.py:360
  116.3 1.5 collective-permute-done.7
  117.8 1.4 collective-permute-start.24
  119.1 12.7 %collective-permute-done.10 = bf16[20,128,128]{2,1,0:T(8,128)(2,1)} collective-permute-done((bf16[20,128,128]{2,1,0:T(8,128)(2,1)}, bf16[20,128,128]{2,1,0:T(8,128)(2,1)}, u32[]{:S(2)}, u32[]{:S(2)}) %collective-permute-start.10) | collective-permute-done | bytes 655392 | tf_op jit(solution)/shard_map/ppermute | solution.py:289
  133.2 24.2 %plan.1 = (s32[40]{0:T(128)S(1)}, s32[2304]{0:T(1024)S(1)}, s32[2304]{0:T(1024)S(1)}, s32[1]{0:T(128)}) custom-call(s32[2]{0:T(128)S(1)} %pad_add_fusion.place_ref, bf16[128,80,128]{2,1,0:T(8,128)(2,1)} %copy-done), custom_call_target="tpu_custom_call" | custom-call | flops 5000000000 | bytes 1048576 | tf_op jit(solution)/shard_map/plan/pallas_call | solution.py:389
  158.2 15.5 %conditional.1 = ((bf16[512,1024]{1,0:T(8,128)(2,1)}, bf16[512,1024]{1,0:T(8,128)(2,1)})) conditional(s32[]{:T(128)} %bitcast.5, (s32[2]{0:T(128)S(1)}, s32[4,8]{1,0:T(4,128)S(1)}, f32[1]{0:T(128)}, s32[40]{0:T(128)S(1)}, s32[2304]{0:T(1024)S(1)}, /*index=5*/s32[2304]{0:T(1024)S(1)}, f32[128,128]{1,0:T(8,128)S(1)}, bf16[512,1024]{1,0:T(8,128)(2,1)S(1)}, ...), branch_computations={%region_0.0_spmd, %region_1.0_spmd} | conditional | flops 12000000000 | bytes 121439128 | solution.py:442
  158.2 15.2 %product.1 = (bf16[512,1024]{1,0:T(8,128)(2,1)}, bf16[512,1024]{1,0:T(8,128)(2,1)}) custom-call(s32[2]{0:T(128)S(1)} %get-tuple-element.82.place_ref, s32[4,8]{1,0:T(4,128)S(1)} %get-tuple-element.83.pattern_ref, f32[1]{0:T(128)} %get-tuple-element.84.shift_ref, s32[40]{0:T(128)S(1)} %get-tuple-element.85.start_ref, s32[2304]{0:T(1024)S(1)} %get-tuple-element.86.left_ref, ...), custom_call_target="tpu_custom_call" | custom-call | flops 12000000000 | bytes 1048576 | tf_op jit(solution)/shard_map/cond/branch_0_fun/product/pallas_call | solution.py:408
  (72 shorter events, 13.6 us)
Async XLA Ops:
  13.9 40.7 %all-to-all-start = ((bf16[64,80,128]{2,1,0:T(8,128)(2,1)}), bf16[64,80,128]{2,1,0:T(8,128)(2,1)}, u32[]{:S(2)}, u32[]{:S(2)}) async-start(bf16[64,80,128]{2,1,0:T(8,128)(2,1)} %broadcast_in_dim.6), calls=%async_computation | async-start | bytes 2621440 | tf_op jit(solution)/shard_map/all_to_all | solution.py:285
  23.5 31.0 %collective-permute-start.4 = (bf16[20,128,128]{2,1,0:T(8,128)(2,1)S(1)}, bf16[20,128,128]{2,1,0:T(8,128)(2,1)}, u32[]{:S(2)}, u32[]{:S(2)}) collective-permute-start(bf16[20,128,128]{2,1,0:T(8,128)(2,1)S(1)} %bitcast.35), channel_id=1, source_target_pairs={{48,0},{56,8},{0,16},{8,24},{16,32},{24,40},{32,48},{40,56},{112,6... | collective-permute-start | bytes 1966088 | tf_op jit(solution)/shard_map/ppermute | solution.py:293
  24.9 29.7 %collective-permute-start.3 = (bf16[20,128,128]{2,1,0:T(8,128)(2,1)S(1)}, bf16[20,128,128]{2,1,0:T(8,128)(2,1)}, u32[]{:S(2)}, u32[]{:S(2)}) collective-permute-start(bf16[20,128,128]{2,1,0:T(8,128)(2,1)S(1)} %bitcast.36), channel_id=1, source_target_pairs={{16,0},{24,8},{32,16},{40,24},{48,32},{56,40},{0,48},{8,56},{80,64... | collective-permute-start | bytes 1966088 | tf_op jit(solution)/shard_map/ppermute | solution.py:293
  26.3 28.2 %collective-permute-start.2 = (bf16[20,128,128]{2,1,0:T(8,128)(2,1)S(1)}, bf16[20,128,128]{2,1,0:T(8,128)(2,1)S(1)}, u32[]{:S(2)}, u32[]{:S(2)}) collective-permute-start(bf16[20,128,128]{2,1,0:T(8,128)(2,1)S(1)} %bitcast.37), channel_id=1, source_target_pairs={{6,0},{7,1},{0,2},{1,3},{2,4},{3,5},{4,6},{5,7},{14,8},{15,9},{8,1... | collective-permute-start | bytes 1966088 | tf_op jit(solution)/shard_map/ppermute | solution.py:289
  26.5 28.0 %collective-permute-start.1 = (bf16[20,128,128]{2,1,0:T(8,128)(2,1)S(1)}, bf16[20,128,128]{2,1,0:T(8,128)(2,1)}, u32[]{:S(2)}, u32[]{:S(2)}) collective-permute-start(bf16[20,128,128]{2,1,0:T(8,128)(2,1)S(1)} %bitcast.38), channel_id=1, source_target_pairs={{2,0},{3,1},{4,2},{5,3},{6,4},{7,5},{0,6},{1,7},{10,8},{11,9},{12,... | collective-permute-start | bytes 1966088 | tf_op jit(solution)/shard_map/ppermute | solution.py:289
  27.8 28.1 %collective-permute-start.8 = (bf16[20,128,128]{2,1,0:T(8,128)(2,1)S(1)}, bf16[20,128,128]{2,1,0:T(8,128)(2,1)}, u32[]{:S(2)}, u32[]{:S(2)}) collective-permute-start(bf16[20,128,128]{2,1,0:T(8,128)(2,1)S(1)} %bitcast.39), channel_id=1, source_target_pairs={{0,64},{1,65},{2,66},{3,67},{4,68},{5,69},{6,70},{7,71},{8,73},{9,... | collective-permute-start | bytes 1966088 | tf_op jit(solution)/shard_map/ppermute | solution.py:302
  54.6 24.3 %collective-permute-start.5 = (bf16[64,80,128]{2,1,0:T(8,128)(2,1)}, bf16[64,80,128]{2,1,0:T(8,128)(2,1)S(1)}, u32[]{:S(2)}, u32[]{:S(2)}) collective-permute-start(bf16[64,80,128]{2,1,0:T(8,128)(2,1)} %all-to-all-done), channel_id=1, source_target_pairs={{0,8},{8,0},{16,24},{24,16},{32,40},{40,32},{48,56},{56,48},{64,72... | collective-permute-start | bytes 3932168 | tf_op jit(solution)/shard_map/ppermute | solution.py:306
  55.7 16.4 %collective-permute-start.12 = (bf16[20,128,128]{2,1,0:T(8,128)(2,1)S(1)}, bf16[20,128,128]{2,1,0:T(8,128)(2,1)}, u32[]{:S(2)}, u32[]{:S(2)}) collective-permute-start(bf16[20,128,128]{2,1,0:T(8,128)(2,1)S(1)} %bitcast.40), channel_id=1, source_target_pairs={{0,64},{8,72},{16,80},{24,88},{32,96},{40,104},{48,112},{56,120},{... | collective-permute-start | bytes 1966088 | tf_op jit(solution)/shard_map/ppermute | solution.py:344
  55.8 21.7 %collective-permute-start.9 = (bf16[20,128,128]{2,1,0:T(8,128)(2,1)}, bf16[20,128,128]{2,1,0:T(8,128)(2,1)}, u32[]{:S(2)}, u32[]{:S(2)}) collective-permute-start(bf16[20,128,128]{2,1,0:T(8,128)(2,1)} %collective-permute-done.8), channel_id=1, source_target_pairs={{0,64},{1,65},{2,66},{3,67},{4,68},{5,69},{6,70},{7,71},{8,73},{9,... | collective-permute-start | bytes 1966088 | tf_op jit(solution)/shard_map/ppermute | solution.py:302
  72.1 27.2 %collective-permute-start.14 = (bf16[20,128,128]{2,1,0:T(8,128)(2,1)}, bf16[20,128,128]{2,1,0:T(8,128)(2,1)}, u32[]{:S(2)}, u32[]{:S(2)}) collective-permute-start(bf16[20,128,128]{2,1,0:T(8,128)(2,1)} %collective-permute-done.12), channel_id=1, source_target_pairs={{16,0},{24,8},{32,16},{40,24},{48,32},{56,40},{0,48},{8,56},{80,64... | collective-permute-start | bytes 1966088 | tf_op jit(solution)/shard_map/ppermute | solution.py:293
  73.0 26.8 %collective-permute-start.13 = (bf16[20,128,128]{2,1,0:T(8,128)(2,1)}, bf16[20,128,128]{2,1,0:T(8,128)(2,1)}, u32[]{:S(2)}, u32[]{:S(2)}) collective-permute-start(bf16[20,128,128]{2,1,0:T(8,128)(2,1)} %collective-permute-done.12), channel_id=1, source_target_pairs={{48,0},{56,8},{0,16},{8,24},{16,32},{24,40},{32,48},{40,56},{112,6... | collective-permute-start | bytes 1966088 | tf_op jit(solution)/shard_map/ppermute | solution.py:293
  73.6 32.1 %collective-permute-start.20 = (bf16[20,128,128]{2,1,0:T(8,128)(2,1)}, bf16[20,128,128]{2,1,0:T(8,128)(2,1)}, u32[]{:S(2)}, u32[]{:S(2)}) collective-permute-start(bf16[20,128,128]{2,1,0:T(8,128)(2,1)} %collective-permute-done.4), channel_id=1, source_target_pairs={{0,8},{8,0},{16,24},{24,16},{32,40},{40,32},{48,56},{56,48},{64,72... | collective-permute-start | bytes 1966088 | tf_op jit(solution)/shard_map/ppermute | solution.py:306
  77.5 24.4 %collective-permute-start.16 = (bf16[20,128,128]{2,1,0:T(8,128)(2,1)}, bf16[20,128,128]{2,1,0:T(8,128)(2,1)}, u32[]{:S(2)}, u32[]{:S(2)}) collective-permute-start(bf16[20,128,128]{2,1,0:T(8,128)(2,1)} %collective-permute-done.3), channel_id=1, source_target_pairs={{16,0},{24,8},{32,16},{40,24},{48,32},{56,40},{0,48},{8,56},{80,64... | collective-permute-start | bytes 1966088 | tf_op jit(solution)/shard_map/ppermute | solution.py:293
  78.9 23.6 %collective-permute-start.11 = (bf16[20,128,128]{2,1,0:T(8,128)(2,1)}, bf16[20,128,128]{2,1,0:T(8,128)(2,1)}, u32[]{:S(2)}, u32[]{:S(2)}) collective-permute-start(bf16[20,128,128]{2,1,0:T(8,128)(2,1)} %collective-permute-done.9), channel_id=1, source_target_pairs={{6,0},{7,1},{0,2},{1,3},{2,4},{3,5},{4,6},{5,7},{14,8},{15,9},{8,1... | collective-permute-start | bytes 1966088 | tf_op jit(solution)/shard_map/ppermute | solution.py:289
  99.8 18.0 %collective-permute-start.7 = (bf16[20,128,128]{2,1,0:T(8,128)(2,1)}, bf16[20,128,128]{2,1,0:T(8,128)(2,1)}, u32[]{:S(2)}, u32[]{:S(2)}) collective-permute-start(bf16[20,128,128]{2,1,0:T(8,128)(2,1)} %collective-permute-done.1), channel_id=1, source_target_pairs={{2,0},{3,1},{4,2},{5,3},{6,4},{7,5},{0,6},{1,7},{10,8},{11,9},{12,... | collective-permute-start | bytes 1966088 | tf_op jit(solution)/shard_map/ppermute | solution.py:289
  101.9 30.0 %collective-permute-start.10 = (bf16[20,128,128]{2,1,0:T(8,128)(2,1)}, bf16[20,128,128]{2,1,0:T(8,128)(2,1)}, u32[]{:S(2)}, u32[]{:S(2)}) collective-permute-start(bf16[20,128,128]{2,1,0:T(8,128)(2,1)} %collective-permute-done.9), channel_id=1, source_target_pairs={{2,0},{3,1},{4,2},{5,3},{6,4},{7,5},{0,6},{1,7},{10,8},{11,9},{12,... | collective-permute-start | bytes 1966088 | tf_op jit(solution)/shard_map/ppermute | solution.py:289
  102.4 29.4 %collective-permute-start.19 = (bf16[20,128,128]{2,1,0:T(8,128)(2,1)}, bf16[20,128,128]{2,1,0:T(8,128)(2,1)}, u32[]{:S(2)}, u32[]{:S(2)}) collective-permute-start(bf16[20,128,128]{2,1,0:T(8,128)(2,1)} %collective-permute-done.16), channel_id=1, source_target_pairs={{0,8},{8,0},{16,24},{24,16},{32,40},{40,32},{48,56},{56,48},{64,72... | collective-permute-start | bytes 1966088 | tf_op jit(solution)/shard_map/ppermute | solution.py:306
  105.7 27.1 %collective-permute-start.17 = (bf16[20,128,128]{2,1,0:T(8,128)(2,1)}, bf16[20,128,128]{2,1,0:T(8,128)(2,1)}, u32[]{:S(2)}, u32[]{:S(2)}) collective-permute-start(bf16[20,128,128]{2,1,0:T(8,128)(2,1)} %collective-permute-done.13), channel_id=1, source_target_pairs={{48,0},{56,8},{0,16},{8,24},{16,32},{24,40},{32,48},{40,56},{112,6... | collective-permute-start | bytes 1966088 | tf_op jit(solution)/shard_map/ppermute | solution.py:293
  115.1 17.6 %collective-permute-start.6 = (bf16[4,128,128]{2,1,0:T(8,128)(2,1)S(1)}, bf16[4,128,128]{2,1,0:T(8,128)(2,1)S(1)}, u32[]{:S(2)}, u32[]{:S(2)}) collective-permute-start(bf16[4,128,128]{2,1,0:T(8,128)(2,1)S(1)} %grid_cols.1), channel_id=1, source_target_pairs={{0,8},{8,0},{16,24},{24,16},{32,40},{40,32},{48,56},{56,48},{64,72... | collective-permute-start | bytes 393224 | tf_op jit(solution)/shard_map/ppermute | solution.py:306
  117.8 40.4 %collective-permute-start.24 = (bf16[20,128,128]{2,1,0:T(8,128)(2,1)}, bf16[20,128,128]{2,1,0:T(8,128)(2,1)}, u32[]{:S(2)}, u32[]{:S(2)}) collective-permute-start(bf16[20,128,128]{2,1,0:T(8,128)(2,1)} %collective-permute-done.13), channel_id=1, source_target_pairs={{0,8},{8,0},{16,24},{24,16},{32,40},{40,32},{48,56},{56,48},{64,72... | collective-permute-start | bytes 1966088 | tf_op jit(solution)/shard_map/ppermute | solution.py:306
  131.8 26.3 %collective-permute-start.15 = (bf16[20,128,128]{2,1,0:T(8,128)(2,1)}, bf16[20,128,128]{2,1,0:T(8,128)(2,1)}, u32[]{:S(2)}, u32[]{:S(2)}) collective-permute-start(bf16[20,128,128]{2,1,0:T(8,128)(2,1)} %collective-permute-done.11), channel_id=1, source_target_pairs={{6,0},{7,1},{0,2},{1,3},{2,4},{3,5},{4,6},{5,7},{14,8},{15,9},{8,1... | collective-permute-start | bytes 1966088 | tf_op jit(solution)/shard_map/ppermute | solution.py:289
  131.8 26.3 %collective-permute-start.21 = (bf16[20,128,128]{2,1,0:T(8,128)(2,1)}, bf16[20,128,128]{2,1,0:T(8,128)(2,1)}, u32[]{:S(2)}, u32[]{:S(2)}) collective-permute-start(bf16[20,128,128]{2,1,0:T(8,128)(2,1)} %collective-permute-done.12), channel_id=1, source_target_pairs={{0,8},{8,0},{16,24},{24,16},{32,40},{40,32},{48,56},{56,48},{64,72... | collective-permute-start | bytes 1966088 | tf_op jit(solution)/shard_map/ppermute | solution.py:306
  132.7 25.4 %collective-permute-start.22 = (bf16[20,128,128]{2,1,0:T(8,128)(2,1)}, bf16[20,128,128]{2,1,0:T(8,128)(2,1)}, u32[]{:S(2)}, u32[]{:S(2)}) collective-permute-start(bf16[20,128,128]{2,1,0:T(8,128)(2,1)} %collective-permute-done.14), channel_id=1, source_target_pairs={{0,8},{8,0},{16,24},{24,16},{32,40},{40,32},{48,56},{56,48},{64,72... | collective-permute-start | bytes 1966088 | tf_op jit(solution)/shard_map/ppermute | solution.py:306
  132.8 25.3 %collective-permute-start.23 = (bf16[20,128,128]{2,1,0:T(8,128)(2,1)}, bf16[20,128,128]{2,1,0:T(8,128)(2,1)}, u32[]{:S(2)}, u32[]{:S(2)}) collective-permute-start(bf16[20,128,128]{2,1,0:T(8,128)(2,1)} %collective-permute-done.17), channel_id=1, source_target_pairs={{0,8},{8,0},{16,24},{24,16},{32,40},{40,32},{48,56},{56,48},{64,72... | collective-permute-start | bytes 1966088 | tf_op jit(solution)/shard_map/ppermute | solution.py:306
  (18 other events, 424.8 us)

commit v2 on v1

--- a/solution.py
+++ b/solution.py
@@ -9,10 +9,11 @@
 
 BS = 128
 CAP = 20
-GROUP = 8
+GROUP = 4
+TURN = 4
 ORDER = 8192
 VOLUME = 0.015625
-LISTED = 2048 + 32 * GROUP
+LISTED = 2048 + 32 * GROUP + TURN * GROUP
 F32 = jnp.float32
 BF16 = jnp.bfloat16
 
@@ -141,62 +142,76 @@
 
 
 def plan_kernel(
-    place_ref, bricks_ref, start_ref, left_ref, right_ref, most_ref, slots_ref, slots, kept_k, kept_slot, kept_device, sem
+    place_ref, bricks_ref, turns_ref, out_ref, left_ref, right_ref, most_ref, slots_ref, slots, kept_left, kept_right, kept_at, sem
 ):
     row, col = place_ref[0], place_ref[1]
     kept = jnp.sum(bricks_ref[:, 64:80, :].astype(F32), axis=1)
-    earlier = lax.broadcasted_iota(jnp.int32, (BS, BS), 0) < lax.broadcasted_iota(jnp.int32, (BS, BS), 1)
-    before = jnp.dot(kept.astype(BF16), earlier.astype(BF16), preferred_element_type=F32)
-    slots_ref[...] = jnp.where(kept > 0.5, before, -1.0).astype(jnp.int32)
-    most_ref[0] = jnp.max(jnp.sum(kept, axis=1, keepdims=True)).astype(jnp.int32)
+    kept = kept.T
+    earlier = lax.broadcasted_iota(jnp.int32, (BS, BS), 1) < lax.broadcasted_iota(jnp.int32, (BS, BS), 0)
+    before = jnp.dot(earlier.astype(BF16), kept.astype(BF16), preferred_element_type=F32)
+    slots_ref[...] = jnp.where(kept > 0.5, before, -1.0)[:40].astype(jnp.int32)
+    most_ref[0] = jnp.max(jnp.sum(kept, axis=0, keepdims=True)).astype(jnp.int32)
     copy = pltpu.make_async_copy(slots_ref, slots, sem)
     copy.start()
     copy.wait()
 
-    def left_row(i, number):
-        def piece(other, number):
+    def block_row(i, number):
+        def piece(other, count):
             device = row // 2 * 8 + other
             base = ((other ^ col) % 2 * 4 + (other // 2 - col // 2) % 4) * CAP
+            right = ((other // 4 ^ row // 8) * 4 + (other - row // 2) % 4) * 2 * CAP
             for j in range(8):
-                slot = slots[device, i * 8 + j]
-                holder = other * 2 + j // 4
-                kept_slot[number] = base + slot
-                kept_device[number] = (holder ^ row) % 2 * 64 + other * 8 + col
-                kept_k[number] = other * 8 + j
-                number += (slot >= 0).astype(jnp.int32)
-            return number
-
-        return lax.fori_loop(0, 8, piece, number)
-
-    def block_row(i, number):
-        count = left_row(i, jnp.int32(0))
+                slot = slots[i * 8 + j, device]
+                kept_left[count] = base + slot
+                kept_right[count] = right + j // 4 * CAP
+                kept_at[count] = j % 4 * 8 * BS + (j // 4 ^ row) % 2 * 64 + other * 8 + col
+                count += (slot >= 0).astype(jnp.int32)
+            return count
+
+        count = lax.fori_loop(0, 8, piece, jnp.int32(0))
+        for more in range(3):
+            kept_left[count + more] = 0
+            kept_right[count + more] = 0
+            kept_at[count + more] = 32 * BS
 
         def block(j, number):
-            start_ref[i * 8 + j] = number // GROUP
-
             def listing(number):
-                def entry(n, number):
-                    k = kept_k[n]
-                    holder = k // 4
-                    slot = slots[kept_device[n], k % 4 * 8 + j]
-                    base = (holder ^ row) % 2 * 8 + (holder // 8 ^ row // 8) * 4 + (holder // 2 - row // 2) % 4
-                    left_ref[number] = kept_slot[n]
-                    right_ref[number] = base * CAP + slot
-                    return number + (slot >= 0).astype(jnp.int32)
-
-                number = lax.fori_loop(0, count, entry, number)
+                start = number // GROUP
+                def four(n, number):
+                    for inner in range(4):
+                        at = kept_at[n * 4 + inner] + j * BS
+                        slot = slots[at >> 7, at & 127]
+                        left_ref[number] = kept_left[n * 4 + inner]
+                        right_ref[number] = kept_right[n * 4 + inner] + slot
+                        number += (slot >= 0).astype(jnp.int32)
+                    return number
+
+                number = lax.fori_loop(0, (count + 3) // 4, four, number)
                 for more in range(GROUP - 1):
                     left_ref[number + more] = 8 * CAP
                     right_ref[number + more] = 0
-                return (number + GROUP - 1) // GROUP * GROUP
-
-            wanted = slots[row // 2 * 8 + col, i * 8 + j] >= 0
+                end = (number + GROUP - 1) // GROUP
+
+                def name(group, carry):
+                    out_ref[group] = i * 8 + j
+                    return carry
+
+                lax.fori_loop(start, end, name, 0)
+                return end * GROUP
+
+            wanted = slots[i * 8 + j, row // 2 * 8 + col] >= 0
             return lax.cond(wanted, listing, lambda n: n, number)
 
         return lax.fori_loop(0, 8, block, number)
 
     number = lax.fori_loop(0, 4, block_row, jnp.int32(0))
-    start_ref[32] = number // GROUP
+    groups = number // GROUP
+    for more in range(TURN):
+        out_ref[groups + more] = 32
+        for inner in range(GROUP):
+            left_ref[number + more * GROUP + inner] = 8 * CAP
+            right_ref[number + more * GROUP + inner] = 0
+    turns_ref[0] = (groups + TURN - 1) // TURN
 
 
 def scaling(frob_ref):
@@ -205,22 +220,49 @@
 
 
 def product_kernel(
-    place_ref, pattern_ref, shift_ref, start_ref, left_ref, right_ref, frob_ref, core_ref, row_grid_ref, col_own_ref, col_other_ref,
+    place_ref, pattern_ref, shift_ref, turns_ref, out_ref, left_ref, right_ref, frob_ref, core_ref, row_grid_ref, col_own_ref, col_other_ref,
     *rest
 ):
-    lefts, rights = rest[:8], rest[8:24]
-    scaled_ref, square_ref, left_all, right_all, acc_ref, col_grid_ref, sems = rest[24:]
-    parts = [(left_all, k, ref) for k, ref in enumerate(lefts)] + [(right_all, k, ref) for k, ref in enumerate(rights)]
+    payload, crossed, own_role, other_role = rest[0], rest[1], rest[2:9], rest[9:16]
+    scaled_ref, square_ref, left_all, right_all, acc_ref, col_grid_ref, sems = rest[16:]
+    core = place_ref[0] % 2
+
+    def part(whole, at, size, source, number):
+        return pltpu.make_async_copy(source, whole.at[pl.ds(at, size)], sems.at[number])
+
     copies = [
-        pltpu.make_async_copy(ref, whole.at[pl.ds(k * CAP, CAP)], sems.at[n])
-        for n, (whole, k, ref) in enumerate(parts)
+        part(left_all, 0, CAP, payload, 0),
+        part(right_all, core * CAP, CAP, payload, 1),
+        part(right_all, (1 - core) * CAP, CAP, crossed, 2),
     ]
     for copy in copies:
         copy.start()
+    for k in range(1, 8):
+        mine, others = own_role[k - 1], other_role[k - 1]
+        of_core_0 = [
+            part(left_all, k * CAP, CAP, others.at[pl.ds(CAP, CAP)], 1 + 2 * k),
+            part(right_all, 2 * k * CAP, 2 * CAP, mine, 2 + 2 * k),
+        ]
+        of_core_1 = [
+            part(left_all, k * CAP, CAP, mine.at[pl.ds(0, CAP)], 1 + 2 * k),
+            part(right_all, 2 * k * CAP, 2 * CAP, others, 2 + 2 * k),
+        ]
+        copies += of_core_0
+
+        @pl.when(core == 0)
+        def _():
+            for copy in of_core_0:
+                copy.start()
+
+        @pl.when(core == 1)
+        def _():
+            for copy in of_core_1:
+                copy.start()
+
     left_all[8 * CAP] = jnp.zeros((BS, BS), BF16)
+    acc_ref[32] = jnp.zeros((BS, BS), F32)
     first_row = place_ref[0] * 4
     first_col = place_ref[1] * 8
-    core = place_ref[0] % 2
     for n in range(4):
         col_grid_ref[core * 4 + n] = col_own_ref[n]
         col_grid_ref[(1 - core) * 4 + n] = col_other_ref[n]
@@ -259,20 +301,25 @@
     for copy in copies:
         copy.wait()
 
+    def turn(t, carry):
+        sums = []
+        for group in range(TURN):
+            at = [(t * TURN + group) * GROUP + n for n in range(GROUP)]
+            left = jnp.concatenate([left_all[left_ref[n]] for n in at], axis=1)
+            right = jnp.concatenate([right_all[right_ref[n]] for n in at], axis=0)
+            sums.append(dot(left, right))
+        for group in range(TURN):
+            acc_ref[out_ref[t * TURN + group]] += sums[group]
+        return carry
+
+    lax.fori_loop(0, turns_ref[0], turn, 0)
     for i in range(4):
         for j in range(8):
             block = (slice(i * BS, (i + 1) * BS), slice(j * BS, (j + 1) * BS))
 
             @pl.when(pattern_ref[i, j] != 0)
             def _():
-                def group(k, acc):
-                    at = [k * GROUP + n for n in range(GROUP)]
-                    left = jnp.concatenate([left_all[left_ref[n]] for n in at], axis=1)
-                    right = jnp.concatenate([right_all[right_ref[n]] for n in at], axis=0)
-                    return acc + dot(left, right)
-
-                acc = lax.fori_loop(start_ref[i * 8 + j], start_ref[i * 8 + j + 1], group, acc_ref[i * 8 + j])
-                square_ref[block] = (acc * (scale * scale)).astype(BF16)
+                square_ref[block] = (acc_ref[i * 8 + j] * (scale * scale)).astype(BF16)
 
 
 VM = pl.BlockSpec(memory_space=pltpu.VMEM)
@@ -285,21 +332,29 @@
     return lax.all_to_all(copies, axis, 0, 0, axis_index_groups=groups)
 
 
-def along_z(value, off):
-    return lax.ppermute(value, "col", [((k + 2 * off) % 8, k) for k in range(8)])
-
-
-def along_x(value, off):
-    return lax.ppermute(value, "row", [(k // 8 * 8 + (k + 2 * off) % 8, k) for k in range(16)])
-
-
-def half_round_y(value):
-    pairs = []
-    for row in range(16):
-        for col in range(8):
-            y = (col % 2 * 2 + row // 8 + (1 if row % 2 == 0 else 3)) % 4
-            pairs.append((row * 8 + col, (y % 2 * 8 + row % 8) * 8 + col // 2 * 2 + y // 2))
-    return lax.ppermute(value, ("row", "col"), pairs)
+def place_of(device):
+    row, col = device // 8, device % 8
+    return row // 2 % 4, col % 2 * 2 + row // 8, col // 2, row % 2
+
+
+def device_of(x, y, z, core):
+    return ((y % 2 * 4 + x % 4) * 2 + core) * 8 + z % 4 * 2 + y // 2
+
+
+def move(value, where):
+    return lax.ppermute(value, ("row", "col"), [(k, device_of(*where(*place_of(k)))) for k in range(128)])
+
+
+def ring(value, off):
+    return move(value, lambda x, y, z, core: (x, y, z - off, core) if core else (x - off, y, z, core))
+
+
+def across_y(value):
+    return move(value, lambda x, y, z, core: (x, 3 - y if core else y ^ 1, z, core))
+
+
+def across_y_again(value):
+    return move(value, lambda x, y, z, core: (x, y ^ 1 if core else y, z, core))
 
 
 def to_core(value):
@@ -315,19 +370,6 @@
     col = lax.axis_index("col")
     place = jnp.stack([row, col]).astype(jnp.int32)
 
-    payload, squares = pl.pallas_call(
-        pack_kernel,
-        in_specs=[SM, SM, VM],
-        out_specs=[VM, VM],
-        out_shape=[jax.ShapeDtypeStruct((CAP * BS, BS), BF16), jax.ShapeDtypeStruct((8, BS), F32)],
-        compiler_params=params(),
-        cost_estimate=lasting(2),
-        name="pack",
-    )(pattern, place, core_matrix)
-    payload = payload.reshape(CAP, BS, BS)
-    own_crossed = to_core(payload)
-
-    (potential, _) = lax.optimization_barrier((potential, own_crossed))
     brick = pl.pallas_call(
         brick_kernel,
         in_specs=[SM, VM],
@@ -340,17 +382,27 @@
     same_core = [[row * 8 + col for row in range(core, 16, 2) for col in range(8)] for core in range(2)]
     half = to_all(brick, ("row", "col"), 64, same_core)
 
-    other_left = half_round_y(half_round_y(payload))
-    other_right = lax.ppermute(payload, "row", [(k, k ^ 8) for k in range(16)])
-    lefts = [payload, along_z(payload, 1), along_z(payload, -1)]
-    rights = [payload, along_x(payload, 1), along_x(payload, -1)]
-    half, *_ = lax.optimization_barrier((half, lefts[1], lefts[2], rights[1], rights[2]))
+    (core_after_brick, _) = lax.optimization_barrier((core_matrix, brick))
+    payload, squares = pl.pallas_call(
+        pack_kernel,
+        in_specs=[SM, SM, VM],
+        out_specs=[VM, VM],
+        out_shape=[jax.ShapeDtypeStruct((CAP * BS, BS), BF16), jax.ShapeDtypeStruct((8, BS), F32)],
+        compiler_params=params(),
+        cost_estimate=lasting(2),
+        name="pack",
+    )(pattern, place, core_after_brick)
+    payload = payload.reshape(CAP, BS, BS)
+    crossed = to_core(payload)
+
+    pair = jnp.concatenate([payload, crossed])
+    step = across_y(pair)
+    after, before = ring(pair, 1), ring(pair, -1)
+    half, step, after, before = lax.optimization_barrier((half, step, after, before))
+
+    far = ring(after, 1)
+    other = across_y_again(step)
     bricks = jnp.concatenate([half, to_core(half)])
-    lefts.insert(2, along_z(lefts[1], 1))
-    lefts += [other_left, along_z(other_left, 1), along_z(other_left, -1)]
-    rights.insert(2, along_x(rights[1], 1))
-    crossed = [own_crossed] + [to_core(piece) for piece in rights[1:]]
-    rights += [other_right, along_x(other_right, 1), along_x(other_right, -1)]
 
     def grid_blocks(count, with_sum, *more):
         extra = [VM, VM] if with_sum else []
@@ -373,54 +425,64 @@
         )(place, home, shift, bricks, centres, exponents, extents, *more)
 
     row_grid, total = grid_blocks(4, True, core_matrix, squares)
-    frob = to_all(total, ("row", "col"), 128).reshape(128, BS)
-
-    left_before, right_before, other_right, right_after, _ = lax.optimization_barrier(
-        (lefts[6], rights[6], other_right, rights[5], frob)
+    after, before, far, other, row_grid, total, bricks = lax.optimization_barrier(
+        (after, before, far, other, row_grid, total, bricks)
     )
-    lefts.insert(6, along_z(left_before, -1))
-    rights.insert(6, along_x(right_before, -1))
-    crossed += [to_core(piece) for piece in (other_right, right_after, rights[6], right_before)]
-    rights = rights + crossed
-
+
+    other_after, other_before = ring(other, 1), ring(other, -1)
+    crossings = [to_core(after), to_core(far), to_core(before)]
     (col_grid,) = grid_blocks(4, False)
-    col_grid_crossed = to_core(col_grid)
-
     *listed, most = pl.pallas_call(
         plan_kernel,
         in_specs=[SM, VM],
-        out_specs=[SM] * 4,
+        out_specs=[SM] * 5,
         out_shape=[
-            jax.ShapeDtypeStruct((40,), jnp.int32),
+            jax.ShapeDtypeStruct((1,), jnp.int32),
+            jax.ShapeDtypeStruct((LISTED // GROUP,), jnp.int32),
             jax.ShapeDtypeStruct((LISTED,), jnp.int32),
             jax.ShapeDtypeStruct((LISTED,), jnp.int32),
             jax.ShapeDtypeStruct((1,), jnp.int32),
         ],
-        scratch_shapes=[pltpu.VMEM((BS, BS), jnp.int32), pltpu.SMEM((BS, BS), jnp.int32)]
+        scratch_shapes=[pltpu.VMEM((40, BS), jnp.int32), pltpu.SMEM((40, BS), jnp.int32)]
         + [pltpu.SMEM((72,), jnp.int32)] * 3
         + [pltpu.SemaphoreType.DMA],
-        cost_estimate=lasting(5),
+        cost_estimate=lasting(7),
         name="plan",
     )(place, bricks)
+    other_after, other_before, col_grid, total, *rest = lax.optimization_barrier(
+        (other_after, other_before, col_grid, total, *crossings, *listed)
+    )
+    crossings, listed = rest[:3], rest[3:]
+
+    other_far = ring(other_before, -1)
+    crossings += [to_core(other), to_core(other_after), to_core(other_before)]
+    col_grid_crossed = to_core(col_grid)
+    frob = to_all(total, ("row", "col"), 128).reshape(128, BS)
+    other_far, col_grid_crossed, frob, *crossings = lax.optimization_barrier(
+        (other_far, col_grid_crossed, frob, *crossings)
+    )
+
+    crossings.insert(5, to_core(other_far))
+    own_role = [after, far, before, other, other_after, other_far, other_before]
     overflow = most[0] > CAP
 
     def sparse():
         return pl.pallas_call(
             product_kernel,
-            in_specs=[SM] * 6 + [VM] * 5 + [ANY] * 24,
+            in_specs=[SM] * 7 + [VM] * 5 + [ANY] * 16,
             out_specs=[VM, VM],
             out_shape=[jax.ShapeDtypeStruct((512, 1024), BF16)] * 2,
             scratch_shapes=[
                 pltpu.VMEM((8 * CAP + 1, BS, BS), BF16),
                 pltpu.VMEM((16 * CAP, BS, BS), BF16),
-                pltpu.VMEM((32, BS, BS), F32),
+                pltpu.VMEM((33, BS, BS), F32),
                 pltpu.VMEM((8, BS, BS), BF16),
-                pltpu.SemaphoreType.DMA((24,)),
+                pltpu.SemaphoreType.DMA((17,)),
             ],
             compiler_params=params(),
             cost_estimate=lasting(12),
             name="product",
-        )(place, pattern, shift, *listed, frob, core_matrix, row_grid, col_grid, col_grid_crossed, *lefts, *rights)
+        )(place, pattern, shift, *listed, frob, core_matrix, row_grid, col_grid, col_grid_crossed, payload, crossed, *own_role, *crossings)
 
     def dense():
         keep = pattern.astype(F32)[:, None, :, None]

time: 180 us -> 141 us (0.78)
  the two profiles are of different devices: /device:TPU:105 before, /device:TPU:1 now
where the time goes in v2:
time: 141 us; the launch traced here: 140 us
  Pallas kernels  40.4 us (29%)
  starting transfers between devices  28.9 us (20%)
  blocking collectives  28.4 us (20%)
  waiting for transfers between devices  24.3 us (17%)
  between operations  15.5 us (11%)
  local copies, waits for them, and re-layouts  2.71 us (2%)
    all_to_all x1, blocking collectives, to_all(): return lax.all_to_all(copies, axis, 0, 0, axis_index_groups=groups)  28.4 us
    pallas_call x2, Pallas kernels, grid_blocks(): pl.pallas_call(functools.partial(grid_kernel, count, with_sum), in_specs=...  17.9 us
    all_to_all x1, waiting for transfers between devices, to_all(): return lax.all_to_all(copies, axis, 0, 0, axis_index_groups=groups)  14 us
    ppermute x10, starting transfers between devices, to_core(): return lax.ppermute(value, 'row', [(k, k ^ 1) for k in range(16)])  11.9 us
    ppermute x8, starting transfers between devices, move(): lax.ppermute(value, ('row', 'col'), [(k, device_of(*where(*place_of(k))))...  11.5 us
    pallas_call x1, Pallas kernels, sparse(): pl.pallas_call(product_kernel, in_specs=[SM] * 7 + [VM] * 5 + [ANY] * 16,...  10.9 us
    pallas_call x1, Pallas kernels, body(): pl.pallas_call(plan_kernel, in_specs=[SM, VM], out_specs=[SM] * 5, out_sh...  9.15 us
    ppermute x8, waiting for transfers between devices, move(): lax.ppermute(value, ('row', 'col'), [(k, device_of(*where(*place_of(k))))...  6.41 us
  transfers between devices with their start and end apart: 19, of which 5 were waited for; matrix products, arithmetic and copies ran while one was open for 1% of the time, Pallas kernels for 19%

profile of v2, /device:TPU:1, one launch (start us, length us, event | category | flops | bytes accessed | tf_op | source)
XLA Modules:
  0.0 140.5 jit_solution(14653476939514643583)
XLA Ops:
  7.2 0.7 copy-done.3
  7.9 0.9 brick.1
  9.2 1.5 %pack.1 = (bf16[2560,128]{1,0:T(8,128)(2,1)S(1)}, f32[8,128]{1,0:T(8,128)S(1)}) custom-call(s32[4,8]{1,0:T(4,128)S(1)} %copy-done.10, s32[2]{0:T(128)S(1)} %pad_add_fusion.place_ref, bf16[512,1024]{1,0:T(8,128)(2,1)S(1)} %copy-done.7), custom_call_target="tpu_custom_call" | custom-call | flops 2000000000 | bytes 1048576 | tf_op jit(solution)/shard_map/pack/pallas_call | solution.py:386
  10.7 1.6 %collective-permute-start = (bf16[20,128,128]{2,1,0:T(8,128)(2,1)S(1)}, bf16[20,128,128]{2,1,0:T(8,128)(2,1)S(1)}, u32[]{:S(2)}, u32[]{:S(2)}) collective-permute-start(bf16[20,128,128]{2,1,0:T(8,128)(2,1)S(1)} %bitcast.32), channel_id=1, source_target_pairs={{0,8},{8,0},{16,24},{24,16},{32,40},{40,32},{48,56},{56,48},{64,72... | collective-permute-start | bytes 1966088 | tf_op jit(solution)/shard_map/ppermute | solution.py:361
  12.2 1.7 %collective-permute-done = bf16[20,128,128]{2,1,0:T(8,128)(2,1)S(1)} collective-permute-done((bf16[20,128,128]{2,1,0:T(8,128)(2,1)S(1)}, bf16[20,128,128]{2,1,0:T(8,128)(2,1)S(1)}, u32[]{:S(2)}, u32[]{:S(2)}) %collective-permute-start) | collective-permute-done | bytes 655392 | tf_op jit(solution)/shard_map/ppermute | solution.py:361
  14.1 1.7 %collective-permute-start.3 = (bf16[40,128,128]{2,1,0:T(8,128)(2,1)S(1)}, bf16[40,128,128]{2,1,0:T(8,128)(2,1)}, u32[]{:S(2)}, u32[]{:S(2)}) collective-permute-start(bf16[40,128,128]{2,1,0:T(8,128)(2,1)S(1)} %pad_maximum_fusion), channel_id=1, source_target_pairs={{0,16},{1,17},{2,18},{3,19},{4,20},{5,21},{6,22},{7,23},{8,10},{9,... | collective-permute-start | bytes 3932168 | tf_op jit(solution)/shard_map/ppermute | solution.py:345
  15.8 2.2 %collective-permute-start.2 = (bf16[40,128,128]{2,1,0:T(8,128)(2,1)S(1)}, bf16[40,128,128]{2,1,0:T(8,128)(2,1)}, u32[]{:S(2)}, u32[]{:S(2)}) collective-permute-start(bf16[40,128,128]{2,1,0:T(8,128)(2,1)S(1)} %pad_maximum_fusion), channel_id=1, source_target_pairs={{0,48},{1,49},{2,50},{3,51},{4,52},{5,53},{6,54},{7,55},{8,14},{9,... | collective-permute-start | bytes 3932168 | tf_op jit(solution)/shard_map/ppermute | solution.py:345
  18.1 2.7 %collective-permute-start.1 = (bf16[40,128,128]{2,1,0:T(8,128)(2,1)S(1)}, bf16[40,128,128]{2,1,0:T(8,128)(2,1)S(1)}, u32[]{:S(2)}, u32[]{:S(2)}) collective-permute-start(bf16[40,128,128]{2,1,0:T(8,128)(2,1)S(1)} %pad_maximum_fusion), channel_id=1, source_target_pairs={{0,64},{1,65},{2,66},{3,67},{4,68},{5,69},{6,70},{7,71},{8,73},{9,... | collective-permute-start | bytes 3932168 | tf_op jit(solution)/shard_map/ppermute | solution.py:345
  21.0 28.4 %all_to_all.10 = bf16[64,80,128]{2,1,0:T(8,128)(2,1)S(1)} all-to-all(bf16[64,80,128]{2,1,0:T(8,128)(2,1)S(1)} %broadcast_in_dim.6), channel_id=1, replica_groups={{0,1,2,3,4,5,6,7,16,17,18,19,20,21,22,23,32,33,34,35,36,37,38,39,48,49,..., dimensions={0} | all-to-all | bytes 2621440 | tf_op jit(solution)/shard_map/all_to_all | solution.py:332
  49.4 5.9 %collective-permute-start.6 = (bf16[64,80,128]{2,1,0:T(8,128)(2,1)S(1)}, bf16[64,80,128]{2,1,0:T(8,128)(2,1)S(1)}, u32[]{:S(2)}, u32[]{:S(2)}) collective-permute-start(bf16[64,80,128]{2,1,0:T(8,128)(2,1)S(1)} %all_to_all.10), channel_id=1, source_target_pairs={{0,8},{8,0},{16,24},{24,16},{32,40},{40,32},{48,56},{56,48},{64,72... | collective-permute-start | bytes 3932168 | tf_op jit(solution)/shard_map/ppermute | solution.py:361
  55.3 1.9 %collective-permute-start.5 = (bf16[40,128,128]{2,1,0:T(8,128)(2,1)S(1)}, bf16[40,128,128]{2,1,0:T(8,128)(2,1)}, u32[]{:S(2)}, u32[]{:S(2)}) collective-permute-start(bf16[40,128,128]{2,1,0:T(8,128)(2,1)S(1)} %collective-permute-done.1), channel_id=1, source_target_pairs={{0,0},{1,1},{2,2},{3,3},{4,4},{5,5},{6,6},{7,7},{8,72},{9,73},{10,... | collective-permute-start | bytes 3932168 | tf_op jit(solution)/shard_map/ppermute | solution.py:345
  58.9 9.0 %grid_rows.1 = (bf16[4,128,128]{2,1,0:T(8,128)(2,1)}, f32[1,128]{1,0:T(1,128)S(1)}) custom-call(s32[2]{0:T(128)S(1)} %pad_add_fusion.place_ref, s32[64]{0:T(128)S(1)} %copy-done.6, f32[1]{0:T(128)S(6)} %copy.24.shift_ref, bf16[128,80,128]{2,1,0:T(8,128)(2,1)S(1)} %constant_dynamic-update-slice_fusion.bricks_ref, s32[3,64,128]{2,1,0:T(8,128)S(1)} %copy-done.2, ...), custom_call_target="tpu_custom_call" | custom-call | flops 8800000000 | bytes 1048576 | tf_op jit(solution)/shard_map/grid_rows/pallas_call | solution.py:412
  67.9 6.1 %collective-permute-done.5 = bf16[40,128,128]{2,1,0:T(8,128)(2,1)} collective-permute-done((bf16[40,128,128]{2,1,0:T(8,128)(2,1)S(1)}, bf16[40,128,128]{2,1,0:T(8,128)(2,1)}, u32[]{:S(2)}, u32[]{:S(2)}) %collective-permute-start.5) | collective-permute-done | bytes 1310752 | tf_op jit(solution)/shard_map/ppermute | solution.py:345
  74.3 2.7 %collective-permute-start.7 = (bf16[40,128,128]{2,1,0:T(8,128)(2,1)}, bf16[40,128,128]{2,1,0:T(8,128)(2,1)}, u32[]{:S(2)}, u32[]{:S(2)}) collective-permute-start(bf16[40,128,128]{2,1,0:T(8,128)(2,1)} %collective-permute-done.5), channel_id=1, source_target_pairs={{0,48},{1,49},{2,50},{3,51},{4,52},{5,53},{6,54},{7,55},{8,14},{9,... | collective-permute-start | bytes 3932168 | tf_op jit(solution)/shard_map/ppermute | solution.py:345
  77.0 1.2 collective-permute-start.9
  78.7 9.1 %plan.1 = (s32[1]{0:T(128)}, s32[548]{0:T(1024)S(1)}, s32[2192]{0:T(1024)}, s32[2192]{0:T(1024)}, s32[1]{0:T(128)}) custom-call(s32[2]{0:T(128)S(1)} %pad_add_fusion.place_ref, bf16[128,80,128]{2,1,0:T(8,128)(2,1)} %copy-done), custom_call_target="tpu_custom_call" | custom-call | flops 7000000000 | bytes 1048576 | tf_op jit(solution)/shard_map/plan/pallas_call | solution.py:435
  87.9 8.9 %grid_cols.1 = bf16[4,128,128]{2,1,0:T(8,128)(2,1)} custom-call(s32[2]{0:T(128)S(1)} %pad_add_fusion.place_ref, s32[64]{0:T(128)S(1)} %copy-done.6, f32[1]{0:T(128)S(6)} %copy.24.shift_ref, bf16[128,80,128]{2,1,0:T(8,128)(2,1)S(1)} %copy-done.1, s32[3,64,128]{2,1,0:T(8,128)S(1)} %copy-done.2, f32[64,128]{1,0:T(8,128)S(1)} %copy-done.4, s32[64,128]{1,0:T(8,128)S(1)} %copy-done.5), custom_call_target="tpu_custom_call" | custom-call | flops 8800000000 | bytes 1048576 | tf_op jit(solution)/shard_map/grid_cols/pallas_call | solution.py:412
  96.8 1.3 collective-permute-start.14
  99.5 5.5 %all-to-all-start.1 = ((f32[128,1,128]{2,1,0:T(1,128)}), f32[128,1,128]{2,1,0:T(1,128)S(1)}, u32[]{:S(2)}, u32[]{:S(2)}) async-start(f32[128,1,128]{2,1,0:T(1,128)} %broadcast_in_dim.8), calls=%async_computation.1 | async-start | bytes 131072 | tf_op jit(solution)/shard_map/all_to_all | solution.py:332
  105.0 14.0 %all-to-all-done.1 = f32[128,1,128]{2,1,0:T(1,128)S(1)} async-done(((f32[128,1,128]{2,1,0:T(1,128)}), f32[128,1,128]{2,1,0:T(1,128)S(1)}, u32[]{:S(2)}, u32[]{:S(2)}) %all-to-all-start.1) | async-done | bytes 65568 | tf_op jit(solution)/shard_map/all_to_all | solution.py:332
  119.0 0.8 collective-permute-start.17
  120.5 2.2 %collective-permute-done.17 = bf16[40,128,128]{2,1,0:T(8,128)(2,1)S(1)} collective-permute-done((bf16[40,128,128]{2,1,0:T(8,128)(2,1)}, bf16[40,128,128]{2,1,0:T(8,128)(2,1)S(1)}, u32[]{:S(2)}, u32[]{:S(2)}) %collective-permute-start.17) | collective-permute-done | bytes 1310752 | tf_op jit(solution)/shard_map/ppermute | solution.py:361
  122.7 10.9 %conditional.1 = ((bf16[512,1024]{1,0:T(8,128)(2,1)}, bf16[512,1024]{1,0:T(8,128)(2,1)})) conditional(s32[]{:T(128)} %bitcast.5, (s32[2]{0:T(128)S(1)}, s32[4,8]{1,0:T(4,128)S(1)}, f32[1]{0:T(128)}, s32[1]{0:T(128)}, s32[548]{0:T(1024)S(1)}, /*index=5*/s32[2192]{0:T(1024)}, s32[2192]{0:T(1024)}, f32[128,128]{1,0:T(8,128)S(1)}, ...), branch_computations={%region_0.0_spmd, %region_1.0_spmd} | conditional | flops 12000000000 | bytes 125633464 | solution.py:504
  122.7 10.9 %product.1 = (bf16[512,1024]{1,0:T(8,128)(2,1)}, bf16[512,1024]{1,0:T(8,128)(2,1)}) custom-call(s32[2]{0:T(128)S(1)} %get-tuple-element.70.place_ref, s32[4,8]{1,0:T(4,128)S(1)} %get-tuple-element.71.pattern_ref, f32[1]{0:T(128)} %get-tuple-element.72.shift_ref, s32[1]{0:T(128)} %get-tuple-element.73.turns_ref, s32[548]{0:T(1024)S(1)} %get-tuple-element.74.out_ref, ...), custom_call_target="tpu_custom_call" | custom-call | flops 12000000000 | bytes 1048576 | tf_op jit(solution)/shard_map/cond/branch_0_fun/product/pallas_call | solution.py:470
  (48 shorter events, 3.9 us)
Async XLA Ops:
  7.2 1.7 %copy-start.10 = (s32[4,8]{1,0:T(4,128)S(1)}, s32[4,8]{1,0:T(4,128)}, u32[]{:S(2)}) copy-start(s32[4,8]{1,0:T(4,128)} %pattern_ref.3) | copy-start | bytes 388
  7.9 1.2 copy-start.7
  10.7 3.3 %collective-permute-start = (bf16[20,128,128]{2,1,0:T(8,128)(2,1)S(1)}, bf16[20,128,128]{2,1,0:T(8,128)(2,1)S(1)}, u32[]{:S(2)}, u32[]{:S(2)}) collective-permute-start(bf16[20,128,128]{2,1,0:T(8,128)(2,1)S(1)} %bitcast.32), channel_id=1, source_target_pairs={{0,8},{8,0},{16,24},{24,16},{32,40},{40,32},{48,56},{56,48},{64,72... | collective-permute-start | bytes 1966088 | tf_op jit(solution)/shard_map/ppermute | solution.py:361
  14.0 6.8 %copy-start.9 = (bf16[20,128,128]{2,1,0:T(8,128)(2,1)}, bf16[20,128,128]{2,1,0:T(8,128)(2,1)S(1)}, u32[]{:S(2)}) copy-start(bf16[20,128,128]{2,1,0:T(8,128)(2,1)S(1)} %collective-permute-done) | copy-start | bytes 1966084
  14.1 35.3 %collective-permute-start.3 = (bf16[40,128,128]{2,1,0:T(8,128)(2,1)S(1)}, bf16[40,128,128]{2,1,0:T(8,128)(2,1)}, u32[]{:S(2)}, u32[]{:S(2)}) collective-permute-start(bf16[40,128,128]{2,1,0:T(8,128)(2,1)S(1)} %pad_maximum_fusion), channel_id=1, source_target_pairs={{0,16},{1,17},{2,18},{3,19},{4,20},{5,21},{6,22},{7,23},{8,10},{9,... | collective-permute-start | bytes 3932168 | tf_op jit(solution)/shard_map/ppermute | solution.py:345
  15.8 33.6 %collective-permute-start.2 = (bf16[40,128,128]{2,1,0:T(8,128)(2,1)S(1)}, bf16[40,128,128]{2,1,0:T(8,128)(2,1)}, u32[]{:S(2)}, u32[]{:S(2)}) collective-permute-start(bf16[40,128,128]{2,1,0:T(8,128)(2,1)S(1)} %pad_maximum_fusion), channel_id=1, source_target_pairs={{0,48},{1,49},{2,50},{3,51},{4,52},{5,53},{6,54},{7,55},{8,14},{9,... | collective-permute-start | bytes 3932168 | tf_op jit(solution)/shard_map/ppermute | solution.py:345
  18.1 31.3 %collective-permute-start.1 = (bf16[40,128,128]{2,1,0:T(8,128)(2,1)S(1)}, bf16[40,128,128]{2,1,0:T(8,128)(2,1)S(1)}, u32[]{:S(2)}, u32[]{:S(2)}) collective-permute-start(bf16[40,128,128]{2,1,0:T(8,128)(2,1)S(1)} %pad_maximum_fusion), channel_id=1, source_target_pairs={{0,64},{1,65},{2,66},{3,67},{4,68},{5,69},{6,70},{7,71},{8,73},{9,... | collective-permute-start | bytes 3932168 | tf_op jit(solution)/shard_map/ppermute | solution.py:345
  49.4 8.8 %collective-permute-start.6 = (bf16[64,80,128]{2,1,0:T(8,128)(2,1)S(1)}, bf16[64,80,128]{2,1,0:T(8,128)(2,1)S(1)}, u32[]{:S(2)}, u32[]{:S(2)}) collective-permute-start(bf16[64,80,128]{2,1,0:T(8,128)(2,1)S(1)} %all_to_all.10), channel_id=1, source_target_pairs={{0,8},{8,0},{16,24},{24,16},{32,40},{40,32},{48,56},{56,48},{64,72... | collective-permute-start | bytes 3932168 | tf_op jit(solution)/shard_map/ppermute | solution.py:361
  55.3 18.7 %collective-permute-start.5 = (bf16[40,128,128]{2,1,0:T(8,128)(2,1)S(1)}, bf16[40,128,128]{2,1,0:T(8,128)(2,1)}, u32[]{:S(2)}, u32[]{:S(2)}) collective-permute-start(bf16[40,128,128]{2,1,0:T(8,128)(2,1)S(1)} %collective-permute-done.1), channel_id=1, source_target_pairs={{0,0},{1,1},{2,2},{3,3},{4,4},{5,5},{6,6},{7,7},{8,72},{9,73},{10,... | collective-permute-start | bytes 3932168 | tf_op jit(solution)/shard_map/ppermute | solution.py:345
  57.2 17.1 %collective-permute-start.4 = (bf16[40,128,128]{2,1,0:T(8,128)(2,1)}, bf16[40,128,128]{2,1,0:T(8,128)(2,1)}, u32[]{:S(2)}, u32[]{:S(2)}) collective-permute-start(bf16[40,128,128]{2,1,0:T(8,128)(2,1)} %collective-permute-done.2), channel_id=1, source_target_pairs={{0,48},{1,49},{2,50},{3,51},{4,52},{5,53},{6,54},{7,55},{8,14},{9,... | collective-permute-start | bytes 3932168 | tf_op jit(solution)/shard_map/ppermute | solution.py:345
  58.4 9.6 %copy-start = (bf16[128,80,128]{2,1,0:T(8,128)(2,1)}, bf16[128,80,128]{2,1,0:T(8,128)(2,1)S(1)}, u32[]{:S(2)}) copy-start(bf16[128,80,128]{2,1,0:T(8,128)(2,1)S(1)} %constant_dynamic-update-slice_fusion.bricks_ref) | copy-start | bytes 7864324
  74.3 13.5 %copy-start.1 = (bf16[128,80,128]{2,1,0:T(8,128)(2,1)S(1)}, bf16[128,80,128]{2,1,0:T(8,128)(2,1)}, u32[]{:S(2)}) copy-start(bf16[128,80,128]{2,1,0:T(8,128)(2,1)} %copy-done) | copy-start | bytes 7864324
  74.3 23.8 %collective-permute-start.8 = (bf16[40,128,128]{2,1,0:T(8,128)(2,1)}, bf16[40,128,128]{2,1,0:T(8,128)(2,1)}, u32[]{:S(2)}, u32[]{:S(2)}) collective-permute-start(bf16[40,128,128]{2,1,0:T(8,128)(2,1)} %collective-permute-done.5), channel_id=1, source_target_pairs={{0,16},{1,17},{2,18},{3,19},{4,20},{5,21},{6,22},{7,23},{8,10},{9,... | collective-permute-start | bytes 3932168 | tf_op jit(solution)/shard_map/ppermute | solution.py:345
  74.3 23.8 %collective-permute-start.7 = (bf16[40,128,128]{2,1,0:T(8,128)(2,1)}, bf16[40,128,128]{2,1,0:T(8,128)(2,1)}, u32[]{:S(2)}, u32[]{:S(2)}) collective-permute-start(bf16[40,128,128]{2,1,0:T(8,128)(2,1)} %collective-permute-done.5), channel_id=1, source_target_pairs={{0,48},{1,49},{2,50},{3,51},{4,52},{5,53},{6,54},{7,55},{8,14},{9,... | collective-permute-start | bytes 3932168 | tf_op jit(solution)/shard_map/ppermute | solution.py:345
  77.0 19.8 %collective-permute-start.9 = (bf16[40,128,128]{2,1,0:T(8,128)(2,1)}, bf16[40,128,128]{2,1,0:T(8,128)(2,1)}, u32[]{:S(2)}, u32[]{:S(2)}) collective-permute-start(bf16[40,128,128]{2,1,0:T(8,128)(2,1)} %collective-permute-done.2), channel_id=1, source_target_pairs={{0,8},{8,0},{16,24},{24,16},{32,40},{40,32},{48,56},{56,48},{64,72... | collective-permute-start | bytes 3932168 | tf_op jit(solution)/shard_map/ppermute | solution.py:361
  78.2 19.9 %collective-permute-start.10 = (bf16[40,128,128]{2,1,0:T(8,128)(2,1)}, bf16[40,128,128]{2,1,0:T(8,128)(2,1)}, u32[]{:S(2)}, u32[]{:S(2)}) collective-permute-start(bf16[40,128,128]{2,1,0:T(8,128)(2,1)} %collective-permute-done.4), channel_id=1, source_target_pairs={{0,8},{8,0},{16,24},{24,16},{32,40},{40,32},{48,56},{56,48},{64,72... | collective-permute-start | bytes 3932168 | tf_op jit(solution)/shard_map/ppermute | solution.py:361
  78.2 19.9 %collective-permute-start.11 = (bf16[40,128,128]{2,1,0:T(8,128)(2,1)}, bf16[40,128,128]{2,1,0:T(8,128)(2,1)}, u32[]{:S(2)}, u32[]{:S(2)}) collective-permute-start(bf16[40,128,128]{2,1,0:T(8,128)(2,1)} %collective-permute-done.3), channel_id=1, source_target_pairs={{0,8},{8,0},{16,24},{24,16},{32,40},{40,32},{48,56},{56,48},{64,72... | collective-permute-start | bytes 3932168 | tf_op jit(solution)/shard_map/ppermute | solution.py:361
  96.8 8.2 %collective-permute-start.14 = (bf16[40,128,128]{2,1,0:T(8,128)(2,1)}, bf16[40,128,128]{2,1,0:T(8,128)(2,1)S(1)}, u32[]{:S(2)}, u32[]{:S(2)}) collective-permute-start(bf16[40,128,128]{2,1,0:T(8,128)(2,1)} %collective-permute-done.5), channel_id=1, source_target_pairs={{0,8},{8,0},{16,24},{24,16},{32,40},{40,32},{48,56},{56,48},{64,72... | collective-permute-start | bytes 3932168 | tf_op jit(solution)/shard_map/ppermute | solution.py:361
  98.1 20.8 %collective-permute-start.15 = (bf16[40,128,128]{2,1,0:T(8,128)(2,1)}, bf16[40,128,128]{2,1,0:T(8,128)(2,1)S(1)}, u32[]{:S(2)}, u32[]{:S(2)}) collective-permute-start(bf16[40,128,128]{2,1,0:T(8,128)(2,1)} %collective-permute-done.7), channel_id=1, source_target_pairs={{0,8},{8,0},{16,24},{24,16},{32,40},{40,32},{48,56},{56,48},{64,72... | collective-permute-start | bytes 3932168 | tf_op jit(solution)/shard_map/ppermute | solution.py:361
  98.2 20.7 %collective-permute-start.16 = (bf16[40,128,128]{2,1,0:T(8,128)(2,1)}, bf16[40,128,128]{2,1,0:T(8,128)(2,1)}, u32[]{:S(2)}, u32[]{:S(2)}) collective-permute-start(bf16[40,128,128]{2,1,0:T(8,128)(2,1)} %collective-permute-done.8), channel_id=1, source_target_pairs={{0,8},{8,0},{16,24},{24,16},{32,40},{40,32},{48,56},{56,48},{64,72... | collective-permute-start | bytes 3932168 | tf_op jit(solution)/shard_map/ppermute | solution.py:361
  98.7 20.2 %collective-permute-start.12 = (bf16[40,128,128]{2,1,0:T(8,128)(2,1)}, bf16[40,128,128]{2,1,0:T(8,128)(2,1)}, u32[]{:S(2)}, u32[]{:S(2)}) collective-permute-start(bf16[40,128,128]{2,1,0:T(8,128)(2,1)} %collective-permute-done.8), channel_id=1, source_target_pairs={{0,16},{1,17},{2,18},{3,19},{4,20},{5,21},{6,22},{7,23},{8,10},{9,... | collective-permute-start | bytes 3932168 | tf_op jit(solution)/shard_map/ppermute | solution.py:345
  98.7 20.2 %collective-permute-start.13 = (bf16[4,128,128]{2,1,0:T(8,128)(2,1)}, bf16[4,128,128]{2,1,0:T(8,128)(2,1)S(1)}, u32[]{:S(2)}, u32[]{:S(2)}) collective-permute-start(bf16[4,128,128]{2,1,0:T(8,128)(2,1)} %grid_cols.1), channel_id=1, source_target_pairs={{0,8},{8,0},{16,24},{24,16},{32,40},{40,32},{48,56},{56,48},{64,72... | collective-permute-start | bytes 393224 | tf_op jit(solution)/shard_map/ppermute | solution.py:361
  99.5 19.5 %all-to-all-start.1 = ((f32[128,1,128]{2,1,0:T(1,128)}), f32[128,1,128]{2,1,0:T(1,128)S(1)}, u32[]{:S(2)}, u32[]{:S(2)}) async-start(f32[128,1,128]{2,1,0:T(1,128)} %broadcast_in_dim.8), calls=%async_computation.1 | async-start | bytes 131072 | tf_op jit(solution)/shard_map/all_to_all | solution.py:332
  119.0 3.7 %collective-permute-start.17 = (bf16[40,128,128]{2,1,0:T(8,128)(2,1)}, bf16[40,128,128]{2,1,0:T(8,128)(2,1)S(1)}, u32[]{:S(2)}, u32[]{:S(2)}) collective-permute-start(bf16[40,128,128]{2,1,0:T(8,128)(2,1)} %collective-permute-done.12), channel_id=1, source_target_pairs={{0,8},{8,0},{16,24},{24,16},{32,40},{40,32},{48,56},{56,48},{64,72... | collective-permute-start | bytes 3932168 | tf_op jit(solution)/shard_map/ppermute | solution.py:361
  (5 other events, 4.3 us)

commit v3 on v2

--- a/solution.py
+++ b/solution.py
@@ -18,8 +18,8 @@
 BF16 = jnp.bfloat16
 
 
-def params(limit=48 * 1024 * 1024):
-    return pltpu.CompilerParams(vmem_limit_bytes=limit)
+def params(mebibytes):
+    return pltpu.CompilerParams(vmem_limit_bytes=mebibytes * 2**20)
 
 
 def pack_kernel(pattern_ref, place_ref, core_ref, payload_ref, sum_ref):
@@ -74,54 +74,54 @@
     return jnp.broadcast_to(row_values, (BS, BS)).T
 
 
-def collocate(cluster, brick_ref, centres_ref, exponents_ref, extents_ref, along_ref, phi_ref, weighted_ref):
-    decay = column(exponents_ref[pl.ds(cluster, 1), :])
-    reach = column(extents_ref[pl.ds(cluster, 1), :].astype(F32))
-    cut = jnp.exp(-decay * (reach * reach + 0.5))
-    at_x = column(centres_ref[0, pl.ds(cluster, 1), :].astype(F32))
-    at_y = column(centres_ref[1, pl.ds(cluster, 1), :].astype(F32))
-    at_z = column(centres_ref[2, pl.ds(cluster, 1), :].astype(F32))
-    off_z = lax.broadcasted_iota(jnp.int32, (BS, BS), 1).astype(F32) - at_z
-    along_z = jnp.exp(-decay * (off_z * off_z))
-    for y in range(8):
-        off_y = y - at_y
-        along_ref[y] = jnp.exp(-decay * (off_y * off_y))
-
-    total = jnp.zeros((BS, BS), F32)
-    for x in range(8):
-        off_x = x - at_x
-        along_xz = along_z * jnp.exp(-decay * (off_x * off_x))
+def values_kernel(place_ref, centres_ref, exponents_ref, extents_ref, phi_ref, along_ref):
+    row, col = place_ref[0], place_ref[1]
+
+    def one(k, carry):
+        cluster = jnp.where(k < 4, row * 4 + k, col * 8 + row % 2 * 4 + k - 4)
+        decay = column(exponents_ref[pl.ds(cluster, 1), :])
+        reach = column(extents_ref[pl.ds(cluster, 1), :].astype(F32))
+        cut = jnp.exp(-decay * (reach * reach + 0.5))
+        at_x = column(centres_ref[0, pl.ds(cluster, 1), :].astype(F32))
+        at_y = column(centres_ref[1, pl.ds(cluster, 1), :].astype(F32))
+        at_z = column(centres_ref[2, pl.ds(cluster, 1), :].astype(F32))
+        off_z = lax.broadcasted_iota(jnp.int32, (BS, BS), 1).astype(F32) - at_z
+        along_z = jnp.exp(-decay * (off_z * off_z))
         for y in range(8):
-            phi = along_xz * along_ref[y]
-            basis = jnp.where(phi >= cut, phi, 0.0).astype(BF16)
-            phi_ref[x, :, y * BS : (y + 1) * BS] = basis
-            weighted_ref[x, :, y * BS : (y + 1) * BS] = basis * brick_ref[x * 8 + y : x * 8 + y + 1, :]
-        total += lax.dot_general(
-            weighted_ref[x], phi_ref[x], (((1,), (1,)), ((), ())), preferred_element_type=F32
-        )
-    return (total * VOLUME).astype(BF16)
-
-
-def grid_kernel(
-    count, with_sum, place_ref, home_ref, shift_ref, bricks_ref, centres_ref, exponents_ref, extents_ref, *rest
-):
+            off_y = y - at_y
+            along_ref[y] = jnp.exp(-decay * (off_y * off_y))
+        for x in range(8):
+            off_x = x - at_x
+            along_xz = along_z * jnp.exp(-decay * (off_x * off_x))
+            for y in range(8):
+                phi = along_xz * along_ref[y]
+                phi_ref[k, x, :, y * BS : (y + 1) * BS] = jnp.where(phi >= cut, phi, 0.0).astype(BF16)
+        return carry
+
+    lax.fori_loop(0, 8, one, 0)
+
+
+def grid_kernel(with_sum, place_ref, home_ref, shift_ref, bricks_ref, phi_ref, *rest):
     if with_sum:
-        core_ref, sum_ref, blocks_ref, total_ref, along_ref, phi_ref, weighted_ref = rest
+        core_ref, sum_ref, blocks_ref, total_ref = rest
     else:
-        blocks_ref, along_ref, phi_ref, weighted_ref = rest
+        (blocks_ref,) = rest
     row, col = place_ref[0], place_ref[1]
     first = row * 4 if with_sum else col * 8 + row % 2 * 4
+    place = 0 if with_sum else 4
 
     def one(k, carry):
-        cluster = first + k
-        home = home_ref[cluster]
+        home = home_ref[first + k]
         index = (home // 8 ^ row) % 2 * 64 + home // 16 * 8 + home % 8
-        blocks_ref[k] = collocate(
-            cluster, bricks_ref.at[index], centres_ref, exponents_ref, extents_ref, along_ref, phi_ref, weighted_ref
-        )
+        total = jnp.zeros((BS, BS), F32)
+        for x in range(8):
+            values = jnp.concatenate([bricks_ref[index, x * 8 + y : x * 8 + y + 1, :] for y in range(8)], axis=1)
+            phi = phi_ref[place + k, x]
+            total += lax.dot_general(phi * values, phi, (((1,), (1,)), ((), ())), preferred_element_type=F32)
+        blocks_ref[k] = (total * VOLUME).astype(BF16)
         return carry
 
-    lax.fori_loop(0, count, one, 0)
+    lax.fori_loop(0, 4, one, 0)
     if with_sum:
         total_ref[...] = jnp.sum(sum_ref[...], axis=0, keepdims=True)
 
@@ -375,7 +375,7 @@
         in_specs=[SM, VM],
         out_specs=VM,
         out_shape=jax.ShapeDtypeStruct((80, BS), BF16),
-        compiler_params=params(),
+        compiler_params=params(4),
         cost_estimate=lasting(1),
         name="brick",
     )(pattern, potential.reshape(64, BS))
@@ -388,7 +388,7 @@
         in_specs=[SM, SM, VM],
         out_specs=[VM, VM],
         out_shape=[jax.ShapeDtypeStruct((CAP * BS, BS), BF16), jax.ShapeDtypeStruct((8, BS), F32)],
-        compiler_params=params(),
+        compiler_params=params(4),
         cost_estimate=lasting(2),
         name="pack",
     )(pattern, place, core_after_brick)
@@ -398,40 +398,53 @@
     pair = jnp.concatenate([payload, crossed])
     step = across_y(pair)
     after, before = ring(pair, 1), ring(pair, -1)
-    half, step, after, before = lax.optimization_barrier((half, step, after, before))
+    phi = pl.pallas_call(
+        values_kernel,
+        in_specs=[SM, VM, VM, VM],
+        out_specs=VM,
+        out_shape=jax.ShapeDtypeStruct((8, 8, BS, 8 * BS), BF16),
+        scratch_shapes=[pltpu.VMEM((8, BS, BS), F32)],
+        compiler_params=params(4),
+        cost_estimate=lasting(10),
+        name="values",
+    )(place, centres, exponents, extents)
+    half, phi, step, after, before = lax.optimization_barrier((half, phi, step, after, before))
 
     far = ring(after, 1)
     other = across_y_again(step)
     bricks = jnp.concatenate([half, to_core(half)])
 
-    def grid_blocks(count, with_sum, *more):
+    def grid_blocks(with_sum, *more):
         extra = [VM, VM] if with_sum else []
-        out_shape = [jax.ShapeDtypeStruct((count, BS, BS), BF16)]
+        out_shape = [jax.ShapeDtypeStruct((4, BS, BS), BF16)]
         if with_sum:
             out_shape.append(jax.ShapeDtypeStruct((1, BS), F32))
         return pl.pallas_call(
-            functools.partial(grid_kernel, count, with_sum),
-            in_specs=[SM, SM, SM, VM, VM, VM, VM] + extra,
+            functools.partial(grid_kernel, with_sum),
+            in_specs=[SM, SM, SM, VM, VM] + extra,
             out_specs=[VM] * len(out_shape),
             out_shape=out_shape,
-            scratch_shapes=[
-                pltpu.VMEM((8, BS, BS), F32),
-                pltpu.VMEM((8, BS, 8 * BS), BF16),
-                pltpu.VMEM((8, BS, 8 * BS), BF16),
-            ],
-            compiler_params=params(),
-            cost_estimate=lasting(2.2 * count),
+            compiler_params=params(8),
+            cost_estimate=lasting(5),
             name="grid_rows" if with_sum else "grid_cols",
-        )(place, home, shift, bricks, centres, exponents, extents, *more)
-
-    row_grid, total = grid_blocks(4, True, core_matrix, squares)
+        )(place, home, shift, bricks, phi, *more)
+
+    row_grid, total = grid_blocks(True, core_matrix, squares)
     after, before, far, other, row_grid, total, bricks = lax.optimization_barrier(
         (after, before, far, other, row_grid, total, bricks)
     )
 
     other_after, other_before = ring(other, 1), ring(other, -1)
     crossings = [to_core(after), to_core(far), to_core(before)]
-    (col_grid,) = grid_blocks(4, False)
+    (col_grid,) = grid_blocks(False)
+    other_after, other_before, col_grid, total, bricks, *crossings = lax.optimization_barrier(
+        (other_after, other_before, col_grid, total, bricks, *crossings)
+    )
+
+    other_far = ring(other_before, -1)
+    crossings += [to_core(other), to_core(other_after), to_core(other_before)]
+    col_grid_crossed = to_core(col_grid)
+    frob = to_all(total, ("row", "col"), 128).reshape(128, BS)
     *listed, most = pl.pallas_call(
         plan_kernel,
         in_specs=[SM, VM],
@@ -446,21 +459,14 @@
         scratch_shapes=[pltpu.VMEM((40, BS), jnp.int32), pltpu.SMEM((40, BS), jnp.int32)]
         + [pltpu.SMEM((72,), jnp.int32)] * 3
         + [pltpu.SemaphoreType.DMA],
-        cost_estimate=lasting(7),
+        compiler_params=params(4),
+        cost_estimate=lasting(9),
         name="plan",
     )(place, bricks)
-    other_after, other_before, col_grid, total, *rest = lax.optimization_barrier(
-        (other_after, other_before, col_grid, total, *crossings, *listed)
+    other_far, col_grid_crossed, frob, *rest = lax.optimization_barrier(
+        (other_far, col_grid_crossed, frob, *crossings, *listed)
     )
-    crossings, listed = rest[:3], rest[3:]
-
-    other_far = ring(other_before, -1)
-    crossings += [to_core(other), to_core(other_after), to_core(other_before)]
-    col_grid_crossed = to_core(col_grid)
-    frob = to_all(total, ("row", "col"), 128).reshape(128, BS)
-    other_far, col_grid_crossed, frob, *crossings = lax.optimization_barrier(
-        (other_far, col_grid_crossed, frob, *crossings)
-    )
+    crossings, listed = rest[:6], rest[6:]
 
     crossings.insert(5, to_core(other_far))
     own_role = [after, far, before, other, other_after, other_far, other_before]
@@ -479,7 +485,7 @@
                 pltpu.VMEM((8, BS, BS), BF16),
                 pltpu.SemaphoreType.DMA((17,)),
             ],
-            compiler_params=params(),
+            compiler_params=params(24),
             cost_estimate=lasting(12),
             name="product",
         )(place, pattern, shift, *listed, frob, core_matrix, row_grid, col_grid, col_grid_crossed, payload, crossed, *own_role, *crossings)

time: 141 us -> 151 us (1.071)
  blocking collectives: 28.4 us -> 0 us
  starting transfers between devices: 28.9 us -> 46.2 us
  local copies, waits for them, and re-layouts: 2.71 us -> 17.4 us
  waiting for transfers between devices: 24.3 us -> 32.7 us
  Pallas kernels: 40.4 us -> 37.3 us
    all_to_all x1 -> x0, blocking collectives: 28.4 us -> none  [to_all(): return lax.all_to_all(copies, axis, 0, 0, axis_index_groups=groups)]
    unnamed x21 -> x35, local copies, waits for them, and re-layouts: 1.71 us -> 15.3 us
    ppermute x8, waiting for transfers between devices: 6.41 us -> 15.7 us  [move(): lax.ppermute(value, ('row', 'col'), [(k, device_of(*where(*place_of(k))))...]
    ppermute x10, starting transfers between devices: 11.9 us -> 21.2 us  [to_core(): return lax.ppermute(value, 'row', [(k, k ^ 1) for k in range(16)])]
    all_to_all x1 -> x2, starting transfers between devices: 5.48 us -> 13.2 us  [to_all(): return lax.all_to_all(copies, axis, 0, 0, axis_index_groups=groups)]
    pallas_call x2 -> x3, Pallas kernels: 17.9 us -> 14.9 us  [the longest x2 7.49 us: grid_blocks(): pl.pallas_call(functools.partial(grid_kernel, with_sum), in_specs=[SM, SM...]
    all_to_all x1 -> x2, waiting for transfers between devices: 14 us -> 13.1 us  [to_all(): return lax.all_to_all(copies, axis, 0, 0, axis_index_groups=groups)]
  transfers between devices with their start and end apart: 19 -> 20, of which waited for: 5 -> 7; matrix products, arithmetic and copies ran while one was open for 1% -> 2% of each run, Pallas kernels for 19% -> 16%
where the time goes in v3:
time: 151 us; the launch traced here: 149 us
  starting transfers between devices  46.2 us (31%)
  Pallas kernels  37.3 us (25%)
  waiting for transfers between devices  32.7 us (22%)
  local copies, waits for them, and re-layouts  17.4 us (12%)
  between operations  15.6 us (10%)
    ppermute x10, starting transfers between devices, to_core(): return lax.ppermute(value, 'row', [(k, k ^ 1) for k in range(16)])  21.2 us
    ppermute x8, waiting for transfers between devices, move(): lax.ppermute(value, ('row', 'col'), [(k, device_of(*where(*place_of(k))))...  15.7 us
    unnamed x35, local copies, waits for them, and re-layouts  15.3 us
    all_to_all x2, starting transfers between devices, to_all(): return lax.all_to_all(copies, axis, 0, 0, axis_index_groups=groups)  13.2 us
    all_to_all x2, waiting for transfers between devices, to_all(): return lax.all_to_all(copies, axis, 0, 0, axis_index_groups=groups)  13.1 us
    ppermute x8, starting transfers between devices, move(): lax.ppermute(value, ('row', 'col'), [(k, device_of(*where(*place_of(k))))...  11.7 us
    pallas_call x1, Pallas kernels, sparse(): pl.pallas_call(product_kernel, in_specs=[SM] * 7 + [VM] * 5 + [ANY] * 16,...  11.6 us
    pallas_call x1, Pallas kernels, body(): pl.pallas_call(plan_kernel, in_specs=[SM, VM], out_specs=[SM] * 5, out_sh...  8.48 us
  transfers between devices with their start and end apart: 20, of which 7 were waited for; matrix products, arithmetic and copies ran while one was open for 2% of the time, Pallas kernels for 16%

profile of v3, /device:TPU:1, one launch (start us, length us, event | category | flops | bytes accessed | tf_op | source)
XLA Modules:
  0.0 149.4 jit_solution(14624717139490864655)
XLA Ops:
  9.2 1.5 %pack.1 = (bf16[2560,128]{1,0:T(8,128)(2,1)S(1)}, f32[8,128]{1,0:T(8,128)S(1)}) custom-call(s32[4,8]{1,0:T(4,128)S(1)} %copy-done.11, s32[2]{0:T(128)S(1)} %pad_add_fusion.place_ref, bf16[512,1024]{1,0:T(8,128)(2,1)S(1)} %copy-done.7), custom_call_target="tpu_custom_call" | custom-call | flops 2000000000 | bytes 1048576 | tf_op jit(solution)/shard_map/pack/pallas_call | solution.py:386
  12.2 1.7 %collective-permute-done = bf16[20,128,128]{2,1,0:T(8,128)(2,1)S(1)} collective-permute-done((bf16[20,128,128]{2,1,0:T(8,128)(2,1)S(1)}, bf16[20,128,128]{2,1,0:T(8,128)(2,1)S(1)}, u32[]{:S(2)}, u32[]{:S(2)}) %collective-permute-start) | collective-permute-done | bytes 655392 | tf_op jit(solution)/shard_map/ppermute | solution.py:361
  14.9 1.8 %collective-permute-start.3 = (bf16[40,128,128]{2,1,0:T(8,128)(2,1)S(1)}, bf16[40,128,128]{2,1,0:T(8,128)(2,1)S(1)}, u32[]{:S(2)}, u32[]{:S(2)}) collective-permute-start(bf16[40,128,128]{2,1,0:T(8,128)(2,1)S(1)} %pad_maximum_fusion), channel_id=1, source_target_pairs={{0,16},{1,17},{2,18},{3,19},{4,20},{5,21},{6,22},{7,23},{8,10},{9,... | collective-permute-start | bytes 3932168 | tf_op jit(solution)/shard_map/ppermute | solution.py:345
  16.8 2.2 %collective-permute-start.2 = (bf16[40,128,128]{2,1,0:T(8,128)(2,1)S(1)}, bf16[40,128,128]{2,1,0:T(8,128)(2,1)}, u32[]{:S(2)}, u32[]{:S(2)}) collective-permute-start(bf16[40,128,128]{2,1,0:T(8,128)(2,1)S(1)} %pad_maximum_fusion), channel_id=1, source_target_pairs={{0,48},{1,49},{2,50},{3,51},{4,52},{5,53},{6,54},{7,55},{8,14},{9,... | collective-permute-start | bytes 3932168 | tf_op jit(solution)/shard_map/ppermute | solution.py:345
  18.9 2.7 %collective-permute-start.1 = (bf16[40,128,128]{2,1,0:T(8,128)(2,1)S(1)}, bf16[40,128,128]{2,1,0:T(8,128)(2,1)}, u32[]{:S(2)}, u32[]{:S(2)}) collective-permute-start(bf16[40,128,128]{2,1,0:T(8,128)(2,1)S(1)} %pad_maximum_fusion), channel_id=1, source_target_pairs={{0,64},{1,65},{2,66},{3,67},{4,68},{5,69},{6,70},{7,71},{8,73},{9,... | collective-permute-start | bytes 3932168 | tf_op jit(solution)/shard_map/ppermute | solution.py:345
  22.9 6.4 %all-to-all-start = ((bf16[64,80,128]{2,1,0:T(8,128)(2,1)}), bf16[64,80,128]{2,1,0:T(8,128)(2,1)}, u32[]{:S(2)}, u32[]{:S(2)}) async-start(bf16[64,80,128]{2,1,0:T(8,128)(2,1)} %broadcast_in_dim.6), calls=%async_computation | async-start | bytes 2621440 | tf_op jit(solution)/shard_map/all_to_all | solution.py:332
  29.4 7.4 %values.1.phi_ref = bf16[8,8,128,1024]{3,2,1,0:T(8,128)(2,1)S(1)} custom-call(s32[2]{0:T(128)S(1)} %pad_add_fusion.place_ref, s32[3,64,128]{2,1,0:T(8,128)S(1)} %copy-done.3, f32[64,128]{1,0:T(8,128)S(1)} %copy-done.5, s32[64,128]{1,0:T(8,128)S(1)} %copy-done.6), custom_call_target="tpu_custom_call" | custom-call | flops 10000000000 | bytes 1048576 | tf_op jit(solution)/shard_map/values/pallas_call | solution.py:401
  36.7 5.7 %copy-done = bf16[8,8,128,1024]{3,2,1,0:T(8,128)(2,1)} copy-done((bf16[8,8,128,1024]{3,2,1,0:T(8,128)(2,1)}, bf16[8,8,128,1024]{3,2,1,0:T(8,128)(2,1)S(1)}, u32[]{:S(2)}) %copy-start) | copy-done | bytes 16777240
  42.5 8.7 %all-to-all-done = bf16[64,80,128]{2,1,0:T(8,128)(2,1)} async-done(((bf16[64,80,128]{2,1,0:T(8,128)(2,1)}), bf16[64,80,128]{2,1,0:T(8,128)(2,1)}, u32[]{:S(2)}, u32[]{:S(2)}) %all-to-all-start) | async-done | bytes 1310752 | tf_op jit(solution)/shard_map/all_to_all | solution.py:332
  51.2 5.1 %collective-permute-start.6 = (bf16[64,80,128]{2,1,0:T(8,128)(2,1)}, bf16[64,80,128]{2,1,0:T(8,128)(2,1)S(1)}, u32[]{:S(2)}, u32[]{:S(2)}) collective-permute-start(bf16[64,80,128]{2,1,0:T(8,128)(2,1)} %all-to-all-done), channel_id=1, source_target_pairs={{0,8},{8,0},{16,24},{24,16},{32,40},{40,32},{48,56},{56,48},{64,72... | collective-permute-start | bytes 3932168 | tf_op jit(solution)/shard_map/ppermute | solution.py:361
  56.3 1.9 %collective-permute-start.5 = (bf16[40,128,128]{2,1,0:T(8,128)(2,1)}, bf16[40,128,128]{2,1,0:T(8,128)(2,1)}, u32[]{:S(2)}, u32[]{:S(2)}) collective-permute-start(bf16[40,128,128]{2,1,0:T(8,128)(2,1)} %collective-permute-done.1), channel_id=1, source_target_pairs={{0,0},{1,1},{2,2},{3,3},{4,4},{5,5},{6,6},{7,7},{8,72},{9,73},{10,... | collective-permute-start | bytes 3932168 | tf_op jit(solution)/shard_map/ppermute | solution.py:345
  60.8 5.8 %copy-done.1 = bf16[8,8,128,1024]{3,2,1,0:T(8,128)(2,1)S(1)} copy-done((bf16[8,8,128,1024]{3,2,1,0:T(8,128)(2,1)S(1)}, bf16[8,8,128,1024]{3,2,1,0:T(8,128)(2,1)}, u32[]{:S(2)}) %copy-start.1) | copy-done | bytes 16777240
  66.6 4.1 %grid_rows.1 = (bf16[4,128,128]{2,1,0:T(8,128)(2,1)}, f32[1,128]{1,0:T(1,128)S(1)}) custom-call(s32[2]{0:T(128)S(1)} %pad_add_fusion.place_ref, s32[64]{0:T(128)S(1)} %copy-done.2, f32[1]{0:T(128)S(6)} %copy.24.shift_ref, bf16[128,80,128]{2,1,0:T(8,128)(2,1)S(1)} %constant_dynamic-update-slice_fusion.bricks_ref, bf16[8,8,128,1024]{3,2,1,0:T(8,128)(2,1)S(1)} %copy-done.1, ...), custom_call_target="tpu_custom_call" | custom-call | flops 5000000000 | bytes 1048576 | tf_op jit(solution)/shard_map/grid_rows/pallas_call | solution.py:422
  70.7 4.4 %collective-permute-done.5 = bf16[40,128,128]{2,1,0:T(8,128)(2,1)} collective-permute-done((bf16[40,128,128]{2,1,0:T(8,128)(2,1)}, bf16[40,128,128]{2,1,0:T(8,128)(2,1)}, u32[]{:S(2)}, u32[]{:S(2)}) %collective-permute-start.5) | collective-permute-done | bytes 1310752 | tf_op jit(solution)/shard_map/ppermute | solution.py:345
  75.2 10.2 %collective-permute-start.9 = (bf16[40,128,128]{2,1,0:T(8,128)(2,1)}, bf16[40,128,128]{2,1,0:T(8,128)(2,1)S(1)}, u32[]{:S(2)}, u32[]{:S(2)}) collective-permute-start(bf16[40,128,128]{2,1,0:T(8,128)(2,1)} %collective-permute-done.2), channel_id=1, source_target_pairs={{0,8},{8,0},{16,24},{24,16},{32,40},{40,32},{48,56},{56,48},{64,72... | collective-permute-start | bytes 3932168 | tf_op jit(solution)/shard_map/ppermute | solution.py:361
  85.9 2.7 %collective-permute-start.7 = (bf16[40,128,128]{2,1,0:T(8,128)(2,1)}, bf16[40,128,128]{2,1,0:T(8,128)(2,1)}, u32[]{:S(2)}, u32[]{:S(2)}) collective-permute-start(bf16[40,128,128]{2,1,0:T(8,128)(2,1)} %collective-permute-done.5), channel_id=1, source_target_pairs={{0,48},{1,49},{2,50},{3,51},{4,52},{5,53},{6,54},{7,55},{8,14},{9,... | collective-permute-start | bytes 3932168 | tf_op jit(solution)/shard_map/ppermute | solution.py:345
  88.6 3.4 %grid_cols.1 = bf16[4,128,128]{2,1,0:T(8,128)(2,1)S(1)} custom-call(s32[2]{0:T(128)S(1)} %pad_add_fusion.place_ref, s32[64]{0:T(128)S(1)} %copy-done.2, f32[1]{0:T(128)S(6)} %copy.24.shift_ref, bf16[128,80,128]{2,1,0:T(8,128)(2,1)S(1)} %constant_dynamic-update-slice_fusion.bricks_ref, bf16[8,8,128,1024]{3,2,1,0:T(8,128)(2,1)S(1)} %copy-done.1), custom_call_target="tpu_custom_call" | custom-call | flops 5000000000 | bytes 1048576 | tf_op jit(solution)/shard_map/grid_cols/pallas_call | solution.py:422
  93.0 11.2 %collective-permute-done.8 = bf16[40,128,128]{2,1,0:T(8,128)(2,1)} collective-permute-done((bf16[40,128,128]{2,1,0:T(8,128)(2,1)}, bf16[40,128,128]{2,1,0:T(8,128)(2,1)}, u32[]{:S(2)}, u32[]{:S(2)}) %collective-permute-start.8) | collective-permute-done | bytes 1310752 | tf_op jit(solution)/shard_map/ppermute | solution.py:345
  106.1 6.8 %all-to-all-start.1 = ((f32[128,1,128]{2,1,0:T(1,128)}), f32[128,1,128]{2,1,0:T(1,128)S(1)}, u32[]{:S(2)}, u32[]{:S(2)}) async-start(f32[128,1,128]{2,1,0:T(1,128)} %broadcast_in_dim.8), calls=%async_computation.1 | async-start | bytes 131072 | tf_op jit(solution)/shard_map/all_to_all | solution.py:332
  114.1 8.5 %plan.1 = (s32[1]{0:T(128)}, s32[548]{0:T(1024)S(1)}, s32[2192]{0:T(1024)S(1)}, s32[2192]{0:T(1024)S(1)}, s32[1]{0:T(128)}) custom-call(s32[2]{0:T(128)S(1)} %pad_add_fusion.place_ref, bf16[128,80,128]{2,1,0:T(8,128)(2,1)S(1)} %constant_dynamic-update-slice_fusion.bricks_ref), custom_call_target="tpu_custom_call" | custom-call | flops 8999999488 | bytes 1048576 | tf_op jit(solution)/shard_map/plan/pallas_call | solution.py:448
  122.6 4.4 %all-to-all-done.1 = f32[128,1,128]{2,1,0:T(1,128)S(1)} async-done(((f32[128,1,128]{2,1,0:T(1,128)}), f32[128,1,128]{2,1,0:T(1,128)S(1)}, u32[]{:S(2)}, u32[]{:S(2)}) %all-to-all-start.1) | async-done | bytes 65568 | tf_op jit(solution)/shard_map/all_to_all | solution.py:332
  128.7 2.2 %collective-permute-done.17 = bf16[40,128,128]{2,1,0:T(8,128)(2,1)S(1)} collective-permute-done((bf16[40,128,128]{2,1,0:T(8,128)(2,1)}, bf16[40,128,128]{2,1,0:T(8,128)(2,1)S(1)}, u32[]{:S(2)}, u32[]{:S(2)}) %collective-permute-start.17) | collective-permute-done | bytes 1310752 | tf_op jit(solution)/shard_map/ppermute | solution.py:361
  131.0 11.6 %conditional.1 = ((bf16[512,1024]{1,0:T(8,128)(2,1)}, bf16[512,1024]{1,0:T(8,128)(2,1)})) conditional(s32[]{:T(128)} %bitcast.5, (s32[2]{0:T(128)S(1)}, s32[4,8]{1,0:T(4,128)S(1)}, f32[1]{0:T(128)}, s32[1]{0:T(128)}, s32[548]{0:T(1024)S(1)}, /*index=5*/s32[2192]{0:T(1024)S(1)}, s32[2192]{0:T(1024)S(1)}, f32[128,128]{1,0:T(8,128)S(1)}, ...), branch_computations={%region_0.0_spmd, %region_1.0_spmd} | conditional | flops 12000000000 | bytes 125633464 | solution.py:510
  131.0 11.6 %product.1 = (bf16[512,1024]{1,0:T(8,128)(2,1)}, bf16[512,1024]{1,0:T(8,128)(2,1)}) custom-call(s32[2]{0:T(128)S(1)} %get-tuple-element.70.place_ref, s32[4,8]{1,0:T(4,128)S(1)} %get-tuple-element.71.pattern_ref, f32[1]{0:T(128)} %get-tuple-element.72.shift_ref, s32[1]{0:T(128)} %get-tuple-element.73.turns_ref, s32[548]{0:T(1024)S(1)} %get-tuple-element.74.out_ref, ...), custom_call_target="tpu_custom_call" | custom-call | flops 12000000000 | bytes 1048576 | tf_op jit(solution)/shard_map/cond/branch_0_fun/product/pallas_call | solution.py:476
  (64 shorter events, 13.4 us)
Async XLA Ops:
  10.7 3.2 %collective-permute-start = (bf16[20,128,128]{2,1,0:T(8,128)(2,1)S(1)}, bf16[20,128,128]{2,1,0:T(8,128)(2,1)S(1)}, u32[]{:S(2)}, u32[]{:S(2)}) collective-permute-start(bf16[20,128,128]{2,1,0:T(8,128)(2,1)S(1)} %bitcast.32), channel_id=1, source_target_pairs={{0,8},{8,0},{16,24},{24,16},{32,40},{40,32},{48,56},{56,48},{64,72... | collective-permute-start | bytes 1966088 | tf_op jit(solution)/shard_map/ppermute | solution.py:361
  14.9 14.4 %copy-start.3 = (s32[3,64,128]{2,1,0:T(8,128)S(1)}, s32[3,64,128]{2,1,0:T(8,128)}, u32[]{:S(2)}) copy-start(s32[3,64,128]{2,1,0:T(8,128)} %centres_ref.1) | copy-start | bytes 294916
  14.9 14.4 %copy-start.5 = (f32[64,128]{1,0:T(8,128)S(1)}, f32[64,128]{1,0:T(8,128)}, u32[]{:S(2)}) copy-start(f32[64,128]{1,0:T(8,128)} %exponents_ref.1) | copy-start | bytes 98308
  14.9 36.2 %collective-permute-start.3 = (bf16[40,128,128]{2,1,0:T(8,128)(2,1)S(1)}, bf16[40,128,128]{2,1,0:T(8,128)(2,1)S(1)}, u32[]{:S(2)}, u32[]{:S(2)}) collective-permute-start(bf16[40,128,128]{2,1,0:T(8,128)(2,1)S(1)} %pad_maximum_fusion), channel_id=1, source_target_pairs={{0,16},{1,17},{2,18},{3,19},{4,20},{5,21},{6,22},{7,23},{8,10},{9,... | collective-permute-start | bytes 3932168 | tf_op jit(solution)/shard_map/ppermute | solution.py:345
  16.8 34.4 %collective-permute-start.2 = (bf16[40,128,128]{2,1,0:T(8,128)(2,1)S(1)}, bf16[40,128,128]{2,1,0:T(8,128)(2,1)}, u32[]{:S(2)}, u32[]{:S(2)}) collective-permute-start(bf16[40,128,128]{2,1,0:T(8,128)(2,1)S(1)} %pad_maximum_fusion), channel_id=1, source_target_pairs={{0,48},{1,49},{2,50},{3,51},{4,52},{5,53},{6,54},{7,55},{8,14},{9,... | collective-permute-start | bytes 3932168 | tf_op jit(solution)/shard_map/ppermute | solution.py:345
  18.9 32.2 %collective-permute-start.1 = (bf16[40,128,128]{2,1,0:T(8,128)(2,1)S(1)}, bf16[40,128,128]{2,1,0:T(8,128)(2,1)}, u32[]{:S(2)}, u32[]{:S(2)}) collective-permute-start(bf16[40,128,128]{2,1,0:T(8,128)(2,1)S(1)} %pad_maximum_fusion), channel_id=1, source_target_pairs={{0,64},{1,65},{2,66},{3,67},{4,68},{5,69},{6,70},{7,71},{8,73},{9,... | collective-permute-start | bytes 3932168 | tf_op jit(solution)/shard_map/ppermute | solution.py:345
  22.9 28.3 %all-to-all-start = ((bf16[64,80,128]{2,1,0:T(8,128)(2,1)}), bf16[64,80,128]{2,1,0:T(8,128)(2,1)}, u32[]{:S(2)}, u32[]{:S(2)}) async-start(bf16[64,80,128]{2,1,0:T(8,128)(2,1)} %broadcast_in_dim.6), calls=%async_computation | async-start | bytes 2621440 | tf_op jit(solution)/shard_map/all_to_all | solution.py:332
  51.2 9.4 %collective-permute-start.6 = (bf16[64,80,128]{2,1,0:T(8,128)(2,1)}, bf16[64,80,128]{2,1,0:T(8,128)(2,1)S(1)}, u32[]{:S(2)}, u32[]{:S(2)}) collective-permute-start(bf16[64,80,128]{2,1,0:T(8,128)(2,1)} %all-to-all-done), channel_id=1, source_target_pairs={{0,8},{8,0},{16,24},{24,16},{32,40},{40,32},{48,56},{56,48},{64,72... | collective-permute-start | bytes 3932168 | tf_op jit(solution)/shard_map/ppermute | solution.py:361
  56.3 18.8 %collective-permute-start.5 = (bf16[40,128,128]{2,1,0:T(8,128)(2,1)}, bf16[40,128,128]{2,1,0:T(8,128)(2,1)}, u32[]{:S(2)}, u32[]{:S(2)}) collective-permute-start(bf16[40,128,128]{2,1,0:T(8,128)(2,1)} %collective-permute-done.1), channel_id=1, source_target_pairs={{0,0},{1,1},{2,2},{3,3},{4,4},{5,5},{6,6},{7,7},{8,72},{9,73},{10,... | collective-permute-start | bytes 3932168 | tf_op jit(solution)/shard_map/ppermute | solution.py:345
  58.2 17.0 %collective-permute-start.4 = (bf16[40,128,128]{2,1,0:T(8,128)(2,1)}, bf16[40,128,128]{2,1,0:T(8,128)(2,1)S(1)}, u32[]{:S(2)}, u32[]{:S(2)}) collective-permute-start(bf16[40,128,128]{2,1,0:T(8,128)(2,1)} %collective-permute-done.2), channel_id=1, source_target_pairs={{0,48},{1,49},{2,50},{3,51},{4,52},{5,53},{6,54},{7,55},{8,14},{9,... | collective-permute-start | bytes 3932168 | tf_op jit(solution)/shard_map/ppermute | solution.py:345
  66.6 18.8 %copy-start.13 = (bf16[40,128,128]{2,1,0:T(8,128)(2,1)S(1)}, bf16[40,128,128]{2,1,0:T(8,128)(2,1)}, u32[]{:S(2)}) copy-start(bf16[40,128,128]{2,1,0:T(8,128)(2,1)} %copy-done.12) | copy-start | bytes 3932164
  75.2 16.7 %copy-start.14 = (bf16[40,128,128]{2,1,0:T(8,128)(2,1)}, bf16[40,128,128]{2,1,0:T(8,128)(2,1)S(1)}, u32[]{:S(2)}) copy-start(bf16[40,128,128]{2,1,0:T(8,128)(2,1)S(1)} %collective-permute-done.4) | copy-start | bytes 3932164
  75.2 16.8 %collective-permute-start.9 = (bf16[40,128,128]{2,1,0:T(8,128)(2,1)}, bf16[40,128,128]{2,1,0:T(8,128)(2,1)S(1)}, u32[]{:S(2)}, u32[]{:S(2)}) collective-permute-start(bf16[40,128,128]{2,1,0:T(8,128)(2,1)} %collective-permute-done.2), channel_id=1, source_target_pairs={{0,8},{8,0},{16,24},{24,16},{32,40},{40,32},{48,56},{56,48},{64,72... | collective-permute-start | bytes 3932168 | tf_op jit(solution)/shard_map/ppermute | solution.py:361
  85.4 7.3 %collective-permute-start.10 = (bf16[40,128,128]{2,1,0:T(8,128)(2,1)S(1)}, bf16[40,128,128]{2,1,0:T(8,128)(2,1)S(1)}, u32[]{:S(2)}, u32[]{:S(2)}) collective-permute-start(bf16[40,128,128]{2,1,0:T(8,128)(2,1)S(1)} %collective-permute-done.4), channel_id=1, source_target_pairs={{0,8},{8,0},{16,24},{24,16},{32,40},{40,32},{48,56},{56,48},{64,72... | collective-permute-start | bytes 3932168 | tf_op jit(solution)/shard_map/ppermute | solution.py:361
  85.4 7.3 %collective-permute-start.11 = (bf16[40,128,128]{2,1,0:T(8,128)(2,1)S(1)}, bf16[40,128,128]{2,1,0:T(8,128)(2,1)S(1)}, u32[]{:S(2)}, u32[]{:S(2)}) collective-permute-start(bf16[40,128,128]{2,1,0:T(8,128)(2,1)S(1)} %copy-done.13), channel_id=1, source_target_pairs={{0,8},{8,0},{16,24},{24,16},{32,40},{40,32},{48,56},{56,48},{64,72... | collective-permute-start | bytes 3932168 | tf_op jit(solution)/shard_map/ppermute | solution.py:361
  85.9 18.3 %collective-permute-start.8 = (bf16[40,128,128]{2,1,0:T(8,128)(2,1)}, bf16[40,128,128]{2,1,0:T(8,128)(2,1)}, u32[]{:S(2)}, u32[]{:S(2)}) collective-permute-start(bf16[40,128,128]{2,1,0:T(8,128)(2,1)} %collective-permute-done.5), channel_id=1, source_target_pairs={{0,16},{1,17},{2,18},{3,19},{4,20},{5,21},{6,22},{7,23},{8,10},{9,... | collective-permute-start | bytes 3932168 | tf_op jit(solution)/shard_map/ppermute | solution.py:345
  85.9 18.3 %collective-permute-start.7 = (bf16[40,128,128]{2,1,0:T(8,128)(2,1)}, bf16[40,128,128]{2,1,0:T(8,128)(2,1)}, u32[]{:S(2)}, u32[]{:S(2)}) collective-permute-start(bf16[40,128,128]{2,1,0:T(8,128)(2,1)} %collective-permute-done.5), channel_id=1, source_target_pairs={{0,48},{1,49},{2,50},{3,51},{4,52},{5,53},{6,54},{7,55},{8,14},{9,... | collective-permute-start | bytes 3932168 | tf_op jit(solution)/shard_map/ppermute | solution.py:345
  92.0 30.6 %collective-permute-start.14 = (bf16[40,128,128]{2,1,0:T(8,128)(2,1)}, bf16[40,128,128]{2,1,0:T(8,128)(2,1)}, u32[]{:S(2)}, u32[]{:S(2)}) collective-permute-start(bf16[40,128,128]{2,1,0:T(8,128)(2,1)} %collective-permute-done.5), channel_id=1, source_target_pairs={{0,8},{8,0},{16,24},{24,16},{32,40},{40,32},{48,56},{56,48},{64,72... | collective-permute-start | bytes 3932168 | tf_op jit(solution)/shard_map/ppermute | solution.py:361
  104.2 22.8 %collective-permute-start.15 = (bf16[40,128,128]{2,1,0:T(8,128)(2,1)}, bf16[40,128,128]{2,1,0:T(8,128)(2,1)}, u32[]{:S(2)}, u32[]{:S(2)}) collective-permute-start(bf16[40,128,128]{2,1,0:T(8,128)(2,1)} %collective-permute-done.7), channel_id=1, source_target_pairs={{0,8},{8,0},{16,24},{24,16},{32,40},{40,32},{48,56},{56,48},{64,72... | collective-permute-start | bytes 3932168 | tf_op jit(solution)/shard_map/ppermute | solution.py:361
  105.1 21.8 %collective-permute-start.16 = (bf16[40,128,128]{2,1,0:T(8,128)(2,1)}, bf16[40,128,128]{2,1,0:T(8,128)(2,1)}, u32[]{:S(2)}, u32[]{:S(2)}) collective-permute-start(bf16[40,128,128]{2,1,0:T(8,128)(2,1)} %collective-permute-done.8), channel_id=1, source_target_pairs={{0,8},{8,0},{16,24},{24,16},{32,40},{40,32},{48,56},{56,48},{64,72... | collective-permute-start | bytes 3932168 | tf_op jit(solution)/shard_map/ppermute | solution.py:361
  105.2 21.8 %collective-permute-start.12 = (bf16[40,128,128]{2,1,0:T(8,128)(2,1)}, bf16[40,128,128]{2,1,0:T(8,128)(2,1)}, u32[]{:S(2)}, u32[]{:S(2)}) collective-permute-start(bf16[40,128,128]{2,1,0:T(8,128)(2,1)} %collective-permute-done.8), channel_id=1, source_target_pairs={{0,16},{1,17},{2,18},{3,19},{4,20},{5,21},{6,22},{7,23},{8,10},{9,... | collective-permute-start | bytes 3932168 | tf_op jit(solution)/shard_map/ppermute | solution.py:345
  106.1 20.9 %all-to-all-start.1 = ((f32[128,1,128]{2,1,0:T(1,128)}), f32[128,1,128]{2,1,0:T(1,128)S(1)}, u32[]{:S(2)}, u32[]{:S(2)}) async-start(f32[128,1,128]{2,1,0:T(1,128)} %broadcast_in_dim.8), calls=%async_computation.1 | async-start | bytes 131072 | tf_op jit(solution)/shard_map/all_to_all | solution.py:332
  112.9 14.0 %collective-permute-start.13 = (bf16[4,128,128]{2,1,0:T(8,128)(2,1)S(1)}, bf16[4,128,128]{2,1,0:T(8,128)(2,1)}, u32[]{:S(2)}, u32[]{:S(2)}) collective-permute-start(bf16[4,128,128]{2,1,0:T(8,128)(2,1)S(1)} %grid_cols.1), channel_id=1, source_target_pairs={{0,8},{8,0},{16,24},{24,16},{32,40},{40,32},{48,56},{56,48},{64,72... | collective-permute-start | bytes 393224 | tf_op jit(solution)/shard_map/ppermute | solution.py:361
  127.0 4.0 %collective-permute-start.17 = (bf16[40,128,128]{2,1,0:T(8,128)(2,1)}, bf16[40,128,128]{2,1,0:T(8,128)(2,1)S(1)}, u32[]{:S(2)}, u32[]{:S(2)}) collective-permute-start(bf16[40,128,128]{2,1,0:T(8,128)(2,1)} %collective-permute-done.12), channel_id=1, source_target_pairs={{0,8},{8,0},{16,24},{24,16},{32,40},{40,32},{48,56},{56,48},{64,72... | collective-permute-start | bytes 3932168 | tf_op jit(solution)/shard_map/ppermute | solution.py:361
  (13 other events, 64.9 us)

commit v4 on v3

--- a/solution.py
+++ b/solution.py
@@ -77,28 +77,25 @@
 def values_kernel(place_ref, centres_ref, exponents_ref, extents_ref, phi_ref, along_ref):
     row, col = place_ref[0], place_ref[1]
 
-    def one(k, carry):
-        cluster = jnp.where(k < 4, row * 4 + k, col * 8 + row % 2 * 4 + k - 4)
-        decay = column(exponents_ref[pl.ds(cluster, 1), :])
-        reach = column(extents_ref[pl.ds(cluster, 1), :].astype(F32))
-        cut = jnp.exp(-decay * (reach * reach + 0.5))
-        at_x = column(centres_ref[0, pl.ds(cluster, 1), :].astype(F32))
-        at_y = column(centres_ref[1, pl.ds(cluster, 1), :].astype(F32))
-        at_z = column(centres_ref[2, pl.ds(cluster, 1), :].astype(F32))
-        off_z = lax.broadcasted_iota(jnp.int32, (BS, BS), 1).astype(F32) - at_z
-        along_z = jnp.exp(-decay * (off_z * off_z))
+    k = pl.program_id(0)
+    cluster = jnp.where(k < 4, row * 4 + k, col * 8 + row % 2 * 4 + k - 4)
+    decay = column(exponents_ref[pl.ds(cluster, 1), :])
+    reach = column(extents_ref[pl.ds(cluster, 1), :].astype(F32))
+    cut = jnp.exp(-decay * (reach * reach + 0.5))
+    at_x = column(centres_ref[0, pl.ds(cluster, 1), :].astype(F32))
+    at_y = column(centres_ref[1, pl.ds(cluster, 1), :].astype(F32))
+    at_z = column(centres_ref[2, pl.ds(cluster, 1), :].astype(F32))
+    off_z = lax.broadcasted_iota(jnp.int32, (BS, BS), 1).astype(F32) - at_z
+    along_z = jnp.exp(-decay * (off_z * off_z))
+    for y in range(8):
+        off_y = y - at_y
+        along_ref[y] = jnp.exp(-decay * (off_y * off_y))
+    for x in range(8):
+        off_x = x - at_x
+        along_xz = along_z * jnp.exp(-decay * (off_x * off_x))
         for y in range(8):
-            off_y = y - at_y
-            along_ref[y] = jnp.exp(-decay * (off_y * off_y))
-        for x in range(8):
-            off_x = x - at_x
-            along_xz = along_z * jnp.exp(-decay * (off_x * off_x))
-            for y in range(8):
-                phi = along_xz * along_ref[y]
-                phi_ref[k, x, :, y * BS : (y + 1) * BS] = jnp.where(phi >= cut, phi, 0.0).astype(BF16)
-        return carry
-
-    lax.fori_loop(0, 8, one, 0)
+            phi = along_xz * along_ref[y]
+            phi_ref[0, x, :, y * BS : (y + 1) * BS] = jnp.where(phi >= cut, phi, 0.0).astype(BF16)
 
 
 def grid_kernel(with_sum, place_ref, home_ref, shift_ref, bricks_ref, phi_ref, *rest):
@@ -108,24 +105,23 @@
         (blocks_ref,) = rest
     row, col = place_ref[0], place_ref[1]
     first = row * 4 if with_sum else col * 8 + row % 2 * 4
-    place = 0 if with_sum else 4
-
-    def one(k, carry):
-        home = home_ref[first + k]
-        index = (home // 8 ^ row) % 2 * 64 + home // 16 * 8 + home % 8
-        total = jnp.zeros((BS, BS), F32)
-        for x in range(8):
-            values = jnp.concatenate([bricks_ref[index, x * 8 + y : x * 8 + y + 1, :] for y in range(8)], axis=1)
-            phi = phi_ref[place + k, x]
-            total += lax.dot_general(phi * values, phi, (((1,), (1,)), ((), ())), preferred_element_type=F32)
-        blocks_ref[k] = (total * VOLUME).astype(BF16)
-        return carry
-
-    lax.fori_loop(0, 4, one, 0)
+
+    k = pl.program_id(0)
+    home = home_ref[first + k]
+    index = (home // 8 ^ row) % 2 * 64 + home // 16 * 8 + home % 8
+    total = jnp.zeros((BS, BS), F32)
+    for x in range(8):
+        values = jnp.concatenate([bricks_ref[index, x * 8 + y : x * 8 + y + 1, :] for y in range(8)], axis=1)
+        phi = phi_ref[0, x]
+        total += lax.dot_general(phi * values, phi, (((1,), (1,)), ((), ())), preferred_element_type=F32)
+    blocks_ref[k] = (total * VOLUME).astype(BF16)
     if with_sum:
-        total_ref[...] = jnp.sum(sum_ref[...], axis=0, keepdims=True)
-
-        @pl.when(col == row // 2)
+
+        @pl.when(k == 0)
+        def _():
+            total_ref[...] = jnp.sum(sum_ref[...], axis=0, keepdims=True)
+
+        @pl.when((k == 3) & (col == row // 2))
         def _():
             eye = identity()
             for i in range(4):
@@ -400,11 +396,12 @@
     after, before = ring(pair, 1), ring(pair, -1)
     phi = pl.pallas_call(
         values_kernel,
+        grid=(8,),
         in_specs=[SM, VM, VM, VM],
-        out_specs=VM,
+        out_specs=pl.BlockSpec((1, 8, BS, 8 * BS), lambda k: (k, 0, 0, 0)),
         out_shape=jax.ShapeDtypeStruct((8, 8, BS, 8 * BS), BF16),
         scratch_shapes=[pltpu.VMEM((8, BS, BS), F32)],
-        compiler_params=params(4),
+        compiler_params=params(8),
         cost_estimate=lasting(10),
         name="values",
     )(place, centres, exponents, extents)
@@ -416,12 +413,14 @@
 
     def grid_blocks(with_sum, *more):
         extra = [VM, VM] if with_sum else []
+        first = 0 if with_sum else 4
         out_shape = [jax.ShapeDtypeStruct((4, BS, BS), BF16)]
         if with_sum:
             out_shape.append(jax.ShapeDtypeStruct((1, BS), F32))
         return pl.pallas_call(
             functools.partial(grid_kernel, with_sum),
-            in_specs=[SM, SM, SM, VM, VM] + extra,
+            grid=(4,),
+            in_specs=[SM, SM, SM, VM, pl.BlockSpec((1, 8, BS, 8 * BS), lambda k: (first + k, 0, 0, 0))] + extra,
             out_specs=[VM] * len(out_shape),
             out_shape=out_shape,
             compiler_params=params(8),
@@ -430,21 +429,21 @@
         )(place, home, shift, bricks, phi, *more)
 
     row_grid, total = grid_blocks(True, core_matrix, squares)
-    after, before, far, other, row_grid, total, bricks = lax.optimization_barrier(
-        (after, before, far, other, row_grid, total, bricks)
+    after, before, far, other, row_grid, bricks = lax.optimization_barrier(
+        (after, before, far, other, row_grid, bricks)
     )
 
     other_after, other_before = ring(other, 1), ring(other, -1)
     crossings = [to_core(after), to_core(far), to_core(before)]
     (col_grid,) = grid_blocks(False)
-    other_after, other_before, col_grid, total, bricks, *crossings = lax.optimization_barrier(
-        (other_after, other_before, col_grid, total, bricks, *crossings)
+    frob = to_all(total, ("row", "col"), 128).reshape(128, BS)
+    other_after, other_before, col_grid, frob, bricks, *crossings = lax.optimization_barrier(
+        (other_after, other_before, col_grid, frob, bricks, *crossings)
     )
 
     other_far = ring(other_before, -1)
     crossings += [to_core(other), to_core(other_after), to_core(other_before)]
     col_grid_crossed = to_core(col_grid)
-    frob = to_all(total, ("row", "col"), 128).reshape(128, BS)
     *listed, most = pl.pallas_call(
         plan_kernel,
         in_specs=[SM, VM],
@@ -463,8 +462,8 @@
         cost_estimate=lasting(9),
         name="plan",
     )(place, bricks)
-    other_far, col_grid_crossed, frob, *rest = lax.optimization_barrier(
-        (other_far, col_grid_crossed, frob, *crossings, *listed)
+    other_far, col_grid_crossed, *rest = lax.optimization_barrier(
+        (other_far, col_grid_crossed, *crossings, *listed)
     )
     crossings, listed = rest[:6], rest[6:]
 

time: 151 us -> 149 us (0.987)
  waiting for transfers between devices: 32.7 us -> 27.4 us
  local copies, waits for them, and re-layouts: 17.4 us -> 21.5 us
  starting transfers between devices: 46.2 us -> 44.6 us
    unnamed x35 -> x23, local copies, waits for them, and re-layouts: 15.3 us -> 19.5 us
    ppermute x8, waiting for transfers between devices: 15.7 us -> 12.3 us  [move(): lax.ppermute(value, ('row', 'col'), [(k, device_of(*where(*place_of(k))))...]
    all_to_all x2, starting transfers between devices: 13.2 us -> 10.5 us  [to_all(): return lax.all_to_all(copies, axis, 0, 0, axis_index_groups=groups)]
    all_to_all x2, waiting for transfers between devices: 13.1 us -> 11.4 us  [to_all(): return lax.all_to_all(copies, axis, 0, 0, axis_index_groups=groups)]
where the time goes in v4:
time: 149 us; the launch traced here: 147 us
  starting transfers between devices  44.6 us (30%)
  Pallas kernels  37.2 us (25%)
  waiting for transfers between devices  27.4 us (18%)
  local copies, waits for them, and re-layouts  21.5 us (14%)
  between operations  15.6 us (10%)
    ppermute x10, starting transfers between devices, to_core(): return lax.ppermute(value, 'row', [(k, k ^ 1) for k in range(16)])  22.1 us
    unnamed x23, local copies, waits for them, and re-layouts  19.5 us
    ppermute x8, waiting for transfers between devices, move(): lax.ppermute(value, ('row', 'col'), [(k, device_of(*where(*place_of(k))))...  12.3 us
    ppermute x8, starting transfers between devices, move(): lax.ppermute(value, ('row', 'col'), [(k, device_of(*where(*place_of(k))))...  12 us
    all_to_all x2, waiting for transfers between devices, to_all(): return lax.all_to_all(copies, axis, 0, 0, axis_index_groups=groups)  11.4 us
    all_to_all x2, starting transfers between devices, to_all(): return lax.all_to_all(copies, axis, 0, 0, axis_index_groups=groups)  10.5 us
    pallas_call x1, Pallas kernels, sparse(): pl.pallas_call(product_kernel, in_specs=[SM] * 7 + [VM] * 5 + [ANY] * 16,...  10.4 us
    pallas_call x2, Pallas kernels, grid_blocks(): pl.pallas_call(functools.partial(grid_kernel, with_sum), grid=(4,), in_sp...  8.36 us
  transfers between devices with their start and end apart: 20, of which 7 were waited for; matrix products, arithmetic and copies ran while one was open for 2% of the time, Pallas kernels for 16%

profile of v4, /device:TPU:1, one launch (start us, length us, event | category | flops | bytes accessed | tf_op | source)
XLA Modules:
  0.0 146.5 jit_solution(11512783882741946385)
XLA Ops:
  8.8 2.2 %pack.1 = (bf16[2560,128]{1,0:T(8,128)(2,1)S(1)}, f32[8,128]{1,0:T(8,128)S(1)}) custom-call(s32[4,8]{1,0:T(4,128)S(1)} %copy-done.10, s32[2]{0:T(128)S(1)} %pad_add_fusion.place_ref, bf16[512,1024]{1,0:T(8,128)(2,1)} %rest_0_.1), custom_call_target="tpu_custom_call" | custom-call | flops 2000000000 | bytes 1048576 | tf_op jit(solution)/shard_map/pack/pallas_call | solution.py:382
  14.4 1.8 %collective-permute-start.3 = (bf16[40,128,128]{2,1,0:T(8,128)(2,1)S(1)}, bf16[40,128,128]{2,1,0:T(8,128)(2,1)}, u32[]{:S(2)}, u32[]{:S(2)}) collective-permute-start(bf16[40,128,128]{2,1,0:T(8,128)(2,1)S(1)} %pad_maximum_fusion), channel_id=1, source_target_pairs={{0,16},{1,17},{2,18},{3,19},{4,20},{5,21},{6,22},{7,23},{8,10},{9,... | collective-permute-start | bytes 3932168 | tf_op jit(solution)/shard_map/ppermute | solution.py:341
  16.1 2.3 %collective-permute-start.2 = (bf16[40,128,128]{2,1,0:T(8,128)(2,1)S(1)}, bf16[40,128,128]{2,1,0:T(8,128)(2,1)}, u32[]{:S(2)}, u32[]{:S(2)}) collective-permute-start(bf16[40,128,128]{2,1,0:T(8,128)(2,1)S(1)} %pad_maximum_fusion), channel_id=1, source_target_pairs={{0,48},{1,49},{2,50},{3,51},{4,52},{5,53},{6,54},{7,55},{8,14},{9,... | collective-permute-start | bytes 3932168 | tf_op jit(solution)/shard_map/ppermute | solution.py:341
  18.4 2.7 %collective-permute-start.1 = (bf16[40,128,128]{2,1,0:T(8,128)(2,1)S(1)}, bf16[40,128,128]{2,1,0:T(8,128)(2,1)}, u32[]{:S(2)}, u32[]{:S(2)}) collective-permute-start(bf16[40,128,128]{2,1,0:T(8,128)(2,1)S(1)} %pad_maximum_fusion), channel_id=1, source_target_pairs={{0,64},{1,65},{2,66},{3,67},{4,68},{5,69},{6,70},{7,71},{8,73},{9,... | collective-permute-start | bytes 3932168 | tf_op jit(solution)/shard_map/ppermute | solution.py:341
  22.3 6.4 %all-to-all-start = ((bf16[64,80,128]{2,1,0:T(8,128)(2,1)}), bf16[64,80,128]{2,1,0:T(8,128)(2,1)}, u32[]{:S(2)}, u32[]{:S(2)}) async-start(bf16[64,80,128]{2,1,0:T(8,128)(2,1)} %broadcast_in_dim.6), calls=%async_computation | async-start | bytes 2621440 | tf_op jit(solution)/shard_map/all_to_all | solution.py:328
  28.8 7.5 %values.1.phi_ref = bf16[8,8,128,1024]{3,2,1,0:T(8,128)(2,1)S(1)} custom-call(s32[2]{0:T(128)S(1)} %pad_add_fusion.place_ref, s32[3,64,128]{2,1,0:T(8,128)S(1)} %copy-done.4, f32[64,128]{1,0:T(8,128)S(1)} %copy-done.6, s32[64,128]{1,0:T(8,128)S(1)} %copy-done.7), custom_call_target="tpu_custom_call" | custom-call | flops 10000000000 | bytes 1048576 | tf_op jit(solution)/shard_map/values/pallas_call | solution.py:397
  36.3 5.7 %copy-done = bf16[8,8,128,1024]{3,2,1,0:T(8,128)(2,1)} copy-done((bf16[8,8,128,1024]{3,2,1,0:T(8,128)(2,1)}, bf16[8,8,128,1024]{3,2,1,0:T(8,128)(2,1)S(1)}, u32[]{:S(2)}) %copy-start) | copy-done | bytes 16777240
  42.1 8.5 %all-to-all-done = bf16[64,80,128]{2,1,0:T(8,128)(2,1)} async-done(((bf16[64,80,128]{2,1,0:T(8,128)(2,1)}), bf16[64,80,128]{2,1,0:T(8,128)(2,1)}, u32[]{:S(2)}, u32[]{:S(2)}) %all-to-all-start) | async-done | bytes 1310752 | tf_op jit(solution)/shard_map/all_to_all | solution.py:328
  50.6 5.1 %collective-permute-start.6 = (bf16[64,80,128]{2,1,0:T(8,128)(2,1)}, bf16[64,80,128]{2,1,0:T(8,128)(2,1)S(1)}, u32[]{:S(2)}, u32[]{:S(2)}) collective-permute-start(bf16[64,80,128]{2,1,0:T(8,128)(2,1)} %all-to-all-done), channel_id=1, source_target_pairs={{0,8},{8,0},{16,24},{24,16},{32,40},{40,32},{48,56},{56,48},{64,72... | collective-permute-start | bytes 3932168 | tf_op jit(solution)/shard_map/ppermute | solution.py:357
  55.7 1.9 %collective-permute-start.5 = (bf16[40,128,128]{2,1,0:T(8,128)(2,1)}, bf16[40,128,128]{2,1,0:T(8,128)(2,1)}, u32[]{:S(2)}, u32[]{:S(2)}) collective-permute-start(bf16[40,128,128]{2,1,0:T(8,128)(2,1)} %collective-permute-done.1), channel_id=1, source_target_pairs={{0,0},{1,1},{2,2},{3,3},{4,4},{5,5},{6,6},{7,7},{8,72},{9,73},{10,... | collective-permute-start | bytes 3932168 | tf_op jit(solution)/shard_map/ppermute | solution.py:341
  60.1 5.8 %copy-done.1 = bf16[8,8,128,1024]{3,2,1,0:T(8,128)(2,1)S(1)} copy-done((bf16[8,8,128,1024]{3,2,1,0:T(8,128)(2,1)S(1)}, bf16[8,8,128,1024]{3,2,1,0:T(8,128)(2,1)}, u32[]{:S(2)}) %copy-start.1) | copy-done | bytes 16777240
  65.8 4.9 %grid_rows.1 = (bf16[4,128,128]{2,1,0:T(8,128)(2,1)}, f32[1,128]{1,0:T(1,128)S(1)}) custom-call(s32[2]{0:T(128)S(1)} %pad_add_fusion.place_ref, s32[64]{0:T(128)S(1)} %copy-done.3, f32[1]{0:T(128)S(6)} %copy.24.shift_ref, bf16[128,80,128]{2,1,0:T(8,128)(2,1)S(1)} %constant_dynamic-update-slice_fusion.bricks_ref, bf16[8,8,128,1024]{3,2,1,0:T(8,128)(2,1)S(1)} %copy-done.1, ...), custom_call_target="tpu_custom_call" | custom-call | flops 5000000000 | bytes 1048576 | tf_op jit(solution)/shard_map/grid_rows/pallas_call | solution.py:420
  70.7 3.9 %collective-permute-done.5 = bf16[40,128,128]{2,1,0:T(8,128)(2,1)} collective-permute-done((bf16[40,128,128]{2,1,0:T(8,128)(2,1)}, bf16[40,128,128]{2,1,0:T(8,128)(2,1)}, u32[]{:S(2)}, u32[]{:S(2)}) %collective-permute-start.5) | collective-permute-done | bytes 1310752 | tf_op jit(solution)/shard_map/ppermute | solution.py:341
  74.7 10.2 %collective-permute-start.9 = (bf16[40,128,128]{2,1,0:T(8,128)(2,1)}, bf16[40,128,128]{2,1,0:T(8,128)(2,1)}, u32[]{:S(2)}, u32[]{:S(2)}) collective-permute-start(bf16[40,128,128]{2,1,0:T(8,128)(2,1)} %collective-permute-done.2), channel_id=1, source_target_pairs={{0,8},{8,0},{16,24},{24,16},{32,40},{40,32},{48,56},{56,48},{64,72... | collective-permute-start | bytes 3932168 | tf_op jit(solution)/shard_map/ppermute | solution.py:357
  85.5 2.7 %collective-permute-start.7 = (bf16[40,128,128]{2,1,0:T(8,128)(2,1)}, bf16[40,128,128]{2,1,0:T(8,128)(2,1)}, u32[]{:S(2)}, u32[]{:S(2)}) collective-permute-start(bf16[40,128,128]{2,1,0:T(8,128)(2,1)} %collective-permute-done.5), channel_id=1, source_target_pairs={{0,48},{1,49},{2,50},{3,51},{4,52},{5,53},{6,54},{7,55},{8,14},{9,... | collective-permute-start | bytes 3932168 | tf_op jit(solution)/shard_map/ppermute | solution.py:341
  88.8 4.1 %all-to-all-start.1 = ((f32[128,1,128]{2,1,0:T(1,128)}), f32[128,1,128]{2,1,0:T(1,128)S(1)}, u32[]{:S(2)}, u32[]{:S(2)}) async-start(f32[128,1,128]{2,1,0:T(1,128)} %broadcast_in_dim.8), calls=%async_computation.1 | async-start | bytes 131072 | tf_op jit(solution)/shard_map/all_to_all | solution.py:328
  92.9 5.8 %copy-done.2 = bf16[8,8,128,1024]{3,2,1,0:T(8,128)(2,1)S(1)} copy-done((bf16[8,8,128,1024]{3,2,1,0:T(8,128)(2,1)S(1)}, bf16[8,8,128,1024]{3,2,1,0:T(8,128)(2,1)}, u32[]{:S(2)}) %copy-start.2) | copy-done | bytes 16777240
  98.6 3.5 %grid_cols.1 = bf16[4,128,128]{2,1,0:T(8,128)(2,1)S(1)} custom-call(s32[2]{0:T(128)S(1)} %pad_add_fusion.place_ref, s32[64]{0:T(128)S(1)} %copy-done.3, f32[1]{0:T(128)S(6)} %copy.24.shift_ref, bf16[128,80,128]{2,1,0:T(8,128)(2,1)S(1)} %constant_dynamic-update-slice_fusion.bricks_ref, bf16[8,8,128,1024]{3,2,1,0:T(8,128)(2,1)S(1)} %copy-done.2), custom_call_target="tpu_custom_call" | custom-call | flops 5000000000 | bytes 1048576 | tf_op jit(solution)/shard_map/grid_cols/pallas_call | solution.py:420
  103.3 2.9 %all-to-all-done.1 = f32[128,1,128]{2,1,0:T(1,128)S(1)} async-done(((f32[128,1,128]{2,1,0:T(1,128)}), f32[128,1,128]{2,1,0:T(1,128)S(1)}, u32[]{:S(2)}, u32[]{:S(2)}) %all-to-all-start.1) | async-done | bytes 65568 | tf_op jit(solution)/shard_map/all_to_all | solution.py:328
  109.0 8.1 %plan.1 = (s32[1]{0:T(128)}, s32[548]{0:T(1024)S(1)}, s32[2192]{0:T(1024)S(1)}, s32[2192]{0:T(1024)S(1)}, s32[1]{0:T(128)}) custom-call(s32[2]{0:T(128)S(1)} %pad_add_fusion.place_ref, bf16[128,80,128]{2,1,0:T(8,128)(2,1)S(1)} %constant_dynamic-update-slice_fusion.bricks_ref), custom_call_target="tpu_custom_call" | custom-call | flops 8999999488 | bytes 1048576 | tf_op jit(solution)/shard_map/plan/pallas_call | solution.py:447
  117.1 8.2 %collective-permute-done.12 = bf16[40,128,128]{2,1,0:T(8,128)(2,1)S(1)} collective-permute-done((bf16[40,128,128]{2,1,0:T(8,128)(2,1)}, bf16[40,128,128]{2,1,0:T(8,128)(2,1)S(1)}, u32[]{:S(2)}, u32[]{:S(2)}) %collective-permute-start.12) | collective-permute-done | bytes 1310752 | tf_op jit(solution)/shard_map/ppermute | solution.py:341
  127.3 2.0 %collective-permute-done.17 = bf16[40,128,128]{2,1,0:T(8,128)(2,1)S(1)} collective-permute-done((bf16[40,128,128]{2,1,0:T(8,128)(2,1)S(1)}, bf16[40,128,128]{2,1,0:T(8,128)(2,1)S(1)}, u32[]{:S(2)}, u32[]{:S(2)}) %collective-permute-start.17) | collective-permute-done | bytes 1310752 | tf_op jit(solution)/shard_map/ppermute | solution.py:357
  129.3 10.4 %conditional.1 = ((bf16[512,1024]{1,0:T(8,128)(2,1)}, bf16[512,1024]{1,0:T(8,128)(2,1)})) conditional(s32[]{:T(128)} %bitcast.7, (s32[2]{0:T(128)S(1)}, s32[4,8]{1,0:T(4,128)S(1)}, f32[1]{0:T(128)}, s32[1]{0:T(128)}, s32[548]{0:T(1024)S(1)}, /*index=5*/s32[2192]{0:T(1024)S(1)}, s32[2192]{0:T(1024)S(1)}, f32[128,128]{1,0:T(8,128)S(1)}, ...), branch_computations={%region_0.0_spmd, %region_1.0_spmd} | conditional | flops 12000000000 | bytes 121439128 | solution.py:509
  129.3 10.4 %product.1 = (bf16[512,1024]{1,0:T(8,128)(2,1)}, bf16[512,1024]{1,0:T(8,128)(2,1)}) custom-call(s32[2]{0:T(128)S(1)} %get-tuple-element.70.place_ref, s32[4,8]{1,0:T(4,128)S(1)} %get-tuple-element.71.pattern_ref, f32[1]{0:T(128)} %get-tuple-element.72.shift_ref, s32[1]{0:T(128)} %get-tuple-element.73.turns_ref, s32[548]{0:T(1024)S(1)} %get-tuple-element.74.out_ref, ...), custom_call_target="tpu_custom_call" | custom-call | flops 12000000000 | bytes 1048576 | tf_op jit(solution)/shard_map/cond/branch_0_fun/product/pallas_call | solution.py:475
  (52 shorter events, 14.6 us)
Async XLA Ops:
  10.9 3.3 %collective-permute-start = (bf16[20,128,128]{2,1,0:T(8,128)(2,1)S(1)}, bf16[20,128,128]{2,1,0:T(8,128)(2,1)S(1)}, u32[]{:S(2)}, u32[]{:S(2)}) collective-permute-start(bf16[20,128,128]{2,1,0:T(8,128)(2,1)S(1)} %bitcast.32), channel_id=1, source_target_pairs={{0,8},{8,0},{16,24},{24,16},{32,40},{40,32},{48,56},{56,48},{64,72... | collective-permute-start | bytes 1966088 | tf_op jit(solution)/shard_map/ppermute | solution.py:357
  14.3 14.4 %copy-start.4 = (s32[3,64,128]{2,1,0:T(8,128)S(1)}, s32[3,64,128]{2,1,0:T(8,128)}, u32[]{:S(2)}) copy-start(s32[3,64,128]{2,1,0:T(8,128)} %centres_ref.1) | copy-start | bytes 294916
  14.3 14.4 %copy-start.6 = (f32[64,128]{1,0:T(8,128)S(1)}, f32[64,128]{1,0:T(8,128)}, u32[]{:S(2)}) copy-start(f32[64,128]{1,0:T(8,128)} %exponents_ref.1) | copy-start | bytes 98308
  14.3 14.4 %copy-start.7 = (s32[64,128]{1,0:T(8,128)S(1)}, s32[64,128]{1,0:T(8,128)}, u32[]{:S(2)}) copy-start(s32[64,128]{1,0:T(8,128)} %extents_ref.1) | copy-start | bytes 98308
  14.4 36.2 %collective-permute-start.3 = (bf16[40,128,128]{2,1,0:T(8,128)(2,1)S(1)}, bf16[40,128,128]{2,1,0:T(8,128)(2,1)}, u32[]{:S(2)}, u32[]{:S(2)}) collective-permute-start(bf16[40,128,128]{2,1,0:T(8,128)(2,1)S(1)} %pad_maximum_fusion), channel_id=1, source_target_pairs={{0,16},{1,17},{2,18},{3,19},{4,20},{5,21},{6,22},{7,23},{8,10},{9,... | collective-permute-start | bytes 3932168 | tf_op jit(solution)/shard_map/ppermute | solution.py:341
  16.1 34.5 %collective-permute-start.2 = (bf16[40,128,128]{2,1,0:T(8,128)(2,1)S(1)}, bf16[40,128,128]{2,1,0:T(8,128)(2,1)}, u32[]{:S(2)}, u32[]{:S(2)}) collective-permute-start(bf16[40,128,128]{2,1,0:T(8,128)(2,1)S(1)} %pad_maximum_fusion), channel_id=1, source_target_pairs={{0,48},{1,49},{2,50},{3,51},{4,52},{5,53},{6,54},{7,55},{8,14},{9,... | collective-permute-start | bytes 3932168 | tf_op jit(solution)/shard_map/ppermute | solution.py:341
  18.4 32.2 %collective-permute-start.1 = (bf16[40,128,128]{2,1,0:T(8,128)(2,1)S(1)}, bf16[40,128,128]{2,1,0:T(8,128)(2,1)}, u32[]{:S(2)}, u32[]{:S(2)}) collective-permute-start(bf16[40,128,128]{2,1,0:T(8,128)(2,1)S(1)} %pad_maximum_fusion), channel_id=1, source_target_pairs={{0,64},{1,65},{2,66},{3,67},{4,68},{5,69},{6,70},{7,71},{8,73},{9,... | collective-permute-start | bytes 3932168 | tf_op jit(solution)/shard_map/ppermute | solution.py:341
  22.3 28.3 %all-to-all-start = ((bf16[64,80,128]{2,1,0:T(8,128)(2,1)}), bf16[64,80,128]{2,1,0:T(8,128)(2,1)}, u32[]{:S(2)}, u32[]{:S(2)}) async-start(bf16[64,80,128]{2,1,0:T(8,128)(2,1)} %broadcast_in_dim.6), calls=%async_computation | async-start | bytes 2621440 | tf_op jit(solution)/shard_map/all_to_all | solution.py:328
  50.6 9.3 %collective-permute-start.6 = (bf16[64,80,128]{2,1,0:T(8,128)(2,1)}, bf16[64,80,128]{2,1,0:T(8,128)(2,1)S(1)}, u32[]{:S(2)}, u32[]{:S(2)}) collective-permute-start(bf16[64,80,128]{2,1,0:T(8,128)(2,1)} %all-to-all-done), channel_id=1, source_target_pairs={{0,8},{8,0},{16,24},{24,16},{32,40},{40,32},{48,56},{56,48},{64,72... | collective-permute-start | bytes 3932168 | tf_op jit(solution)/shard_map/ppermute | solution.py:357
  55.7 19.0 %collective-permute-start.5 = (bf16[40,128,128]{2,1,0:T(8,128)(2,1)}, bf16[40,128,128]{2,1,0:T(8,128)(2,1)}, u32[]{:S(2)}, u32[]{:S(2)}) collective-permute-start(bf16[40,128,128]{2,1,0:T(8,128)(2,1)} %collective-permute-done.1), channel_id=1, source_target_pairs={{0,0},{1,1},{2,2},{3,3},{4,4},{5,5},{6,6},{7,7},{8,72},{9,73},{10,... | collective-permute-start | bytes 3932168 | tf_op jit(solution)/shard_map/ppermute | solution.py:341
  57.6 17.1 %collective-permute-start.4 = (bf16[40,128,128]{2,1,0:T(8,128)(2,1)}, bf16[40,128,128]{2,1,0:T(8,128)(2,1)}, u32[]{:S(2)}, u32[]{:S(2)}) collective-permute-start(bf16[40,128,128]{2,1,0:T(8,128)(2,1)} %collective-permute-done.2), channel_id=1, source_target_pairs={{0,48},{1,49},{2,50},{3,51},{4,52},{5,53},{6,54},{7,55},{8,14},{9,... | collective-permute-start | bytes 3932168 | tf_op jit(solution)/shard_map/ppermute | solution.py:341
  74.7 27.4 %collective-permute-start.9 = (bf16[40,128,128]{2,1,0:T(8,128)(2,1)}, bf16[40,128,128]{2,1,0:T(8,128)(2,1)}, u32[]{:S(2)}, u32[]{:S(2)}) collective-permute-start(bf16[40,128,128]{2,1,0:T(8,128)(2,1)} %collective-permute-done.2), channel_id=1, source_target_pairs={{0,8},{8,0},{16,24},{24,16},{32,40},{40,32},{48,56},{56,48},{64,72... | collective-permute-start | bytes 3932168 | tf_op jit(solution)/shard_map/ppermute | solution.py:357
  84.9 21.2 %collective-permute-start.10 = (bf16[40,128,128]{2,1,0:T(8,128)(2,1)}, bf16[40,128,128]{2,1,0:T(8,128)(2,1)}, u32[]{:S(2)}, u32[]{:S(2)}) collective-permute-start(bf16[40,128,128]{2,1,0:T(8,128)(2,1)} %collective-permute-done.4), channel_id=1, source_target_pairs={{0,8},{8,0},{16,24},{24,16},{32,40},{40,32},{48,56},{56,48},{64,72... | collective-permute-start | bytes 3932168 | tf_op jit(solution)/shard_map/ppermute | solution.py:357
  84.9 21.2 %collective-permute-start.11 = (bf16[40,128,128]{2,1,0:T(8,128)(2,1)}, bf16[40,128,128]{2,1,0:T(8,128)(2,1)}, u32[]{:S(2)}, u32[]{:S(2)}) collective-permute-start(bf16[40,128,128]{2,1,0:T(8,128)(2,1)} %collective-permute-done.3), channel_id=1, source_target_pairs={{0,8},{8,0},{16,24},{24,16},{32,40},{40,32},{48,56},{56,48},{64,72... | collective-permute-start | bytes 3932168 | tf_op jit(solution)/shard_map/ppermute | solution.py:357
  85.5 20.7 %collective-permute-start.8 = (bf16[40,128,128]{2,1,0:T(8,128)(2,1)}, bf16[40,128,128]{2,1,0:T(8,128)(2,1)}, u32[]{:S(2)}, u32[]{:S(2)}) collective-permute-start(bf16[40,128,128]{2,1,0:T(8,128)(2,1)} %collective-permute-done.5), channel_id=1, source_target_pairs={{0,16},{1,17},{2,18},{3,19},{4,20},{5,21},{6,22},{7,23},{8,10},{9,... | collective-permute-start | bytes 3932168 | tf_op jit(solution)/shard_map/ppermute | solution.py:341
  85.5 20.7 %collective-permute-start.7 = (bf16[40,128,128]{2,1,0:T(8,128)(2,1)}, bf16[40,128,128]{2,1,0:T(8,128)(2,1)}, u32[]{:S(2)}, u32[]{:S(2)}) collective-permute-start(bf16[40,128,128]{2,1,0:T(8,128)(2,1)} %collective-permute-done.5), channel_id=1, source_target_pairs={{0,48},{1,49},{2,50},{3,51},{4,52},{5,53},{6,54},{7,55},{8,14},{9,... | collective-permute-start | bytes 3932168 | tf_op jit(solution)/shard_map/ppermute | solution.py:341
  88.8 17.3 %all-to-all-start.1 = ((f32[128,1,128]{2,1,0:T(1,128)}), f32[128,1,128]{2,1,0:T(1,128)S(1)}, u32[]{:S(2)}, u32[]{:S(2)}) async-start(f32[128,1,128]{2,1,0:T(1,128)} %broadcast_in_dim.8), calls=%async_computation.1 | async-start | bytes 131072 | tf_op jit(solution)/shard_map/all_to_all | solution.py:328
  102.1 15.0 %collective-permute-start.14 = (bf16[40,128,128]{2,1,0:T(8,128)(2,1)}, bf16[40,128,128]{2,1,0:T(8,128)(2,1)}, u32[]{:S(2)}, u32[]{:S(2)}) collective-permute-start(bf16[40,128,128]{2,1,0:T(8,128)(2,1)} %collective-permute-done.5), channel_id=1, source_target_pairs={{0,8},{8,0},{16,24},{24,16},{32,40},{40,32},{48,56},{56,48},{64,72... | collective-permute-start | bytes 3932168 | tf_op jit(solution)/shard_map/ppermute | solution.py:357
  106.2 23.1 %copy-start.9 = (bf16[20,128,128]{2,1,0:T(8,128)(2,1)S(1)}, bf16[20,128,128]{2,1,0:T(8,128)(2,1)}, u32[]{:S(2)}) copy-start(bf16[20,128,128]{2,1,0:T(8,128)(2,1)} %copy-done.8) | copy-start | bytes 1966084
  106.2 10.9 %collective-permute-start.15 = (bf16[40,128,128]{2,1,0:T(8,128)(2,1)}, bf16[40,128,128]{2,1,0:T(8,128)(2,1)S(1)}, u32[]{:S(2)}, u32[]{:S(2)}) collective-permute-start(bf16[40,128,128]{2,1,0:T(8,128)(2,1)} %collective-permute-done.7), channel_id=1, source_target_pairs={{0,8},{8,0},{16,24},{24,16},{32,40},{40,32},{48,56},{56,48},{64,72... | collective-permute-start | bytes 3932168 | tf_op jit(solution)/shard_map/ppermute | solution.py:357
  107.1 10.0 %collective-permute-start.16 = (bf16[40,128,128]{2,1,0:T(8,128)(2,1)}, bf16[40,128,128]{2,1,0:T(8,128)(2,1)S(1)}, u32[]{:S(2)}, u32[]{:S(2)}) collective-permute-start(bf16[40,128,128]{2,1,0:T(8,128)(2,1)} %collective-permute-done.8), channel_id=1, source_target_pairs={{0,8},{8,0},{16,24},{24,16},{32,40},{40,32},{48,56},{56,48},{64,72... | collective-permute-start | bytes 3932168 | tf_op jit(solution)/shard_map/ppermute | solution.py:357
  107.2 18.2 %collective-permute-start.12 = (bf16[40,128,128]{2,1,0:T(8,128)(2,1)}, bf16[40,128,128]{2,1,0:T(8,128)(2,1)S(1)}, u32[]{:S(2)}, u32[]{:S(2)}) collective-permute-start(bf16[40,128,128]{2,1,0:T(8,128)(2,1)} %collective-permute-done.8), channel_id=1, source_target_pairs={{0,16},{1,17},{2,18},{3,19},{4,20},{5,21},{6,22},{7,23},{8,10},{9,... | collective-permute-start | bytes 3932168 | tf_op jit(solution)/shard_map/ppermute | solution.py:341
  107.7 9.4 %collective-permute-start.13 = (bf16[4,128,128]{2,1,0:T(8,128)(2,1)S(1)}, bf16[4,128,128]{2,1,0:T(8,128)(2,1)S(1)}, u32[]{:S(2)}, u32[]{:S(2)}) collective-permute-start(bf16[4,128,128]{2,1,0:T(8,128)(2,1)S(1)} %grid_cols.1), channel_id=1, source_target_pairs={{0,8},{8,0},{16,24},{24,16},{32,40},{40,32},{48,56},{56,48},{64,72... | collective-permute-start | bytes 393224 | tf_op jit(solution)/shard_map/ppermute | solution.py:357
  125.3 3.9 %collective-permute-start.17 = (bf16[40,128,128]{2,1,0:T(8,128)(2,1)S(1)}, bf16[40,128,128]{2,1,0:T(8,128)(2,1)S(1)}, u32[]{:S(2)}, u32[]{:S(2)}) collective-permute-start(bf16[40,128,128]{2,1,0:T(8,128)(2,1)S(1)} %collective-permute-done.12), channel_id=1, source_target_pairs={{0,8},{8,0},{16,24},{24,16},{32,40},{40,32},{48,56},{56,48},{64,72... | collective-permute-start | bytes 3932168 | tf_op jit(solution)/shard_map/ppermute | solution.py:357
  (7 other events, 29.4 us)

commit v5 on v3

--- a/solution.py
+++ b/solution.py
@@ -74,10 +74,17 @@
     return jnp.broadcast_to(row_values, (BS, BS)).T
 
 
-def values_kernel(place_ref, centres_ref, exponents_ref, extents_ref, phi_ref, along_ref):
+def values_kernel(place_ref, centres_ref, exponents_ref, extents_ref, phi_ref, along_ref, slots, sems):
     row, col = place_ref[0], place_ref[1]
 
+    def copy(k):
+        return pltpu.make_async_copy(slots.at[k % 2], phi_ref.at[k], sems.at[k % 2])
+
     def one(k, carry):
+        @pl.when(k >= 2)
+        def _():
+            copy(k - 2).wait()
+
         cluster = jnp.where(k < 4, row * 4 + k, col * 8 + row % 2 * 4 + k - 4)
         decay = column(exponents_ref[pl.ds(cluster, 1), :])
         reach = column(extents_ref[pl.ds(cluster, 1), :].astype(F32))
@@ -95,28 +102,38 @@
             along_xz = along_z * jnp.exp(-decay * (off_x * off_x))
             for y in range(8):
                 phi = along_xz * along_ref[y]
-                phi_ref[k, x, :, y * BS : (y + 1) * BS] = jnp.where(phi >= cut, phi, 0.0).astype(BF16)
+                slots[k % 2, x, :, y * BS : (y + 1) * BS] = jnp.where(phi >= cut, phi, 0.0).astype(BF16)
+        copy(k).start()
         return carry
 
     lax.fori_loop(0, 8, one, 0)
+    copy(6).wait()
+    copy(7).wait()
 
 
 def grid_kernel(with_sum, place_ref, home_ref, shift_ref, bricks_ref, phi_ref, *rest):
     if with_sum:
-        core_ref, sum_ref, blocks_ref, total_ref = rest
+        core_ref, sum_ref, blocks_ref, total_ref, slots, sems = rest
     else:
-        (blocks_ref,) = rest
+        blocks_ref, slots, sems = rest
     row, col = place_ref[0], place_ref[1]
     first = row * 4 if with_sum else col * 8 + row % 2 * 4
     place = 0 if with_sum else 4
 
+    def copy(k):
+        return pltpu.make_async_copy(phi_ref.at[place + k], slots.at[k], sems.at[k])
+
+    for k in range(4):
+        copy(k).start()
+
     def one(k, carry):
         home = home_ref[first + k]
         index = (home // 8 ^ row) % 2 * 64 + home // 16 * 8 + home % 8
+        copy(k).wait()
         total = jnp.zeros((BS, BS), F32)
         for x in range(8):
             values = jnp.concatenate([bricks_ref[index, x * 8 + y : x * 8 + y + 1, :] for y in range(8)], axis=1)
-            phi = phi_ref[place + k, x]
+            phi = slots[k, x]
             total += lax.dot_general(phi * values, phi, (((1,), (1,)), ((), ())), preferred_element_type=F32)
         blocks_ref[k] = (total * VOLUME).astype(BF16)
         return carry
@@ -223,8 +240,8 @@
     place_ref, pattern_ref, shift_ref, turns_ref, out_ref, left_ref, right_ref, frob_ref, core_ref, row_grid_ref, col_own_ref, col_other_ref,
     *rest
 ):
-    payload, crossed, own_role, other_role = rest[0], rest[1], rest[2:9], rest[9:16]
-    scaled_ref, square_ref, left_all, right_all, acc_ref, col_grid_ref, sems = rest[16:]
+    payload, crossed, own_role, other_role, halves = rest[0], rest[1], rest[2:9], rest[9:16], rest[16:18]
+    scaled_ref, square_ref, left_all, right_all, acc_ref, col_grid_ref, sems = rest[18:]
     core = place_ref[0] % 2
 
     def part(whole, at, size, source, number):
@@ -237,16 +254,19 @@
     ]
     for copy in copies:
         copy.start()
+    along_x = {1: 0, 2: 2, 3: 1, 4: 3, 5: 5, 6: 6, 7: 4}
+    along_z = {1: 0, 2: 2, 3: 1, 4: 4, 5: 5, 7: 6}
+    low, others_high = halves
     for k in range(1, 8):
-        mine, others = own_role[k - 1], other_role[k - 1]
-        of_core_0 = [
-            part(left_all, k * CAP, CAP, others.at[pl.ds(CAP, CAP)], 1 + 2 * k),
-            part(right_all, 2 * k * CAP, 2 * CAP, mine, 2 + 2 * k),
-        ]
-        of_core_1 = [
-            part(left_all, k * CAP, CAP, mine.at[pl.ds(0, CAP)], 1 + 2 * k),
-            part(right_all, 2 * k * CAP, 2 * CAP, others, 2 + 2 * k),
-        ]
+        of_core_0 = [part(right_all, 2 * k * CAP, 2 * CAP, own_role[along_x[k]], 2 + 2 * k)]
+        of_core_1 = [part(right_all, 2 * k * CAP, 2 * CAP, other_role[along_x[k]], 2 + 2 * k)]
+        if k == 6:
+            of_core_0.append(part(left_all, k * CAP, CAP, others_high, 1 + 2 * k))
+            of_core_1.append(part(left_all, k * CAP, CAP, low, 1 + 2 * k))
+        else:
+            theirs, mine = other_role[along_z[k]], own_role[along_z[k]]
+            of_core_0.append(part(left_all, k * CAP, CAP, theirs.at[pl.ds(CAP, CAP)], 1 + 2 * k))
+            of_core_1.append(part(left_all, k * CAP, CAP, mine.at[pl.ds(0, CAP)], 1 + 2 * k))
         copies += of_core_0
 
         @pl.when(core == 0)
@@ -325,6 +345,7 @@
 VM = pl.BlockSpec(memory_space=pltpu.VMEM)
 SM = pl.BlockSpec(memory_space=pltpu.SMEM)
 ANY = pl.BlockSpec(memory_space=pl.ANY)
+HBM = pl.BlockSpec(memory_space=pltpu.HBM)
 
 
 def to_all(value, axis, count, groups=None):
@@ -354,7 +375,16 @@
 
 
 def across_y_again(value):
-    return move(value, lambda x, y, z, core: (x, y ^ 1 if core else y, z, core))
+    return move(value, lambda x, y, z, core: (x, y ^ 1, z, core) if core else (x + 1, y, z, core))
+
+
+def ring_of_core_1(value, off):
+    pairs = []
+    for k in range(128):
+        x, y, z, core = place_of(k)
+        if core == 1:
+            pairs.append((k, device_of(x, y, z - off, core)))
+    return lax.ppermute(value, ("row", "col"), pairs)
 
 
 def to_core(value):
@@ -401,17 +431,21 @@
     phi = pl.pallas_call(
         values_kernel,
         in_specs=[SM, VM, VM, VM],
-        out_specs=VM,
+        out_specs=HBM,
         out_shape=jax.ShapeDtypeStruct((8, 8, BS, 8 * BS), BF16),
-        scratch_shapes=[pltpu.VMEM((8, BS, BS), F32)],
-        compiler_params=params(4),
+        scratch_shapes=[
+            pltpu.VMEM((8, BS, BS), F32),
+            pltpu.VMEM((2, 8, BS, 8 * BS), BF16),
+            pltpu.SemaphoreType.DMA((2,)),
+        ],
+        compiler_params=params(49),
         cost_estimate=lasting(10),
         name="values",
     )(place, centres, exponents, extents)
-    half, phi, step, after, before = lax.optimization_barrier((half, phi, step, after, before))
-
+
+    half, phi = lax.optimization_barrier((half, phi))
     far = ring(after, 1)
-    other = across_y_again(step)
+    second = across_y_again(step)
     bricks = jnp.concatenate([half, to_core(half)])
 
     def grid_blocks(with_sum, *more):
@@ -421,30 +455,25 @@
             out_shape.append(jax.ShapeDtypeStruct((1, BS), F32))
         return pl.pallas_call(
             functools.partial(grid_kernel, with_sum),
-            in_specs=[SM, SM, SM, VM, VM] + extra,
+            in_specs=[SM, SM, SM, VM, HBM] + extra,
             out_specs=[VM] * len(out_shape),
             out_shape=out_shape,
-            compiler_params=params(8),
+            scratch_shapes=[pltpu.VMEM((4, 8, BS, 8 * BS), BF16), pltpu.SemaphoreType.DMA((4,))],
+            compiler_params=params(49),
             cost_estimate=lasting(5),
             name="grid_rows" if with_sum else "grid_cols",
         )(place, home, shift, bricks, phi, *more)
 
     row_grid, total = grid_blocks(True, core_matrix, squares)
-    after, before, far, other, row_grid, total, bricks = lax.optimization_barrier(
-        (after, before, far, other, row_grid, total, bricks)
+    crossings = [to_core(after), to_core(before)]
+    after, before, far, step, second, row_grid, total, bricks, *crossings = lax.optimization_barrier(
+        (after, before, far, step, second, row_grid, total, bricks, *crossings)
     )
 
-    other_after, other_before = ring(other, 1), ring(other, -1)
-    crossings = [to_core(after), to_core(far), to_core(before)]
+    third = ring(second, -1)
+    other_after = ring(jnp.where(row % 2 == 0, step, second), 1)
+    crossings += [to_core(far), to_core(step)]
     (col_grid,) = grid_blocks(False)
-    other_after, other_before, col_grid, total, bricks, *crossings = lax.optimization_barrier(
-        (other_after, other_before, col_grid, total, bricks, *crossings)
-    )
-
-    other_far = ring(other_before, -1)
-    crossings += [to_core(other), to_core(other_after), to_core(other_before)]
-    col_grid_crossed = to_core(col_grid)
-    frob = to_all(total, ("row", "col"), 128).reshape(128, BS)
     *listed, most = pl.pallas_call(
         plan_kernel,
         in_specs=[SM, VM],
@@ -463,19 +492,27 @@
         cost_estimate=lasting(9),
         name="plan",
     )(place, bricks)
-    other_far, col_grid_crossed, frob, *rest = lax.optimization_barrier(
-        (other_far, col_grid_crossed, frob, *crossings, *listed)
+    other_after, third, second, col_grid, total, *rest = lax.optimization_barrier(
+        (other_after, third, second, col_grid, total, *crossings, *listed)
     )
-    crossings, listed = rest[:6], rest[6:]
-
-    crossings.insert(5, to_core(other_far))
-    own_role = [after, far, before, other, other_after, other_far, other_before]
+    crossings, listed = rest[:4], rest[4:]
+
+    low, high = ring_of_core_1(third[:CAP], -1), ring_of_core_1(other_after[CAP:], 1)
+    crossings += [to_core(second), to_core(other_after), to_core(third)]
+    col_grid_crossed = to_core(col_grid)
+    frob = to_all(total, ("row", "col"), 128).reshape(128, BS)
+    low, high, col_grid_crossed, frob, *crossings = lax.optimization_barrier(
+        (low, high, col_grid_crossed, frob, *crossings)
+    )
+
+    halves = [low, to_core(high)]
+    own_role = [after, before, far, step, second, other_after, third]
     overflow = most[0] > CAP
 
     def sparse():
         return pl.pallas_call(
             product_kernel,
-            in_specs=[SM] * 7 + [VM] * 5 + [ANY] * 16,
+            in_specs=[SM] * 7 + [VM] * 5 + [ANY] * 18,
             out_specs=[VM, VM],
             out_shape=[jax.ShapeDtypeStruct((512, 1024), BF16)] * 2,
             scratch_shapes=[
@@ -483,12 +520,12 @@
                 pltpu.VMEM((16 * CAP, BS, BS), BF16),
                 pltpu.VMEM((33, BS, BS), F32),
                 pltpu.VMEM((8, BS, BS), BF16),
-                pltpu.SemaphoreType.DMA((17,)),
+                pltpu.SemaphoreType.DMA((18,)),
             ],
             compiler_params=params(24),
             cost_estimate=lasting(12),
             name="product",
-        )(place, pattern, shift, *listed, frob, core_matrix, row_grid, col_grid, col_grid_crossed, payload, crossed, *own_role, *crossings)
+        )(place, pattern, shift, *listed, frob, core_matrix, row_grid, col_grid, col_grid_crossed, payload, crossed, *own_role, *crossings, *halves)
 
     def dense():
         keep = pattern.astype(F32)[:, None, :, None]

time: 151 us -> 146 us (0.967)
  blocking collectives: 0 us -> 17.2 us
  local copies, waits for them, and re-layouts: 17.4 us -> 4.02 us
  starting transfers between devices: 46.2 us -> 36.3 us
  waiting for transfers between devices: 32.7 us -> 24.9 us
  Pallas kernels: 37.3 us -> 42.9 us
  other arithmetic: 0.19 us -> 4.03 us
    all_to_all x0 -> x1, blocking collectives: none -> 17.2 us  [to_all(): return lax.all_to_all(copies, axis, 0, 0, axis_index_groups=groups)]
    unnamed x35 -> x15, local copies, waits for them, and re-layouts: 15.3 us -> 1.14 us
    ppermute x10 -> x11, starting transfers between devices: 21.2 us -> 8.56 us  [to_core(): return lax.ppermute(value, 'row', [(k, k ^ 1) for k in range(16)])]
    all_to_all x2 -> x1, waiting for transfers between devices: 13.1 us -> 2.65 us  [to_all(): return lax.all_to_all(copies, axis, 0, 0, axis_index_groups=groups)]
    ppermute x0 -> x2, starting transfers between devices: none -> 6.98 us  [ring_of_core_1(): return lax.ppermute(value, ('row', 'col'), pairs)]
    ppermute x8 -> x7, waiting for transfers between devices: 15.7 us -> 19.4 us  [move(): lax.ppermute(value, ('row', 'col'), [(k, device_of(*where(*place_of(k))))...]
    pallas_call x2, Pallas kernels: 7.49 us -> 10.2 us  [grid_blocks(): pl.pallas_call(functools.partial(grid_kernel, with_sum), in_specs=[SM, SM...]
    ppermute x8 -> x7, starting transfers between devices: 11.7 us -> 9.38 us  [move(): lax.ppermute(value, ('row', 'col'), [(k, device_of(*where(*place_of(k))))...]
  transfers between devices with their start and end apart: 20 -> 21, of which waited for: 7 -> 8; matrix products, arithmetic and copies ran while one was open for 2% -> 5% of each run, Pallas kernels for 16% -> 20%
where the time goes in v5:
time: 146 us; the launch traced here: 145 us
  Pallas kernels  42.9 us (29%)
  starting transfers between devices  36.3 us (25%)
  waiting for transfers between devices  24.9 us (17%)
  blocking collectives  17.2 us (12%)
  between operations  15.5 us (11%)
  other arithmetic  4.03 us (3%)
  local copies, waits for them, and re-layouts  4.02 us (3%)
    ppermute x7, waiting for transfers between devices, move(): lax.ppermute(value, ('row', 'col'), [(k, device_of(*where(*place_of(k))))...  19.4 us
    all_to_all x1, blocking collectives, to_all(): return lax.all_to_all(copies, axis, 0, 0, axis_index_groups=groups)  17.2 us
    all_to_all x1, starting transfers between devices, to_all(): return lax.all_to_all(copies, axis, 0, 0, axis_index_groups=groups)  11.4 us
    pallas_call x1, Pallas kernels, sparse(): pl.pallas_call(product_kernel, in_specs=[SM] * 7 + [VM] * 5 + [ANY] * 18,...  10.8 us
    pallas_call x1, Pallas kernels, body(): pl.pallas_call(values_kernel, in_specs=[SM, VM, VM, VM], out_specs=HBM, o...  10.2 us
    pallas_call x2, Pallas kernels, grid_blocks(): pl.pallas_call(functools.partial(grid_kernel, with_sum), in_specs=[SM, SM...  10.2 us
    ppermute x7, starting transfers between devices, move(): lax.ppermute(value, ('row', 'col'), [(k, device_of(*where(*place_of(k))))...  9.38 us
    ppermute x11, starting transfers between devices, to_core(): return lax.ppermute(value, 'row', [(k, k ^ 1) for k in range(16)])  8.56 us
  transfers between devices with their start and end apart: 21, of which 8 were waited for; matrix products, arithmetic and copies ran while one was open for 5% of the time, Pallas kernels for 20%

profile of v5, /device:TPU:1, one launch (start us, length us, event | category | flops | bytes accessed | tf_op | source)
XLA Modules:
  0.0 144.8 jit_solution(17084540917101710709)
XLA Ops:
  9.2 2.4 %pack.1 = (bf16[2560,128]{1,0:T(8,128)(2,1)}, f32[8,128]{1,0:T(8,128)S(1)}) custom-call(s32[4,8]{1,0:T(4,128)S(1)} %copy-done.6, s32[2]{0:T(128)S(1)} %pad_add_fusion.place_ref, bf16[512,1024]{1,0:T(8,128)(2,1)S(1)} %copy-done.5), custom_call_target="tpu_custom_call" | custom-call | flops 2000000000 | bytes 1048576 | tf_op jit(solution)/shard_map/pack/pallas_call | solution.py:416
  14.2 11.4 %all-to-all-start = ((bf16[64,80,128]{2,1,0:T(8,128)(2,1)}), bf16[64,80,128]{2,1,0:T(8,128)(2,1)S(1)}, u32[]{:S(2)}, u32[]{:S(2)}) async-start(bf16[64,80,128]{2,1,0:T(8,128)(2,1)} %broadcast_in_dim.6), calls=%async_computation | async-start | bytes 2621440 | tf_op jit(solution)/shard_map/all_to_all | solution.py:353
  25.6 2.5 %pad_maximum_fusion = bf16[40,128,128]{2,1,0:T(8,128)(2,1)} fusion(bf16[20,128,128]{2,1,0:T(8,128)(2,1)} %collective-permute-done, bf16[20,128,128]{2,1,0:T(8,128)(2,1)} %bitcast.4), kind=kLoop, calls=%fused_computation.13 | loop fusion | flops 655360 | bytes 2621440 | tf_op jit(solution)/shard_map/concatenate | solution.py:428
  28.1 2.3 %collective-permute-start.4 = (bf16[40,128,128]{2,1,0:T(8,128)(2,1)}, bf16[40,128,128]{2,1,0:T(8,128)(2,1)}, u32[]{:S(2)}, u32[]{:S(2)}) collective-permute-start(bf16[40,128,128]{2,1,0:T(8,128)(2,1)} %pad_maximum_fusion), channel_id=1, source_target_pairs={{0,64},{1,65},{2,66},{3,67},{4,68},{5,69},{6,70},{7,71},{8,73},{9,... | collective-permute-start | bytes 3932168 | tf_op jit(solution)/shard_map/ppermute | solution.py:366
  31.6 1.5 %collective-permute-start.1 = (bf16[40,128,128]{2,1,0:T(8,128)(2,1)}, bf16[40,128,128]{2,1,0:T(8,128)(2,1)}, u32[]{:S(2)}, u32[]{:S(2)}) collective-permute-start(bf16[40,128,128]{2,1,0:T(8,128)(2,1)} %pad_maximum_fusion), channel_id=1, source_target_pairs={{0,48},{1,49},{2,50},{3,51},{4,52},{5,53},{6,54},{7,55},{8,14},{9,... | collective-permute-start | bytes 3932168 | tf_op jit(solution)/shard_map/ppermute | solution.py:366
  33.1 10.2 %values.1.phi_ref = bf16[8,8,128,1024]{3,2,1,0:T(8,128)(2,1)} custom-call(s32[2]{0:T(128)S(1)} %pad_add_fusion.place_ref, s32[3,64,128]{2,1,0:T(8,128)S(1)} %copy-done.1, f32[64,128]{1,0:T(8,128)S(1)} %copy-done.3, s32[64,128]{1,0:T(8,128)S(1)} %copy-done.4), custom_call_target="tpu_custom_call" | custom-call | flops 10000000000 | bytes 1048576 | tf_op jit(solution)/shard_map/values/pallas_call | solution.py:431
  43.3 2.6 %all-to-all-done = bf16[64,80,128]{2,1,0:T(8,128)(2,1)S(1)} async-done(((bf16[64,80,128]{2,1,0:T(8,128)(2,1)}), bf16[64,80,128]{2,1,0:T(8,128)(2,1)S(1)}, u32[]{:S(2)}, u32[]{:S(2)}) %all-to-all-start) | async-done | bytes 1310752 | tf_op jit(solution)/shard_map/all_to_all | solution.py:353
  46.0 1.9 %collective-permute-start.6 = (bf16[64,80,128]{2,1,0:T(8,128)(2,1)S(1)}, bf16[64,80,128]{2,1,0:T(8,128)(2,1)}, u32[]{:S(2)}, u32[]{:S(2)}) collective-permute-start(bf16[64,80,128]{2,1,0:T(8,128)(2,1)S(1)} %all-to-all-done), channel_id=1, source_target_pairs={{0,8},{8,0},{16,24},{24,16},{32,40},{40,32},{48,56},{56,48},{64,72... | collective-permute-start | bytes 3932168 | tf_op jit(solution)/shard_map/ppermute | solution.py:391
  47.9 9.3 %collective-permute-done.4 = bf16[40,128,128]{2,1,0:T(8,128)(2,1)} collective-permute-done((bf16[40,128,128]{2,1,0:T(8,128)(2,1)}, bf16[40,128,128]{2,1,0:T(8,128)(2,1)}, u32[]{:S(2)}, u32[]{:S(2)}) %collective-permute-start.4) | collective-permute-done | bytes 1310752 | tf_op jit(solution)/shard_map/ppermute | solution.py:366
  58.8 1.6 %collective-permute-start.3 = (bf16[40,128,128]{2,1,0:T(8,128)(2,1)}, bf16[40,128,128]{2,1,0:T(8,128)(2,1)}, u32[]{:S(2)}, u32[]{:S(2)}) collective-permute-start(bf16[40,128,128]{2,1,0:T(8,128)(2,1)} %collective-permute-done.1), channel_id=1, source_target_pairs={{0,48},{1,49},{2,50},{3,51},{4,52},{5,53},{6,54},{7,55},{8,14},{9,... | collective-permute-start | bytes 3932168 | tf_op jit(solution)/shard_map/ppermute | solution.py:366
  61.2 1.5 %constant_dynamic-update-slice_fusion.bricks_ref = bf16[128,80,128]{2,1,0:T(8,128)(2,1)S(1)} fusion(bf16[128,80,128]{2,1,0:T(8,128)(2,1)S(1)} %constant_dynamic-update-slice_fusion.1, bf16[64,80,128]{2,1,0:T(8,128)(2,1)} %collective-permute-done.6), kind=kLoop, calls=%fused_computation.15 | loop fusion | bytes 2621440 | tf_op jit(solution)/shard_map/concatenate | solution.py:449
  62.7 5.1 %grid_rows.1 = (bf16[4,128,128]{2,1,0:T(8,128)(2,1)S(1)}, f32[1,128]{1,0:T(1,128)S(1)}) custom-call(s32[2]{0:T(128)S(1)} %pad_add_fusion.place_ref, s32[64]{0:T(128)S(1)} %copy-done, f32[1]{0:T(128)S(6)} %copy.24.shift_ref, bf16[128,80,128]{2,1,0:T(8,128)(2,1)S(1)} %constant_dynamic-update-slice_fusion.bricks_ref, bf16[8,8,128,1024]{3,2,1,0:T(8,128)(2,1)} %values.1.phi_ref, ...), custom_call_target="tpu_custom_call" | custom-call | flops 5000000000 | bytes 1048576 | tf_op jit(solution)/shard_map/grid_rows/pallas_call | solution.py:456
  67.8 6.4 %collective-permute-done.5 = bf16[40,128,128]{2,1,0:T(8,128)(2,1)} collective-permute-done((bf16[40,128,128]{2,1,0:T(8,128)(2,1)}, bf16[40,128,128]{2,1,0:T(8,128)(2,1)}, u32[]{:S(2)}, u32[]{:S(2)}) %collective-permute-start.5) | collective-permute-done | bytes 1310752 | tf_op jit(solution)/shard_map/ppermute | solution.py:366
  74.2 1.6 %collective-permute-done.3 = bf16[40,128,128]{2,1,0:T(8,128)(2,1)} collective-permute-done((bf16[40,128,128]{2,1,0:T(8,128)(2,1)}, bf16[40,128,128]{2,1,0:T(8,128)(2,1)}, u32[]{:S(2)}, u32[]{:S(2)}) %collective-permute-start.3) | collective-permute-done | bytes 1310752 | tf_op jit(solution)/shard_map/ppermute | solution.py:366
  78.1 1.5 %broadcast_select_fusion = bf16[40,128,128]{2,1,0:T(8,128)(2,1)S(1)} fusion(bf16[40,128,128]{2,1,0:T(8,128)(2,1)} %collective-permute-done.4, bf16[40,128,128]{2,1,0:T(8,128)(2,1)} %collective-permute-done.5, pred[]{:T(512)S(6)} %eq.29), kind=kLoop, calls=%fused_computation.14 | loop fusion | flops 655360 | bytes 3932161 | tf_op jit(solution)/shard_map/jit(_where)/select_n | solution.py:474
  79.6 1.5 %collective-permute-start.9 = (bf16[40,128,128]{2,1,0:T(8,128)(2,1)S(1)}, bf16[40,128,128]{2,1,0:T(8,128)(2,1)S(1)}, u32[]{:S(2)}, u32[]{:S(2)}) collective-permute-start(bf16[40,128,128]{2,1,0:T(8,128)(2,1)S(1)} %broadcast_select_fusion), channel_id=1, source_target_pairs={{0,48},{1,49},{2,50},{3,51},{4,52},{5,53},{6,54},{7,55},{8,14},{9,... | collective-permute-start | bytes 3932168 | tf_op jit(solution)/shard_map/ppermute | solution.py:366
  82.1 5.1 %grid_cols.1 = bf16[4,128,128]{2,1,0:T(8,128)(2,1)S(1)} custom-call(s32[2]{0:T(128)S(1)} %pad_add_fusion.place_ref, s32[64]{0:T(128)S(1)} %copy-done, f32[1]{0:T(128)S(6)} %copy.24.shift_ref, bf16[128,80,128]{2,1,0:T(8,128)(2,1)S(1)} %constant_dynamic-update-slice_fusion.bricks_ref, bf16[8,8,128,1024]{3,2,1,0:T(8,128)(2,1)} %values.1.phi_ref), custom_call_target="tpu_custom_call" | custom-call | flops 5000000000 | bytes 1048576 | tf_op jit(solution)/shard_map/grid_cols/pallas_call | solution.py:456
  87.2 8.4 %plan.1 = (s32[1]{0:T(128)}, s32[548]{0:T(1024)S(1)}, s32[2192]{0:T(1024)S(1)}, s32[2192]{0:T(1024)S(1)}, s32[1]{0:T(128)}) custom-call(s32[2]{0:T(128)S(1)} %pad_add_fusion.place_ref, bf16[128,80,128]{2,1,0:T(8,128)(2,1)S(1)} %constant_dynamic-update-slice_fusion.bricks_ref), custom_call_target="tpu_custom_call" | custom-call | flops 8999999488 | bytes 1048576 | tf_op jit(solution)/shard_map/plan/pallas_call | solution.py:477
  98.2 4.0 %collective-permute-start.14 = (bf16[20,128,128]{2,1,0:T(8,128)(2,1)S(1)}, bf16[20,128,128]{2,1,0:T(8,128)(2,1)S(1)}, u32[]{:S(2)}, u32[]{:S(2)}) collective-permute-start(bf16[20,128,128]{2,1,0:T(8,128)(2,1)S(1)} %slice.7), channel_id=1, source_target_pairs={{8,14},{9,15},{10,8},{11,9},{12,10},{13,11},{14,12},{15,13},{24,30... | collective-permute-start | bytes 1966088 | tf_op jit(solution)/shard_map/ppermute | solution.py:387
  102.3 1.8 %collective-permute-done.15 = bf16[4,128,128]{2,1,0:T(8,128)(2,1)S(1)} collective-permute-done((bf16[4,128,128]{2,1,0:T(8,128)(2,1)S(1)}, bf16[4,128,128]{2,1,0:T(8,128)(2,1)S(1)}, u32[]{:S(2)}, u32[]{:S(2)}) %collective-permute-start.15) | collective-permute-done | bytes 131104 | tf_op jit(solution)/shard_map/ppermute | solution.py:391
  104.1 3.0 %collective-permute-start.13 = (bf16[20,128,128]{2,1,0:T(8,128)(2,1)S(1)}, bf16[20,128,128]{2,1,0:T(8,128)(2,1)S(1)}, u32[]{:S(2)}, u32[]{:S(2)}) collective-permute-start(bf16[20,128,128]{2,1,0:T(8,128)(2,1)S(1)} %slice.6), channel_id=1, source_target_pairs={{8,10},{9,11},{10,12},{11,13},{12,14},{13,15},{14,8},{15,9},{24,26... | collective-permute-start | bytes 1966088 | tf_op jit(solution)/shard_map/ppermute | solution.py:387
  107.1 17.2 %all_to_all.10 = f32[128,1,128]{2,1,0:T(1,128)S(1)} all-to-all(f32[128,1,128]{2,1,0:T(1,128)S(1)} %broadcast_in_dim.8), channel_id=1, replica_groups=mesh['row'=16,'col'=8] {'row','col'}, dimensions={0} | all-to-all | bytes 131072 | tf_op jit(solution)/shard_map/all_to_all | solution.py:353
  127.2 10.8 %conditional.1 = ((bf16[512,1024]{1,0:T(8,128)(2,1)}, bf16[512,1024]{1,0:T(8,128)(2,1)})) conditional(s32[]{:T(128)} %bitcast.5, (s32[2]{0:T(128)S(1)}, s32[4,8]{1,0:T(4,128)S(1)}, f32[1]{0:T(128)}, s32[1]{0:T(128)}, s32[548]{0:T(1024)S(1)}, /*index=5*/s32[2192]{0:T(1024)S(1)}, s32[2192]{0:T(1024)S(1)}, f32[128,128]{1,0:T(8,128)S(1)}, ...), branch_computations={%region_0.1_spmd, %region_1.3_spmd} | conditional | flops 12000000000 | bytes 121439128 | solution.py:547
  127.2 10.8 %product.1 = (bf16[512,1024]{1,0:T(8,128)(2,1)}, bf16[512,1024]{1,0:T(8,128)(2,1)}) custom-call(s32[2]{0:T(128)S(1)} %get-tuple-element.74.place_ref, s32[4,8]{1,0:T(4,128)S(1)} %get-tuple-element.75.pattern_ref, f32[1]{0:T(128)} %get-tuple-element.76.shift_ref, s32[1]{0:T(128)} %get-tuple-element.77.turns_ref, s32[548]{0:T(1024)S(1)} %get-tuple-element.78.out_ref, ...), custom_call_target="tpu_custom_call" | custom-call | flops 12000000000 | bytes 1048576 | tf_op jit(solution)/shard_map/cond/branch_0_fun/product/pallas_call | solution.py:513
  (50 shorter events, 15.8 us)
Async XLA Ops:
  11.6 14.0 %collective-permute-start = (bf16[20,128,128]{2,1,0:T(8,128)(2,1)}, bf16[20,128,128]{2,1,0:T(8,128)(2,1)}, u32[]{:S(2)}, u32[]{:S(2)}) collective-permute-start(bf16[20,128,128]{2,1,0:T(8,128)(2,1)} %bitcast.4), channel_id=1, source_target_pairs={{0,8},{8,0},{16,24},{24,16},{32,40},{40,32},{48,56},{56,48},{64,72... | collective-permute-start | bytes 1966088 | tf_op jit(solution)/shard_map/ppermute | solution.py:391
  14.2 18.9 %copy-start.1 = (s32[3,64,128]{2,1,0:T(8,128)S(1)}, s32[3,64,128]{2,1,0:T(8,128)}, u32[]{:S(2)}) copy-start(s32[3,64,128]{2,1,0:T(8,128)} %centres_ref.1) | copy-start | bytes 294916
  14.2 18.9 %copy-start.3 = (f32[64,128]{1,0:T(8,128)S(1)}, f32[64,128]{1,0:T(8,128)}, u32[]{:S(2)}) copy-start(f32[64,128]{1,0:T(8,128)} %exponents_ref.1) | copy-start | bytes 98308
  14.2 18.9 %copy-start.4 = (s32[64,128]{1,0:T(8,128)S(1)}, s32[64,128]{1,0:T(8,128)}, u32[]{:S(2)}) copy-start(s32[64,128]{1,0:T(8,128)} %extents_ref.1) | copy-start | bytes 98308
  14.2 31.8 %all-to-all-start = ((bf16[64,80,128]{2,1,0:T(8,128)(2,1)}), bf16[64,80,128]{2,1,0:T(8,128)(2,1)S(1)}, u32[]{:S(2)}, u32[]{:S(2)}) async-start(bf16[64,80,128]{2,1,0:T(8,128)(2,1)} %broadcast_in_dim.6), calls=%async_computation | async-start | bytes 2621440 | tf_op jit(solution)/shard_map/all_to_all | solution.py:353
  28.1 29.1 %collective-permute-start.4 = (bf16[40,128,128]{2,1,0:T(8,128)(2,1)}, bf16[40,128,128]{2,1,0:T(8,128)(2,1)}, u32[]{:S(2)}, u32[]{:S(2)}) collective-permute-start(bf16[40,128,128]{2,1,0:T(8,128)(2,1)} %pad_maximum_fusion), channel_id=1, source_target_pairs={{0,64},{1,65},{2,66},{3,67},{4,68},{5,69},{6,70},{7,71},{8,73},{9,... | collective-permute-start | bytes 3932168 | tf_op jit(solution)/shard_map/ppermute | solution.py:366
  30.4 27.9 %collective-permute-start.2 = (bf16[40,128,128]{2,1,0:T(8,128)(2,1)}, bf16[40,128,128]{2,1,0:T(8,128)(2,1)}, u32[]{:S(2)}, u32[]{:S(2)}) collective-permute-start(bf16[40,128,128]{2,1,0:T(8,128)(2,1)} %pad_maximum_fusion), channel_id=1, source_target_pairs={{0,16},{1,17},{2,18},{3,19},{4,20},{5,21},{6,22},{7,23},{8,10},{9,... | collective-permute-start | bytes 3932168 | tf_op jit(solution)/shard_map/ppermute | solution.py:366
  31.6 26.7 %collective-permute-start.1 = (bf16[40,128,128]{2,1,0:T(8,128)(2,1)}, bf16[40,128,128]{2,1,0:T(8,128)(2,1)}, u32[]{:S(2)}, u32[]{:S(2)}) collective-permute-start(bf16[40,128,128]{2,1,0:T(8,128)(2,1)} %pad_maximum_fusion), channel_id=1, source_target_pairs={{0,48},{1,49},{2,50},{3,51},{4,52},{5,53},{6,54},{7,55},{8,14},{9,... | collective-permute-start | bytes 3932168 | tf_op jit(solution)/shard_map/ppermute | solution.py:366
  46.0 15.2 %collective-permute-start.6 = (bf16[64,80,128]{2,1,0:T(8,128)(2,1)S(1)}, bf16[64,80,128]{2,1,0:T(8,128)(2,1)}, u32[]{:S(2)}, u32[]{:S(2)}) collective-permute-start(bf16[64,80,128]{2,1,0:T(8,128)(2,1)S(1)} %all-to-all-done), channel_id=1, source_target_pairs={{0,8},{8,0},{16,24},{24,16},{32,40},{40,32},{48,56},{56,48},{64,72... | collective-permute-start | bytes 3932168 | tf_op jit(solution)/shard_map/ppermute | solution.py:391
  57.1 17.1 %collective-permute-start.5 = (bf16[40,128,128]{2,1,0:T(8,128)(2,1)}, bf16[40,128,128]{2,1,0:T(8,128)(2,1)}, u32[]{:S(2)}, u32[]{:S(2)}) collective-permute-start(bf16[40,128,128]{2,1,0:T(8,128)(2,1)} %collective-permute-done.4), channel_id=1, source_target_pairs={{0,16},{1,17},{2,18},{3,19},{4,20},{5,21},{6,22},{7,23},{8,72},{9,... | collective-permute-start | bytes 3932168 | tf_op jit(solution)/shard_map/ppermute | solution.py:366
  58.3 15.9 %collective-permute-start.8 = (bf16[40,128,128]{2,1,0:T(8,128)(2,1)}, bf16[40,128,128]{2,1,0:T(8,128)(2,1)}, u32[]{:S(2)}, u32[]{:S(2)}) collective-permute-start(bf16[40,128,128]{2,1,0:T(8,128)(2,1)} %collective-permute-done.2), channel_id=1, source_target_pairs={{0,8},{8,0},{16,24},{24,16},{32,40},{40,32},{48,56},{56,48},{64,72... | collective-permute-start | bytes 3932168 | tf_op jit(solution)/shard_map/ppermute | solution.py:391
  58.3 15.9 %collective-permute-start.7 = (bf16[40,128,128]{2,1,0:T(8,128)(2,1)}, bf16[40,128,128]{2,1,0:T(8,128)(2,1)}, u32[]{:S(2)}, u32[]{:S(2)}) collective-permute-start(bf16[40,128,128]{2,1,0:T(8,128)(2,1)} %collective-permute-done.1), channel_id=1, source_target_pairs={{0,8},{8,0},{16,24},{24,16},{32,40},{40,32},{48,56},{56,48},{64,72... | collective-permute-start | bytes 3932168 | tf_op jit(solution)/shard_map/ppermute | solution.py:391
  58.8 17.1 %collective-permute-start.3 = (bf16[40,128,128]{2,1,0:T(8,128)(2,1)}, bf16[40,128,128]{2,1,0:T(8,128)(2,1)}, u32[]{:S(2)}, u32[]{:S(2)}) collective-permute-start(bf16[40,128,128]{2,1,0:T(8,128)(2,1)} %collective-permute-done.1), channel_id=1, source_target_pairs={{0,48},{1,49},{2,50},{3,51},{4,52},{5,53},{6,54},{7,55},{8,14},{9,... | collective-permute-start | bytes 3932168 | tf_op jit(solution)/shard_map/ppermute | solution.py:366
  75.9 20.6 %collective-permute-start.12 = (bf16[40,128,128]{2,1,0:T(8,128)(2,1)}, bf16[40,128,128]{2,1,0:T(8,128)(2,1)S(1)}, u32[]{:S(2)}, u32[]{:S(2)}) collective-permute-start(bf16[40,128,128]{2,1,0:T(8,128)(2,1)} %collective-permute-done.4), channel_id=1, source_target_pairs={{0,8},{8,0},{16,24},{24,16},{32,40},{40,32},{48,56},{56,48},{64,72... | collective-permute-start | bytes 3932168 | tf_op jit(solution)/shard_map/ppermute | solution.py:391
  76.9 19.6 %collective-permute-start.10 = (bf16[40,128,128]{2,1,0:T(8,128)(2,1)}, bf16[40,128,128]{2,1,0:T(8,128)(2,1)S(1)}, u32[]{:S(2)}, u32[]{:S(2)}) collective-permute-start(bf16[40,128,128]{2,1,0:T(8,128)(2,1)} %collective-permute-done.5), channel_id=1, source_target_pairs={{0,16},{1,17},{2,18},{3,19},{4,20},{5,21},{6,22},{7,23},{8,10},{9,... | collective-permute-start | bytes 3932168 | tf_op jit(solution)/shard_map/ppermute | solution.py:366
  79.6 16.8 %collective-permute-start.9 = (bf16[40,128,128]{2,1,0:T(8,128)(2,1)S(1)}, bf16[40,128,128]{2,1,0:T(8,128)(2,1)S(1)}, u32[]{:S(2)}, u32[]{:S(2)}) collective-permute-start(bf16[40,128,128]{2,1,0:T(8,128)(2,1)S(1)} %broadcast_select_fusion), channel_id=1, source_target_pairs={{0,48},{1,49},{2,50},{3,51},{4,52},{5,53},{6,54},{7,55},{8,14},{9,... | collective-permute-start | bytes 3932168 | tf_op jit(solution)/shard_map/ppermute | solution.py:366
  81.1 15.4 %collective-permute-start.11 = (bf16[40,128,128]{2,1,0:T(8,128)(2,1)}, bf16[40,128,128]{2,1,0:T(8,128)(2,1)S(1)}, u32[]{:S(2)}, u32[]{:S(2)}) collective-permute-start(bf16[40,128,128]{2,1,0:T(8,128)(2,1)} %collective-permute-done.3), channel_id=1, source_target_pairs={{0,8},{8,0},{16,24},{24,16},{32,40},{40,32},{48,56},{56,48},{64,72... | collective-permute-start | bytes 3932168 | tf_op jit(solution)/shard_map/ppermute | solution.py:391
  96.5 27.8 %collective-permute-start.16 = (bf16[40,128,128]{2,1,0:T(8,128)(2,1)}, bf16[40,128,128]{2,1,0:T(8,128)(2,1)S(1)}, u32[]{:S(2)}, u32[]{:S(2)}) collective-permute-start(bf16[40,128,128]{2,1,0:T(8,128)(2,1)} %collective-permute-done.5), channel_id=1, source_target_pairs={{0,8},{8,0},{16,24},{24,16},{32,40},{40,32},{48,56},{56,48},{64,72... | collective-permute-start | bytes 3932168 | tf_op jit(solution)/shard_map/ppermute | solution.py:391
  97.5 26.8 %collective-permute-start.18 = (bf16[40,128,128]{2,1,0:T(8,128)(2,1)S(1)}, bf16[40,128,128]{2,1,0:T(8,128)(2,1)S(1)}, u32[]{:S(2)}, u32[]{:S(2)}) collective-permute-start(bf16[40,128,128]{2,1,0:T(8,128)(2,1)S(1)} %collective-permute-done.10), channel_id=1, source_target_pairs={{0,8},{8,0},{16,24},{24,16},{32,40},{40,32},{48,56},{56,48},{64,72... | collective-permute-start | bytes 3932168 | tf_op jit(solution)/shard_map/ppermute | solution.py:391
  97.6 26.7 %collective-permute-start.17 = (bf16[40,128,128]{2,1,0:T(8,128)(2,1)S(1)}, bf16[40,128,128]{2,1,0:T(8,128)(2,1)S(1)}, u32[]{:S(2)}, u32[]{:S(2)}) collective-permute-start(bf16[40,128,128]{2,1,0:T(8,128)(2,1)S(1)} %collective-permute-done.9), channel_id=1, source_target_pairs={{0,8},{8,0},{16,24},{24,16},{32,40},{40,32},{48,56},{56,48},{64,72... | collective-permute-start | bytes 3932168 | tf_op jit(solution)/shard_map/ppermute | solution.py:391
  98.0 6.1 %collective-permute-start.15 = (bf16[4,128,128]{2,1,0:T(8,128)(2,1)S(1)}, bf16[4,128,128]{2,1,0:T(8,128)(2,1)S(1)}, u32[]{:S(2)}, u32[]{:S(2)}) collective-permute-start(bf16[4,128,128]{2,1,0:T(8,128)(2,1)S(1)} %grid_cols.1), channel_id=1, source_target_pairs={{0,8},{8,0},{16,24},{24,16},{32,40},{40,32},{48,56},{56,48},{64,72... | collective-permute-start | bytes 393224 | tf_op jit(solution)/shard_map/ppermute | solution.py:391
  98.2 26.1 %collective-permute-start.14 = (bf16[20,128,128]{2,1,0:T(8,128)(2,1)S(1)}, bf16[20,128,128]{2,1,0:T(8,128)(2,1)S(1)}, u32[]{:S(2)}, u32[]{:S(2)}) collective-permute-start(bf16[20,128,128]{2,1,0:T(8,128)(2,1)S(1)} %slice.7), channel_id=1, source_target_pairs={{8,14},{9,15},{10,8},{11,9},{12,10},{13,11},{14,12},{15,13},{24,30... | collective-permute-start | bytes 1966088 | tf_op jit(solution)/shard_map/ppermute | solution.py:387
  104.1 20.2 %collective-permute-start.13 = (bf16[20,128,128]{2,1,0:T(8,128)(2,1)S(1)}, bf16[20,128,128]{2,1,0:T(8,128)(2,1)S(1)}, u32[]{:S(2)}, u32[]{:S(2)}) collective-permute-start(bf16[20,128,128]{2,1,0:T(8,128)(2,1)S(1)} %slice.6), channel_id=1, source_target_pairs={{8,10},{9,11},{10,12},{11,13},{12,14},{13,15},{14,8},{15,9},{24,26... | collective-permute-start | bytes 1966088 | tf_op jit(solution)/shard_map/ppermute | solution.py:387
  124.3 2.9 %collective-permute-start.19 = (bf16[20,128,128]{2,1,0:T(8,128)(2,1)S(1)}, bf16[20,128,128]{2,1,0:T(8,128)(2,1)S(1)}, u32[]{:S(2)}, u32[]{:S(2)}) collective-permute-start(bf16[20,128,128]{2,1,0:T(8,128)(2,1)S(1)} %collective-permute-done.14), channel_id=1, source_target_pairs={{0,8},{8,0},{16,24},{24,16},{32,40},{40,32},{48,56},{56,48},{64,72... | collective-permute-start | bytes 1966088 | tf_op jit(solution)/shard_map/ppermute | solution.py:391
  (4 other events, 5.3 us)

commit v6 on v5

--- a/solution.py
+++ b/solution.py
@@ -256,12 +256,12 @@
         copy.start()
     along_x = {1: 0, 2: 2, 3: 1, 4: 3, 5: 5, 6: 6, 7: 4}
     along_z = {1: 0, 2: 2, 3: 1, 4: 4, 5: 5, 7: 6}
-    low, others_high = halves
+    low, high = halves
     for k in range(1, 8):
         of_core_0 = [part(right_all, 2 * k * CAP, 2 * CAP, own_role[along_x[k]], 2 + 2 * k)]
         of_core_1 = [part(right_all, 2 * k * CAP, 2 * CAP, other_role[along_x[k]], 2 + 2 * k)]
         if k == 6:
-            of_core_0.append(part(left_all, k * CAP, CAP, others_high, 1 + 2 * k))
+            of_core_0.append(part(left_all, k * CAP, CAP, high, 1 + 2 * k))
             of_core_1.append(part(left_all, k * CAP, CAP, low, 1 + 2 * k))
         else:
             theirs, mine = other_role[along_z[k]], own_role[along_z[k]]
@@ -378,11 +378,11 @@
     return move(value, lambda x, y, z, core: (x, y ^ 1, z, core) if core else (x + 1, y, z, core))
 
 
-def ring_of_core_1(value, off):
+def from_core_1(value, off, core):
     pairs = []
     for k in range(128):
-        x, y, z, core = place_of(k)
-        if core == 1:
+        x, y, z, source = place_of(k)
+        if source == 1:
             pairs.append((k, device_of(x, y, z - off, core)))
     return lax.ppermute(value, ("row", "col"), pairs)
 
@@ -443,7 +443,8 @@
         name="values",
     )(place, centres, exponents, extents)
 
-    half, phi = lax.optimization_barrier((half, phi))
+    half, phi, step, after, before = lax.optimization_barrier((half, phi, step, after, before))
+
     far = ring(after, 1)
     second = across_y_again(step)
     bricks = jnp.concatenate([half, to_core(half)])
@@ -466,13 +467,14 @@
 
     row_grid, total = grid_blocks(True, core_matrix, squares)
     crossings = [to_core(after), to_core(before)]
-    after, before, far, step, second, row_grid, total, bricks, *crossings = lax.optimization_barrier(
-        (after, before, far, step, second, row_grid, total, bricks, *crossings)
+    frob = to_all(total, ("row", "col"), 128).reshape(128, BS)
+    after, before, far, step, second, row_grid, frob, bricks, *crossings = lax.optimization_barrier(
+        (after, before, far, step, second, row_grid, frob, bricks, *crossings)
     )
 
     third = ring(second, -1)
     other_after = ring(jnp.where(row % 2 == 0, step, second), 1)
-    crossings += [to_core(far), to_core(step)]
+    crossings += [to_core(far), to_core(step), to_core(second)]
     (col_grid,) = grid_blocks(False)
     *listed, most = pl.pallas_call(
         plan_kernel,
@@ -492,20 +494,17 @@
         cost_estimate=lasting(9),
         name="plan",
     )(place, bricks)
-    other_after, third, second, col_grid, total, *rest = lax.optimization_barrier(
-        (other_after, third, second, col_grid, total, *crossings, *listed)
+    other_after, third, col_grid, *rest = lax.optimization_barrier(
+        (other_after, third, col_grid, *crossings, *listed)
     )
-    crossings, listed = rest[:4], rest[4:]
-
-    low, high = ring_of_core_1(third[:CAP], -1), ring_of_core_1(other_after[CAP:], 1)
-    crossings += [to_core(second), to_core(other_after), to_core(third)]
+    crossings, listed = rest[:5], rest[5:]
+
+    low, high = from_core_1(third[:CAP], -1, 1), from_core_1(other_after[CAP:], 1, 0)
+    crossings += [to_core(other_after), to_core(third)]
     col_grid_crossed = to_core(col_grid)
-    frob = to_all(total, ("row", "col"), 128).reshape(128, BS)
-    low, high, col_grid_crossed, frob, *crossings = lax.optimization_barrier(
-        (low, high, col_grid_crossed, frob, *crossings)
-    )
-
-    halves = [low, to_core(high)]
+    low, high, col_grid_crossed, *crossings = lax.optimization_barrier((low, high, col_grid_crossed, *crossings))
+
+    halves = [low, high]
     own_role = [after, before, far, step, second, other_after, third]
     overflow = most[0] > CAP
 

time: 146 us -> 137 us (0.938)
  blocking collectives: 17.2 us -> 0 us
  waiting for transfers between devices: 24.9 us -> 34 us
  starting transfers between devices: 36.3 us -> 38.8 us
  other arithmetic: 4.03 us -> 1.67 us
  Pallas kernels: 42.9 us -> 41.3 us
    all_to_all x1 -> x0, blocking collectives: 17.2 us -> none  [to_all(): return lax.all_to_all(copies, axis, 0, 0, axis_index_groups=groups)]
    ppermute x7, waiting for transfers between devices: 19.4 us -> 3.66 us  [move(): lax.ppermute(value, ('row', 'col'), [(k, device_of(*where(*place_of(k))))...]
    all_to_all x1 -> x2, waiting for transfers between devices: 2.65 us -> 18.3 us  [to_all(): return lax.all_to_all(copies, axis, 0, 0, axis_index_groups=groups)]
    ppermute x2, waiting for transfers between devices: 0.01 us -> 9.18 us  [from_core_1(): return lax.ppermute(value, ('row', 'col'), pairs)]
    concatenate x1, other arithmetic: 2.47 us -> 0.11 us  [body(): pair = jnp.concatenate([payload, crossed])]
    ppermute x11 -> x10, starting transfers between devices: 8.56 us -> 10.6 us  [to_core(): return lax.ppermute(value, 'row', [(k, k ^ 1) for k in range(16)])]
    all_to_all x1 -> x2, starting transfers between devices: 11.4 us -> 11.9 us  [to_all(): return lax.all_to_all(copies, axis, 0, 0, axis_index_groups=groups)]
    ppermute x11 -> x10, waiting for transfers between devices: 2.94 us -> 2.85 us  [to_core(): return lax.ppermute(value, 'row', [(k, k ^ 1) for k in range(16)])]
  transfers between devices with their start and end apart: 21 -> 21, of which waited for: 8 -> 10; matrix products, arithmetic and copies ran while one was open for 5% -> 4% of each run, Pallas kernels for 20% -> 21%
where the time goes in v6:
time: 137 us; the launch traced here: 136 us
  Pallas kernels  41.3 us (30%)
  starting transfers between devices  38.8 us (28%)
  waiting for transfers between devices  34 us (25%)
  between operations  15.7 us (11%)
  local copies, waits for them, and re-layouts  4.74 us (3%)
  other arithmetic  1.67 us (1%)
    all_to_all x2, waiting for transfers between devices, to_all(): return lax.all_to_all(copies, axis, 0, 0, axis_index_groups=groups)  18.3 us
    all_to_all x2, starting transfers between devices, to_all(): return lax.all_to_all(copies, axis, 0, 0, axis_index_groups=groups)  11.9 us
    ppermute x10, starting transfers between devices, to_core(): return lax.ppermute(value, 'row', [(k, k ^ 1) for k in range(16)])  10.6 us
    pallas_call x1, Pallas kernels, sparse(): pl.pallas_call(product_kernel, in_specs=[SM] * 7 + [VM] * 5 + [ANY] * 18,...  10.5 us
    pallas_call x1, Pallas kernels, body(): pl.pallas_call(values_kernel, in_specs=[SM, VM, VM, VM], out_specs=HBM, o...  10.2 us
    pallas_call x2, Pallas kernels, grid_blocks(): pl.pallas_call(functools.partial(grid_kernel, with_sum), in_specs=[SM, SM...  10.2 us
    ppermute x7, starting transfers between devices, move(): lax.ppermute(value, ('row', 'col'), [(k, device_of(*where(*place_of(k))))...  9.78 us
    ppermute x2, waiting for transfers between devices, from_core_1(): return lax.ppermute(value, ('row', 'col'), pairs)  9.18 us
  transfers between devices with their start and end apart: 21, of which 10 were waited for; matrix products, arithmetic and copies ran while one was open for 4% of the time, Pallas kernels for 21%

profile of v6, /device:TPU:1, one launch (start us, length us, event | category | flops | bytes accessed | tf_op | source)
XLA Modules:
  0.0 136.2 jit_solution(17328063662376979066)
XLA Ops:
  9.2 1.5 %pack.1 = (bf16[2560,128]{1,0:T(8,128)(2,1)S(1)}, f32[8,128]{1,0:T(8,128)S(1)}) custom-call(s32[4,8]{1,0:T(4,128)S(1)} %copy-done.12, s32[2]{0:T(128)S(1)} %pad_add_fusion.place_ref, bf16[512,1024]{1,0:T(8,128)(2,1)S(1)} %copy-done.5), custom_call_target="tpu_custom_call" | custom-call | flops 2000000000 | bytes 1048576 | tf_op jit(solution)/shard_map/pack/pallas_call | solution.py:416
  12.2 1.7 %collective-permute-done = bf16[20,128,128]{2,1,0:T(8,128)(2,1)S(1)} collective-permute-done((bf16[20,128,128]{2,1,0:T(8,128)(2,1)S(1)}, bf16[20,128,128]{2,1,0:T(8,128)(2,1)S(1)}, u32[]{:S(2)}, u32[]{:S(2)}) %collective-permute-start) | collective-permute-done | bytes 655392 | tf_op jit(solution)/shard_map/ppermute | solution.py:391
  14.0 1.9 %collective-permute-start.3 = (bf16[40,128,128]{2,1,0:T(8,128)(2,1)S(1)}, bf16[40,128,128]{2,1,0:T(8,128)(2,1)}, u32[]{:S(2)}, u32[]{:S(2)}) collective-permute-start(bf16[40,128,128]{2,1,0:T(8,128)(2,1)S(1)} %pad_maximum_fusion), channel_id=1, source_target_pairs={{0,16},{1,17},{2,18},{3,19},{4,20},{5,21},{6,22},{7,23},{8,10},{9,... | collective-permute-start | bytes 3932168 | tf_op jit(solution)/shard_map/ppermute | solution.py:366
  15.9 2.2 %collective-permute-start.2 = (bf16[40,128,128]{2,1,0:T(8,128)(2,1)S(1)}, bf16[40,128,128]{2,1,0:T(8,128)(2,1)}, u32[]{:S(2)}, u32[]{:S(2)}) collective-permute-start(bf16[40,128,128]{2,1,0:T(8,128)(2,1)S(1)} %pad_maximum_fusion), channel_id=1, source_target_pairs={{0,48},{1,49},{2,50},{3,51},{4,52},{5,53},{6,54},{7,55},{8,14},{9,... | collective-permute-start | bytes 3932168 | tf_op jit(solution)/shard_map/ppermute | solution.py:366
  18.1 2.7 %collective-permute-start.1 = (bf16[40,128,128]{2,1,0:T(8,128)(2,1)S(1)}, bf16[40,128,128]{2,1,0:T(8,128)(2,1)}, u32[]{:S(2)}, u32[]{:S(2)}) collective-permute-start(bf16[40,128,128]{2,1,0:T(8,128)(2,1)S(1)} %pad_maximum_fusion), channel_id=1, source_target_pairs={{0,64},{1,65},{2,66},{3,67},{4,68},{5,69},{6,70},{7,71},{8,73},{9,... | collective-permute-start | bytes 3932168 | tf_op jit(solution)/shard_map/ppermute | solution.py:366
  22.0 6.5 %all-to-all-start = ((bf16[64,80,128]{2,1,0:T(8,128)(2,1)}), bf16[64,80,128]{2,1,0:T(8,128)(2,1)}, u32[]{:S(2)}, u32[]{:S(2)}) async-start(bf16[64,80,128]{2,1,0:T(8,128)(2,1)} %broadcast_in_dim.6), calls=%async_computation | async-start | bytes 2621440 | tf_op jit(solution)/shard_map/all_to_all | solution.py:353
  28.5 10.2 %values.1.phi_ref = bf16[8,8,128,1024]{3,2,1,0:T(8,128)(2,1)} custom-call(s32[2]{0:T(128)S(1)} %pad_add_fusion.place_ref, s32[3,64,128]{2,1,0:T(8,128)S(1)} %copy-done.1, f32[64,128]{1,0:T(8,128)S(1)} %copy-done.3, s32[64,128]{1,0:T(8,128)S(1)} %copy-done.4), custom_call_target="tpu_custom_call" | custom-call | flops 10000000000 | bytes 1048576 | tf_op jit(solution)/shard_map/values/pallas_call | solution.py:431
  38.8 11.5 %all-to-all-done = bf16[64,80,128]{2,1,0:T(8,128)(2,1)} async-done(((bf16[64,80,128]{2,1,0:T(8,128)(2,1)}), bf16[64,80,128]{2,1,0:T(8,128)(2,1)}, u32[]{:S(2)}, u32[]{:S(2)}) %all-to-all-start) | async-done | bytes 1310752 | tf_op jit(solution)/shard_map/all_to_all | solution.py:353
  50.3 5.0 %collective-permute-start.6 = (bf16[64,80,128]{2,1,0:T(8,128)(2,1)}, bf16[64,80,128]{2,1,0:T(8,128)(2,1)S(1)}, u32[]{:S(2)}, u32[]{:S(2)}) collective-permute-start(bf16[64,80,128]{2,1,0:T(8,128)(2,1)} %all-to-all-done), channel_id=1, source_target_pairs={{0,8},{8,0},{16,24},{24,16},{32,40},{40,32},{48,56},{56,48},{64,72... | collective-permute-start | bytes 3932168 | tf_op jit(solution)/shard_map/ppermute | solution.py:391
  57.3 1.5 %constant_dynamic-update-slice_fusion.1 = bf16[128,80,128]{2,1,0:T(8,128)(2,1)S(1)} fusion(bf16[64,80,128]{2,1,0:T(8,128)(2,1)} %all-to-all-done), kind=kLoop, calls=%fused_computation.16 | loop fusion | bytes 2621440
  59.4 5.1 %grid_rows.1 = (bf16[4,128,128]{2,1,0:T(8,128)(2,1)S(1)}, f32[1,128]{1,0:T(1,128)S(1)}) custom-call(s32[2]{0:T(128)S(1)} %pad_add_fusion.place_ref, s32[64]{0:T(128)S(1)} %copy-done, f32[1]{0:T(128)S(6)} %copy.24.shift_ref, bf16[128,80,128]{2,1,0:T(8,128)(2,1)S(1)} %constant_dynamic-update-slice_fusion.bricks_ref, bf16[8,8,128,1024]{3,2,1,0:T(8,128)(2,1)} %values.1.phi_ref, ...), custom_call_target="tpu_custom_call" | custom-call | flops 5000000000 | bytes 1048576 | tf_op jit(solution)/shard_map/grid_rows/pallas_call | solution.py:457
  65.2 5.4 %all-to-all-start.1 = ((f32[128,1,128]{2,1,0:T(1,128)}), f32[128,1,128]{2,1,0:T(1,128)S(1)}, u32[]{:S(2)}, u32[]{:S(2)}) async-start(f32[128,1,128]{2,1,0:T(1,128)} %broadcast_in_dim.8), calls=%async_computation.1 | async-start | bytes 131072 | tf_op jit(solution)/shard_map/all_to_all | solution.py:353
  70.6 1.9 %collective-permute-done.5 = bf16[40,128,128]{2,1,0:T(8,128)(2,1)} collective-permute-done((bf16[40,128,128]{2,1,0:T(8,128)(2,1)}, bf16[40,128,128]{2,1,0:T(8,128)(2,1)}, u32[]{:S(2)}, u32[]{:S(2)}) %collective-permute-start.5) | collective-permute-done | bytes 1310752 | tf_op jit(solution)/shard_map/ppermute | solution.py:366
  73.3 6.7 %all-to-all-done.1 = f32[128,1,128]{2,1,0:T(1,128)S(1)} async-done(((f32[128,1,128]{2,1,0:T(1,128)}), f32[128,1,128]{2,1,0:T(1,128)S(1)}, u32[]{:S(2)}, u32[]{:S(2)}) %all-to-all-start.1) | async-done | bytes 65568 | tf_op jit(solution)/shard_map/all_to_all | solution.py:353
  81.8 1.5 %broadcast_select_fusion = bf16[40,128,128]{2,1,0:T(8,128)(2,1)S(1)} fusion(bf16[40,128,128]{2,1,0:T(8,128)(2,1)} %collective-permute-done.1, bf16[40,128,128]{2,1,0:T(8,128)(2,1)} %collective-permute-done.5, pred[]{:T(512)S(6)} %eq.29), kind=kLoop, calls=%fused_computation.14 | loop fusion | flops 655360 | bytes 3932161 | tf_op jit(solution)/shard_map/jit(_where)/select_n | solution.py:476
  83.3 2.2 %collective-permute-start.9 = (bf16[40,128,128]{2,1,0:T(8,128)(2,1)S(1)}, bf16[40,128,128]{2,1,0:T(8,128)(2,1)S(1)}, u32[]{:S(2)}, u32[]{:S(2)}) collective-permute-start(bf16[40,128,128]{2,1,0:T(8,128)(2,1)S(1)} %broadcast_select_fusion), channel_id=1, source_target_pairs={{0,48},{1,49},{2,50},{3,51},{4,52},{5,53},{6,54},{7,55},{8,14},{9,... | collective-permute-start | bytes 3932168 | tf_op jit(solution)/shard_map/ppermute | solution.py:366
  86.0 5.0 %grid_cols.1 = bf16[4,128,128]{2,1,0:T(8,128)(2,1)S(1)} custom-call(s32[2]{0:T(128)S(1)} %pad_add_fusion.place_ref, s32[64]{0:T(128)S(1)} %copy-done, f32[1]{0:T(128)S(6)} %copy.24.shift_ref, bf16[128,80,128]{2,1,0:T(8,128)(2,1)S(1)} %constant_dynamic-update-slice_fusion.bricks_ref, bf16[8,8,128,1024]{3,2,1,0:T(8,128)(2,1)} %values.1.phi_ref), custom_call_target="tpu_custom_call" | custom-call | flops 5000000000 | bytes 1048576 | tf_op jit(solution)/shard_map/grid_cols/pallas_call | solution.py:457
  91.0 8.1 %plan.1 = (s32[1]{0:T(128)}, s32[548]{0:T(1024)S(1)}, s32[2192]{0:T(1024)S(1)}, s32[2192]{0:T(1024)S(1)}, s32[1]{0:T(128)}) custom-call(s32[2]{0:T(128)S(1)} %pad_add_fusion.place_ref, bf16[128,80,128]{2,1,0:T(8,128)(2,1)S(1)} %constant_dynamic-update-slice_fusion.bricks_ref), custom_call_target="tpu_custom_call" | custom-call | flops 8999999488 | bytes 1048576 | tf_op jit(solution)/shard_map/plan/pallas_call | solution.py:479
  101.7 4.6 %collective-permute-start.15 = (bf16[20,128,128]{2,1,0:T(8,128)(2,1)S(1)}, bf16[20,128,128]{2,1,0:T(8,128)(2,1)S(1)}, u32[]{:S(2)}, u32[]{:S(2)}) collective-permute-start(bf16[20,128,128]{2,1,0:T(8,128)(2,1)S(1)} %slice.7), channel_id=1, source_target_pairs={{8,6},{9,7},{10,0},{11,1},{12,2},{13,3},{14,4},{15,5},{24,22},{25,... | collective-permute-start | bytes 1966088 | tf_op jit(solution)/shard_map/ppermute | solution.py:387
  106.3 1.9 %collective-permute-start.14 = (bf16[20,128,128]{2,1,0:T(8,128)(2,1)S(1)}, bf16[20,128,128]{2,1,0:T(8,128)(2,1)S(1)}, u32[]{:S(2)}, u32[]{:S(2)}) collective-permute-start(bf16[20,128,128]{2,1,0:T(8,128)(2,1)S(1)} %slice.6), channel_id=1, source_target_pairs={{8,10},{9,11},{10,12},{11,13},{12,14},{13,15},{14,8},{15,9},{24,26... | collective-permute-start | bytes 1966088 | tf_op jit(solution)/shard_map/ppermute | solution.py:387
  109.6 3.9 %collective-permute-done.15 = bf16[20,128,128]{2,1,0:T(8,128)(2,1)S(1)} collective-permute-done((bf16[20,128,128]{2,1,0:T(8,128)(2,1)S(1)}, bf16[20,128,128]{2,1,0:T(8,128)(2,1)S(1)}, u32[]{:S(2)}, u32[]{:S(2)}) %collective-permute-start.15) | collective-permute-done | bytes 655392 | tf_op jit(solution)/shard_map/ppermute | solution.py:387
  113.6 5.2 %collective-permute-done.14 = bf16[20,128,128]{2,1,0:T(8,128)(2,1)S(1)} collective-permute-done((bf16[20,128,128]{2,1,0:T(8,128)(2,1)S(1)}, bf16[20,128,128]{2,1,0:T(8,128)(2,1)S(1)}, u32[]{:S(2)}, u32[]{:S(2)}) %collective-permute-start.14) | collective-permute-done | bytes 655392 | tf_op jit(solution)/shard_map/ppermute | solution.py:387
  118.9 10.5 %conditional.1 = ((bf16[512,1024]{1,0:T(8,128)(2,1)}, bf16[512,1024]{1,0:T(8,128)(2,1)})) conditional(s32[]{:T(128)} %bitcast.7, (s32[2]{0:T(128)S(1)}, s32[4,8]{1,0:T(4,128)S(1)}, f32[1]{0:T(128)}, s32[1]{0:T(128)}, s32[548]{0:T(1024)S(1)}, /*index=5*/s32[2192]{0:T(1024)S(1)}, s32[2192]{0:T(1024)S(1)}, f32[128,128]{1,0:T(8,128)S(1)}, ...), branch_computations={%region_0.1_spmd, %region_1.3_spmd} | conditional | flops 12000000000 | bytes 121439128 | solution.py:546
  118.9 10.5 %product.1 = (bf16[512,1024]{1,0:T(8,128)(2,1)}, bf16[512,1024]{1,0:T(8,128)(2,1)}) custom-call(s32[2]{0:T(128)S(1)} %get-tuple-element.74.place_ref, s32[4,8]{1,0:T(4,128)S(1)} %get-tuple-element.75.pattern_ref, f32[1]{0:T(128)} %get-tuple-element.76.shift_ref, s32[1]{0:T(128)} %get-tuple-element.77.turns_ref, s32[548]{0:T(1024)S(1)} %get-tuple-element.78.out_ref, ...), custom_call_target="tpu_custom_call" | custom-call | flops 12000000000 | bytes 1048576 | tf_op jit(solution)/shard_map/cond/branch_0_fun/product/pallas_call | solution.py:512
  (61 shorter events, 13.6 us)
Async XLA Ops:
  10.7 3.2 %collective-permute-start = (bf16[20,128,128]{2,1,0:T(8,128)(2,1)S(1)}, bf16[20,128,128]{2,1,0:T(8,128)(2,1)S(1)}, u32[]{:S(2)}, u32[]{:S(2)}) collective-permute-start(bf16[20,128,128]{2,1,0:T(8,128)(2,1)S(1)} %bitcast.32), channel_id=1, source_target_pairs={{0,8},{8,0},{16,24},{24,16},{32,40},{40,32},{48,56},{56,48},{64,72... | collective-permute-start | bytes 1966088 | tf_op jit(solution)/shard_map/ppermute | solution.py:391
  14.0 36.3 %collective-permute-start.3 = (bf16[40,128,128]{2,1,0:T(8,128)(2,1)S(1)}, bf16[40,128,128]{2,1,0:T(8,128)(2,1)}, u32[]{:S(2)}, u32[]{:S(2)}) collective-permute-start(bf16[40,128,128]{2,1,0:T(8,128)(2,1)S(1)} %pad_maximum_fusion), channel_id=1, source_target_pairs={{0,16},{1,17},{2,18},{3,19},{4,20},{5,21},{6,22},{7,23},{8,10},{9,... | collective-permute-start | bytes 3932168 | tf_op jit(solution)/shard_map/ppermute | solution.py:366
  15.9 34.4 %collective-permute-start.2 = (bf16[40,128,128]{2,1,0:T(8,128)(2,1)S(1)}, bf16[40,128,128]{2,1,0:T(8,128)(2,1)}, u32[]{:S(2)}, u32[]{:S(2)}) collective-permute-start(bf16[40,128,128]{2,1,0:T(8,128)(2,1)S(1)} %pad_maximum_fusion), channel_id=1, source_target_pairs={{0,48},{1,49},{2,50},{3,51},{4,52},{5,53},{6,54},{7,55},{8,14},{9,... | collective-permute-start | bytes 3932168 | tf_op jit(solution)/shard_map/ppermute | solution.py:366
  18.1 32.2 %collective-permute-start.1 = (bf16[40,128,128]{2,1,0:T(8,128)(2,1)S(1)}, bf16[40,128,128]{2,1,0:T(8,128)(2,1)}, u32[]{:S(2)}, u32[]{:S(2)}) collective-permute-start(bf16[40,128,128]{2,1,0:T(8,128)(2,1)S(1)} %pad_maximum_fusion), channel_id=1, source_target_pairs={{0,64},{1,65},{2,66},{3,67},{4,68},{5,69},{6,70},{7,71},{8,73},{9,... | collective-permute-start | bytes 3932168 | tf_op jit(solution)/shard_map/ppermute | solution.py:366
  22.0 28.3 %all-to-all-start = ((bf16[64,80,128]{2,1,0:T(8,128)(2,1)}), bf16[64,80,128]{2,1,0:T(8,128)(2,1)}, u32[]{:S(2)}, u32[]{:S(2)}) async-start(bf16[64,80,128]{2,1,0:T(8,128)(2,1)} %broadcast_in_dim.6), calls=%async_computation | async-start | bytes 2621440 | tf_op jit(solution)/shard_map/all_to_all | solution.py:353
  50.3 8.8 %collective-permute-start.6 = (bf16[64,80,128]{2,1,0:T(8,128)(2,1)}, bf16[64,80,128]{2,1,0:T(8,128)(2,1)S(1)}, u32[]{:S(2)}, u32[]{:S(2)}) collective-permute-start(bf16[64,80,128]{2,1,0:T(8,128)(2,1)} %all-to-all-done), channel_id=1, source_target_pairs={{0,8},{8,0},{16,24},{24,16},{32,40},{40,32},{48,56},{56,48},{64,72... | collective-permute-start | bytes 3932168 | tf_op jit(solution)/shard_map/ppermute | solution.py:391
  55.4 15.2 %collective-permute-start.8 = (bf16[40,128,128]{2,1,0:T(8,128)(2,1)}, bf16[40,128,128]{2,1,0:T(8,128)(2,1)}, u32[]{:S(2)}, u32[]{:S(2)}) collective-permute-start(bf16[40,128,128]{2,1,0:T(8,128)(2,1)} %collective-permute-done.3), channel_id=1, source_target_pairs={{0,8},{8,0},{16,24},{24,16},{32,40},{40,32},{48,56},{56,48},{64,72... | collective-permute-start | bytes 3932168 | tf_op jit(solution)/shard_map/ppermute | solution.py:391
  55.5 17.1 %collective-permute-start.5 = (bf16[40,128,128]{2,1,0:T(8,128)(2,1)}, bf16[40,128,128]{2,1,0:T(8,128)(2,1)}, u32[]{:S(2)}, u32[]{:S(2)}) collective-permute-start(bf16[40,128,128]{2,1,0:T(8,128)(2,1)} %collective-permute-done.1), channel_id=1, source_target_pairs={{0,16},{1,17},{2,18},{3,19},{4,20},{5,21},{6,22},{7,23},{8,72},{9,... | collective-permute-start | bytes 3932168 | tf_op jit(solution)/shard_map/ppermute | solution.py:366
  55.5 17.1 %collective-permute-start.7 = (bf16[40,128,128]{2,1,0:T(8,128)(2,1)}, bf16[40,128,128]{2,1,0:T(8,128)(2,1)}, u32[]{:S(2)}, u32[]{:S(2)}) collective-permute-start(bf16[40,128,128]{2,1,0:T(8,128)(2,1)} %collective-permute-done.2), channel_id=1, source_target_pairs={{0,8},{8,0},{16,24},{24,16},{32,40},{40,32},{48,56},{56,48},{64,72... | collective-permute-start | bytes 3932168 | tf_op jit(solution)/shard_map/ppermute | solution.py:391
  56.3 17.1 %collective-permute-start.4 = (bf16[40,128,128]{2,1,0:T(8,128)(2,1)}, bf16[40,128,128]{2,1,0:T(8,128)(2,1)}, u32[]{:S(2)}, u32[]{:S(2)}) collective-permute-start(bf16[40,128,128]{2,1,0:T(8,128)(2,1)} %collective-permute-done.2), channel_id=1, source_target_pairs={{0,48},{1,49},{2,50},{3,51},{4,52},{5,53},{6,54},{7,55},{8,14},{9,... | collective-permute-start | bytes 3932168 | tf_op jit(solution)/shard_map/ppermute | solution.py:366
  65.2 14.9 %all-to-all-start.1 = ((f32[128,1,128]{2,1,0:T(1,128)}), f32[128,1,128]{2,1,0:T(1,128)S(1)}, u32[]{:S(2)}, u32[]{:S(2)}) async-start(f32[128,1,128]{2,1,0:T(1,128)} %broadcast_in_dim.8), calls=%async_computation.1 | async-start | bytes 131072 | tf_op jit(solution)/shard_map/all_to_all | solution.py:353
  80.1 20.0 %collective-permute-start.13 = (bf16[40,128,128]{2,1,0:T(8,128)(2,1)}, bf16[40,128,128]{2,1,0:T(8,128)(2,1)S(1)}, u32[]{:S(2)}, u32[]{:S(2)}) collective-permute-start(bf16[40,128,128]{2,1,0:T(8,128)(2,1)} %collective-permute-done.5), channel_id=1, source_target_pairs={{0,8},{8,0},{16,24},{24,16},{32,40},{40,32},{48,56},{56,48},{64,72... | collective-permute-start | bytes 3932168 | tf_op jit(solution)/shard_map/ppermute | solution.py:391
  81.2 18.9 %collective-permute-start.10 = (bf16[40,128,128]{2,1,0:T(8,128)(2,1)}, bf16[40,128,128]{2,1,0:T(8,128)(2,1)S(1)}, u32[]{:S(2)}, u32[]{:S(2)}) collective-permute-start(bf16[40,128,128]{2,1,0:T(8,128)(2,1)} %collective-permute-done.5), channel_id=1, source_target_pairs={{0,16},{1,17},{2,18},{3,19},{4,20},{5,21},{6,22},{7,23},{8,10},{9,... | collective-permute-start | bytes 3932168 | tf_op jit(solution)/shard_map/ppermute | solution.py:366
  81.7 18.4 %collective-permute-start.12 = (bf16[40,128,128]{2,1,0:T(8,128)(2,1)}, bf16[40,128,128]{2,1,0:T(8,128)(2,1)S(1)}, u32[]{:S(2)}, u32[]{:S(2)}) collective-permute-start(bf16[40,128,128]{2,1,0:T(8,128)(2,1)} %collective-permute-done.1), channel_id=1, source_target_pairs={{0,8},{8,0},{16,24},{24,16},{32,40},{40,32},{48,56},{56,48},{64,72... | collective-permute-start | bytes 3932168 | tf_op jit(solution)/shard_map/ppermute | solution.py:391
  83.3 16.8 %collective-permute-start.9 = (bf16[40,128,128]{2,1,0:T(8,128)(2,1)S(1)}, bf16[40,128,128]{2,1,0:T(8,128)(2,1)S(1)}, u32[]{:S(2)}, u32[]{:S(2)}) collective-permute-start(bf16[40,128,128]{2,1,0:T(8,128)(2,1)S(1)} %broadcast_select_fusion), channel_id=1, source_target_pairs={{0,48},{1,49},{2,50},{3,51},{4,52},{5,53},{6,54},{7,55},{8,14},{9,... | collective-permute-start | bytes 3932168 | tf_op jit(solution)/shard_map/ppermute | solution.py:366
  85.4 14.7 %collective-permute-start.11 = (bf16[40,128,128]{2,1,0:T(8,128)(2,1)}, bf16[40,128,128]{2,1,0:T(8,128)(2,1)S(1)}, u32[]{:S(2)}, u32[]{:S(2)}) collective-permute-start(bf16[40,128,128]{2,1,0:T(8,128)(2,1)} %collective-permute-done.4), channel_id=1, source_target_pairs={{0,8},{8,0},{16,24},{24,16},{32,40},{40,32},{48,56},{56,48},{64,72... | collective-permute-start | bytes 3932168 | tf_op jit(solution)/shard_map/ppermute | solution.py:391
  99.1 19.7 %copy-start.7 = (bf16[512,1024]{1,0:T(8,128)(2,1)S(1)}, bf16[512,1024]{1,0:T(8,128)(2,1)}, u32[]{:S(2)}) copy-start(bf16[512,1024]{1,0:T(8,128)(2,1)} %rest_0_.1) | copy-start | bytes 3145732
  99.1 19.7 %copy-start.9 = (bf16[2560,128]{1,0:T(8,128)(2,1)S(1)}, bf16[2560,128]{1,0:T(8,128)(2,1)}, u32[]{:S(2)}) copy-start(bf16[2560,128]{1,0:T(8,128)(2,1)} %copy-done.8) | copy-start | bytes 1966084
  99.1 19.7 %copy-start.11 = (bf16[20,128,128]{2,1,0:T(8,128)(2,1)S(1)}, bf16[20,128,128]{2,1,0:T(8,128)(2,1)}, u32[]{:S(2)}) copy-start(bf16[20,128,128]{2,1,0:T(8,128)(2,1)} %copy-done.10) | copy-start | bytes 1966084
  100.1 18.7 %collective-permute-start.18 = (bf16[40,128,128]{2,1,0:T(8,128)(2,1)S(1)}, bf16[40,128,128]{2,1,0:T(8,128)(2,1)S(1)}, u32[]{:S(2)}, u32[]{:S(2)}) collective-permute-start(bf16[40,128,128]{2,1,0:T(8,128)(2,1)S(1)} %collective-permute-done.10), channel_id=1, source_target_pairs={{0,8},{8,0},{16,24},{24,16},{32,40},{40,32},{48,56},{56,48},{64,72... | collective-permute-start | bytes 3932168 | tf_op jit(solution)/shard_map/ppermute | solution.py:391
  101.5 17.3 %collective-permute-start.17 = (bf16[40,128,128]{2,1,0:T(8,128)(2,1)S(1)}, bf16[40,128,128]{2,1,0:T(8,128)(2,1)S(1)}, u32[]{:S(2)}, u32[]{:S(2)}) collective-permute-start(bf16[40,128,128]{2,1,0:T(8,128)(2,1)S(1)} %collective-permute-done.9), channel_id=1, source_target_pairs={{0,8},{8,0},{16,24},{24,16},{32,40},{40,32},{48,56},{56,48},{64,72... | collective-permute-start | bytes 3932168 | tf_op jit(solution)/shard_map/ppermute | solution.py:391
  101.7 11.9 %collective-permute-start.15 = (bf16[20,128,128]{2,1,0:T(8,128)(2,1)S(1)}, bf16[20,128,128]{2,1,0:T(8,128)(2,1)S(1)}, u32[]{:S(2)}, u32[]{:S(2)}) collective-permute-start(bf16[20,128,128]{2,1,0:T(8,128)(2,1)S(1)} %slice.7), channel_id=1, source_target_pairs={{8,6},{9,7},{10,0},{11,1},{12,2},{13,3},{14,4},{15,5},{24,22},{25,... | collective-permute-start | bytes 1966088 | tf_op jit(solution)/shard_map/ppermute | solution.py:387
  106.3 12.5 %collective-permute-start.14 = (bf16[20,128,128]{2,1,0:T(8,128)(2,1)S(1)}, bf16[20,128,128]{2,1,0:T(8,128)(2,1)S(1)}, u32[]{:S(2)}, u32[]{:S(2)}) collective-permute-start(bf16[20,128,128]{2,1,0:T(8,128)(2,1)S(1)} %slice.6), channel_id=1, source_target_pairs={{8,10},{9,11},{10,12},{11,13},{12,14},{13,15},{14,8},{15,9},{24,26... | collective-permute-start | bytes 1966088 | tf_op jit(solution)/shard_map/ppermute | solution.py:387
  108.2 1.4 %collective-permute-start.16 = (bf16[4,128,128]{2,1,0:T(8,128)(2,1)S(1)}, bf16[4,128,128]{2,1,0:T(8,128)(2,1)S(1)}, u32[]{:S(2)}, u32[]{:S(2)}) collective-permute-start(bf16[4,128,128]{2,1,0:T(8,128)(2,1)S(1)} %grid_cols.1), channel_id=1, source_target_pairs={{0,8},{8,0},{16,24},{24,16},{32,40},{40,32},{48,56},{56,48},{64,72... | collective-permute-start | bytes 393224 | tf_op jit(solution)/shard_map/ppermute | solution.py:391
  (10 other events, 69.8 us)
